TPU v7x, 128 devices: a whole 4x4x4 slice. The times are simulated.
128 devices in a mesh: dp: 16 (over x, z_lo, core), mp: 8 (over z_hi, y).
Axes of the slice: x: 4, y: 4, z: 4 (z_hi: 2, z_lo: 2; z = z_hi * 2 + z_lo), core: 2. Of those that a mesh axis runs over, the one named last changes fastest.
Arguments:
- taps: bfloat16 [3, 512, 8192], P(None, ('dp', 'mp')), may hold values from -6 to 6
- gain: float32 [8192], P('dp'), may hold values from 0.5 to 1.5
- join_weight: bfloat16 [3, 8192, 8192], P(None, 'mp', 'dp'), may hold values from -0.0390625 to 0.0390625
- head_weight: bfloat16 [8192, 16384], P('mp', 'dp'), may hold values from -0.1875 to 0.1875
- targets: int32 [2, 16, 32], P(None, None, 'mp'), may hold values from 0 to 16383
- masks: int32 [2, 16, 32], P(None, None, 'mp'), may hold values from 0 to 1, as said below
- first_codes: bfloat16 [3, 8192, 8192], P(None, 'mp', 'dp'), may hold values from -1 to 1
- first_scales: float32 [3, 8192, 32], P(None, 'mp', 'dp'), may hold values from 1e-05 to 0.0001
- second_codes: bfloat16 [3, 8192, 8192], P(None, 'mp', 'dp'), may hold values from 0.099609375 to 1
- second_scales: float32 [3, 8192, 32], P(None, 'mp', 'dp'), may hold values from 1e-10 to 1e-09
Outputs:
- new_join: bfloat16 [3, 8192, 8192], P(None, 'mp', 'dp')
- new_first_codes: bfloat16 [3, 8192, 8192], P(None, 'mp', 'dp')
- new_first_scales: float32 [3, 8192, 32], P(None, 'mp', 'dp')
- new_second_codes: bfloat16 [3, 8192, 8192], P(None, 'mp', 'dp')
- new_second_scales: float32 [3, 8192, 32], P(None, 'mp', 'dp')
- loss: float32 [], replicated
Inputs may be any that keep to these rules, and one draw needn't show every extreme that they name: Every step k has at least one token with masks[k] = 1.
All inputs are finite; a program needn't handle non-finite values. Where the computation divides by a largest or mean magnitude, that divisor is 1e-20 or more.
Results may differ from a plain program's by a relative error of at most 0.01.
Values may be sent and summed in bfloat16 or wider, within the bound.
No kernel may reach another device: no remote copies, remote signals or barrier semaphores. Data moves between devices by JAX's collectives and lax.ppermute only.
A program may use at most 128 MiB of HBM per device.

v0:
```python
import jax
import jax.numpy as jnp
from jax import lax
from jax.sharding import PartitionSpec as P

D = 8192
STEPS = 2
BLOCK = 256


norm_eps = 1e-05
clip_norm = 1.0
learn_rate = 0.0003
weight_decay = 0.1
beta_first = 0.9
beta_second = 0.999
step_count = 10.0
adam_eps = 1e-08
scale_eps = 1e-12


def contract_first(left, right):
    return lax.dot_general(
        left, right, (((0,), (0,)), ((), ())), preferred_element_type=jnp.float32
    )


def contract_last(left, right):
    return lax.dot_general(
        left, right, (((1,), (1,)), ((), ())), preferred_element_type=jnp.float32
    )


def adam_blocks(weights, grads, first_codes, first_scales, second_codes, second_scales):
    shape = weights.shape
    blocked = shape[:-1] + (shape[-1] // BLOCK, BLOCK)
    grad_blocks = grads.reshape(blocked)
    first_prev = first_codes.astype(jnp.float32).reshape(blocked) * first_scales[..., None]
    second_prev = second_codes.astype(jnp.float32).reshape(blocked) * second_scales[..., None]
    first_new = beta_first * first_prev + (1.0 - beta_first) * grad_blocks
    second_new = beta_second * second_prev + (1.0 - beta_second) * grad_blocks * grad_blocks
    current = weights.astype(jnp.float32).reshape(blocked)
    update = (
        first_new
        / (1.0 - beta_first**step_count)
        / (jnp.sqrt(second_new / (1.0 - beta_second**step_count)) + adam_eps)
        + weight_decay * current
    )
    new_weights = (current - learn_rate * update).reshape(shape).astype(jnp.bfloat16)
    first_scale = jnp.max(jnp.abs(first_new), -1) + scale_eps
    first_out = (first_new / first_scale[..., None]).reshape(shape).astype(jnp.bfloat16)
    second_scale = jnp.max(jnp.abs(second_new), -1) + scale_eps
    second_out = (second_new / second_scale[..., None]).reshape(shape).astype(jnp.bfloat16)
    return (new_weights, first_out, first_scale, second_out, second_scale)


def shards(
    taps,
    gain,
    join_weight,
    head_weight,
    targets,
    masks,
    first_codes,
    first_scales,
    second_codes,
    second_scales,
):
    dp_count = lax.axis_size("dp")
    slab_rows = taps.shape[1]
    local_taps = lax.all_to_all(taps, "mp", split_axis=2, concat_axis=1, tiled=True)
    own_rows = local_taps.shape[1]
    gathered = lax.all_gather(local_taps, "dp", axis=1, tiled=True)
    all_rows = gathered.shape[1]
    vocab_local = head_weight.shape[1]
    mask_float = masks.astype(jnp.float32)
    counts = lax.psum(jnp.sum(mask_float, axis=(1, 2)), "mp")
    constant = jnp.dot(gathered[0], join_weight[0], preferred_element_type=jnp.float32) + jnp.dot(
        gathered[1], join_weight[1], preferred_element_type=jnp.float32
    )
    vocab_ids = (
        lax.broadcasted_iota(jnp.int32, (dp_count, slab_rows, vocab_local), 2)
        + lax.axis_index("dp") * vocab_local
    )
    top_rows = gathered[2]
    saved = []
    loss_local = jnp.zeros((), jnp.float32)
    for step in range(STEPS):
        partial_sum = constant + jnp.dot(
            top_rows, join_weight[2], preferred_element_type=jnp.float32
        )
        joining = lax.psum_scatter(
            partial_sum.reshape(dp_count, own_rows, -1), "mp", scatter_dimension=1, tiled=True
        )
        squares = lax.psum(jnp.sum(joining * joining, -1), "dp")
        inverse = lax.rsqrt(squares / D + norm_eps)
        hidden = (joining * inverse[..., None] * gain).astype(jnp.bfloat16)
        moved = lax.all_to_all(
            lax.all_to_all(hidden, "dp", split_axis=0, concat_axis=2, tiled=True),
            "mp",
            split_axis=2,
            concat_axis=1,
            tiled=True,
        )
        hidden_rows = lax.all_gather(moved.reshape(own_rows, -1), "dp", axis=0, tiled=True)
        logit_part = jnp.dot(hidden_rows, head_weight, preferred_element_type=jnp.float32)
        logits = lax.psum_scatter(
            logit_part.reshape(dp_count, own_rows, -1), "mp", scatter_dimension=1, tiled=True
        )
        onehot = (vocab_ids == targets[step][..., None]).astype(jnp.float32)
        exp_total, picked = lax.psum(
            (jnp.sum(jnp.exp(logits), -1), jnp.sum(logits * onehot, -1)), "dp"
        )
        log_total = jnp.log(exp_total)
        loss_local = loss_local + jnp.sum(mask_float[step] * (log_total - picked) / counts[step])
        probs = jnp.exp(logits - log_total[..., None])
        logit_grad = ((mask_float[step] / counts[step])[..., None] * (probs - onehot)).astype(
            jnp.bfloat16
        )
        saved.append((top_rows, joining, inverse, logit_grad))
        top_rows = hidden_rows
    grads = jnp.zeros(join_weight.shape, jnp.float32)
    carried = None
    for step in reversed(range(STEPS)):
        top_rows, joining, inverse, logit_grad = saved[step]
        grad_rows = lax.all_gather(logit_grad, "mp", axis=1, tiled=True).reshape(all_rows, -1)

        def head_term(start, count, grad_rows=grad_rows):
            return contract_last(grad_rows, head_weight)

        hidden_grad = lax.psum_scatter(
            head_term(jnp.int32(0), own_rows * lax.axis_size("dp")),
            "dp",
            scatter_dimension=0,
            tiled=True,
        )
        if carried is not None:
            hidden_grad = hidden_grad + carried
        row_grad = lax.all_to_all(
            lax.all_to_all(
                hidden_grad.reshape(1, own_rows, -1), "mp", split_axis=1, concat_axis=2, tiled=True
            ),
            "dp",
            split_axis=2,
            concat_axis=0,
            tiled=True,
        )
        scaled = row_grad * gain
        inner = lax.psum(jnp.sum(scaled * joining, -1), "dp")
        joining_grad = (
            inverse[..., None] * scaled
            - (inverse * inverse * inverse * inner / D)[..., None] * joining
        ).astype(jnp.bfloat16)
        grad_full = lax.all_gather(joining_grad, "mp", axis=1, tiled=True).reshape(all_rows, -1)
        grads = grads + jnp.stack(
            [
                contract_first(gathered[0], grad_full),
                contract_first(gathered[1], grad_full),
                contract_first(top_rows, grad_full),
            ]
        )
        if step > 0:

            def feedback_term(start, count, source=grad_full):
                return contract_last(source, join_weight[2])

            carried = lax.psum_scatter(
                feedback_term(jnp.int32(0), own_rows * lax.axis_size("dp")).astype(jnp.bfloat16),
                "dp",
                scatter_dimension=0,
                tiled=True,
            ).astype(jnp.float32)
    square_sum = jnp.sum(grads * grads)
    loss = lax.psum(loss_local, "mp")
    norm_sq = lax.psum(square_sum, ("dp", "mp"))
    clip = jnp.minimum(1.0, clip_norm / (jnp.sqrt(norm_sq) + 1e-06))
    new_join, new_first, first_scale, new_second, second_scale = adam_blocks(
        join_weight, grads * clip, first_codes, first_scales, second_codes, second_scales
    )
    return (new_join, new_first, first_scale, new_second, second_scale, loss)


def solution(mesh):
    return jax.shard_map(
        shards,
        mesh=mesh,
        in_specs=(
            P(None, ("dp", "mp"), None),
            P("dp"),
            P(None, "mp", "dp"),
            P("mp", "dp"),
            P(None, None, "mp"),
            P(None, None, "mp"),
            P(None, "mp", "dp"),
            P(None, "mp", "dp"),
            P(None, "mp", "dp"),
            P(None, "mp", "dp"),
        ),
        out_specs=(
            P(None, "mp", "dp"),
            P(None, "mp", "dp"),
            P(None, "mp", "dp"),
            P(None, "mp", "dp"),
            P(None, "mp", "dp"),
            P(),
        ),
        check_vma=False,
    )
```

profile of v0, /device:TPU:1, one launch (start us, length us, event | category | flops | bytes accessed | tf_op | source)
XLA Modules:
  0.0 1437.5 jit_solution(10140225107885773631)
XLA Ops:
  62.8 34.9 %all-gather.6.cloned.1.call-done = bf16[3,512,1024]{2,1,0:T(8,128)(2,1)} async-done(((bf16[3,32,1024]{2,1,0:T(8,128)(2,1)}), bf16[3,512,1024]{2,1,0:T(8,128)(2,1)}) %all-gather.6.cloned.1.call-update) | async-done | bytes 3145744 | tf_op jit(solution)/shard_map/all_gather | solution.py:73
  105.8 70.3 %reduce-scatter.8.cloned.1.call-done = f32[16,4,512]{2,0,1:T(8,128)} async-done(((f32[16,32,512]{2,0,1:T(8,128)}), f32[16,4,512]{2,0,1:T(8,128)}) %reduce-scatter.8.cloned.1.call-update) | async-done | bytes 131088 | tf_op jit(solution)/shard_map/reduce_scatter | solution.py:92
  177.0 29.0 %psum.77 = f32[16,4]{0,1:T(4,128)S(1)} all-reduce(f32[16,4]{0,1:T(4,128)S(1)} %multiply_reduce_fusion.4), channel_id=1, replica_groups=mesh['dp'=16,'mp'=8] {'dp'}, use_global_device_ids=true, to_apply=%region_2.0 | all-reduce | flops 64 | bytes 512 | tf_op jit(solution)/shard_map/psum | solution.py:95
  224.2 46.5 %reduce = bf16[8192,4]{1,0:T(8,128)(2,1)} reduce(bf16[8192,1,4]{2,1,0:T(2,128)(2,1)} %bitcast.214, bf16[]{:T(256)} %broadcast.105), dimensions={1}, to_apply=%bitcast.169.reduce_sub_computation | reduce | bytes 131074
  302.6 29.4 %all-gather.8.cloned.1.call-done = bf16[512,1024]{1,0:T(8,128)(2,1)} async-done(((bf16[32,1024]{1,0:T(8,128)(2,1)}), bf16[512,1024]{1,0:T(8,128)(2,1)}) %all-gather.8.cloned.1.call-update) | async-done | bytes 1048592 | tf_op jit(solution)/shard_map/all_gather | solution.py:105
  335.9 70.6 %reduce-scatter.10.cloned.1.call-done = f32[16,4,512]{2,0,1:T(8,128)} async-done(((f32[16,32,512]{2,0,1:T(8,128)}), f32[16,4,512]{2,0,1:T(8,128)}) %reduce-scatter.10.cloned.1.call-update) | async-done | bytes 131088 | tf_op jit(solution)/shard_map/reduce_scatter | solution.py:92
  407.5 29.0 %psum.78 = f32[16,4]{0,1:T(4,128)S(1)} all-reduce(f32[16,4]{0,1:T(4,128)S(1)} %multiply_reduce_fusion.3), channel_id=1, replica_groups=mesh['dp'=16,'mp'=8] {'dp'}, use_global_device_ids=true, to_apply=%region_5.0 | all-reduce | flops 64 | bytes 512 | tf_op jit(solution)/shard_map/psum | solution.py:95
  453.8 46.5 %reduce.1 = bf16[8192,4]{1,0:T(8,128)(2,1)} reduce(bf16[8192,1,4]{2,1,0:T(2,128)(2,1)} %bitcast.216, bf16[]{:T(256)} %broadcast.105), dimensions={1}, to_apply=%bitcast.171.reduce_sub_computation | reduce | bytes 131074
  536.4 25.3 %all-gather.10.cloned.1.call-done = bf16[512,1024]{1,0:T(8,128)(2,1)} async-done(((bf16[32,1024]{1,0:T(8,128)(2,1)}), bf16[512,1024]{1,0:T(8,128)(2,1)}) %all-gather.10.cloned.1.call-update) | async-done | bytes 1048592 | tf_op jit(solution)/shard_map/all_gather | solution.py:105
  567.0 20.3 %psum.79 = f32[2]{0:T(128)S(1)} all-reduce(f32[2]{0:T(128)S(1)} %convert_reduce_fusion), channel_id=1, replica_groups=mesh['dp'=16,'mp'=8] {'mp'}, use_global_device_ids=true, to_apply=%region_7.0 | all-reduce | flops 2 | bytes 16 | tf_op jit(solution)/shard_map/psum | solution.py:77
  589.2 50.4 %reduce-scatter.16.cloned.1.call-done = f32[16,4,1024]{2,0,1:T(8,128)} async-done(((f32[16,32,1024]{2,0,1:T(8,128)}), f32[16,4,1024]{2,0,1:T(8,128)}) %reduce-scatter.16.cloned.1.call-update) | async-done | bytes 262160 | tf_op jit(solution)/shard_map/reduce_scatter | solution.py:107
  639.6 78.9 %reduce-scatter.12.cloned.1.call-done = f32[16,4,1024]{2,0,1:T(8,128)} async-done(((f32[16,32,1024]{2,0,1:T(8,128)}), f32[16,4,1024]{2,0,1:T(8,128)}) %reduce-scatter.12.cloned.1.call-update) | async-done | bytes 262160 | tf_op jit(solution)/shard_map/reduce_scatter | solution.py:107
  719.7 28.7 %psum.80 = f32[16,4]{0,1:T(4,128)S(1)} all-reduce(f32[16,4]{0,1:T(4,128)S(1)} %get-tuple-element.51), channel_id=1, replica_groups=mesh['dp'=16,'mp'=8] {'dp'}, use_global_device_ids=true, to_apply=%region_10.0 | all-reduce | flops 64 | bytes 512 | tf_op jit(solution)/shard_map/psum | solution.py:111
  750.2 44.1 %all-gather.12.cloned.1.call-done = bf16[16,32,1024]{2,0,1:T(8,128)(2,1)} async-done(((bf16[16,4,1024]{2,0,1:T(8,128)(2,1)}), bf16[16,32,1024]{2,0,1:T(8,128)(2,1)}) %all-gather.12.cloned.1.call-update) | async-done | bytes 1048592 | tf_op jit(solution)/shard_map/all_gather | solution.py:126
  798.8 59.9 %reduce-scatter.14.cloned.1.call-done = f32[32,1024]{1,0:T(8,128)} async-done(((f32[512,1024]{1,0:T(8,128)}), f32[32,1024]{1,0:T(8,128)}) %reduce-scatter.14.cloned.1.call-update) | async-done | bytes 131088 | tf_op jit(solution)/shard_map/reduce_scatter | solution.py:131
  876.0 38.4 %reduce.2 = f32[8192,4]{1,0:T(8,128)} reduce(f32[8192,1,4]{2,1,0:T(1,128)} %bitcast.215, f32[]{:T(128)} %broadcast.107), dimensions={1}, to_apply=%bitcast.173.reduce_sub_computation | reduce | bytes 262148
  946.1 26.9 %all-reduce.1 = (f32[16,4]{0,1:T(4,128)S(1)}, f32[16,4]{0,1:T(4,128)S(1)}) all-reduce(f32[16,4]{0,1:T(4,128)S(1)} %multiply_reduce_fusion.2, f32[16,4]{0,1:T(4,128)S(1)} %get-tuple-element.56), channel_id=1, replica_groups=mesh['dp'=16,'mp'=8] {'dp'}, use_global_device_ids=true, to_apply=%region_13.0 | all-reduce | flops 128 | bytes 1024 | tf_op jit(solution)/shard_map/psum | solution.py:149
  974.0 29.4 %all_gather.25 = bf16[16,32,512]{2,0,1:T(8,128)(2,1)S(1)} all-gather(bf16[16,4,512]{2,0,1:T(8,128)(2,1)S(1)} %subtract_convert_fusion.1), channel_id=1, replica_groups=mesh['dp'=16,'mp'=8] {'mp'}, dimensions={1}, use_global_device_ids=true | all-gather | bytes 589824 | tf_op jit(solution)/shard_map/all_gather | solution.py:154
  1033.9 42.2 %reduce-scatter.20.cloned.1.call-done = bf16[32,1024]{1,0:T(8,128)(2,1)} async-done(((bf16[512,1024]{1,0:T(8,128)(2,1)}), bf16[32,1024]{1,0:T(8,128)(2,1)}) %reduce-scatter.20.cloned.1.call-update) | async-done | bytes 65552 | tf_op jit(solution)/shard_map/reduce_scatter | solution.py:167
  1076.2 64.7 %reduce-scatter.18.cloned.1.call-done = f32[32,1024]{1,0:T(8,128)} async-done(((f32[512,1024]{1,0:T(8,128)}), f32[32,1024]{1,0:T(8,128)}) %reduce-scatter.18.cloned.1.call-update) | async-done | bytes 131088 | tf_op jit(solution)/shard_map/reduce_scatter | solution.py:131
  1159.2 38.4 %reduce.4 = f32[8192,4]{1,0:T(8,128)} reduce(f32[8192,1,4]{2,1,0:T(1,128)} %bitcast.220, f32[]{:T(128)} %broadcast.107), dimensions={1}, to_apply=%bitcast.175.reduce_sub_computation | reduce | bytes 262148
  1230.2 27.4 %all-reduce = (f32[16,4]{0,1:T(4,128)S(1)}, f32[16,4]{0,1:T(4,128)S(1)}, f32[16,4]{0,1:T(4,128)S(1)}) all-reduce(f32[16,4]{0,1:T(4,128)S(1)} %multiply_reduce_fusion.1, f32[16,4]{0,1:T(4,128)S(1)} %get-tuple-element.50, f32[16,4]{0,1:T(4,128)S(1)} %get-tuple-element.57), channel_id=1, replica_groups=mesh['dp'=16,'mp'=8] {'dp'}, use_global_device_ids=true, to_apply=%region_20.0 | all-reduce | flops 192 | bytes 1536 | tf_op jit(solution)/shard_map/psum | solution.py:149
  1281.6 30.1 %all_gather.27 = bf16[16,32,512]{2,0,1:T(8,128)(2,1)S(1)} all-gather(bf16[16,4,512]{2,0,1:T(8,128)(2,1)S(1)} %subtract_convert_fusion), channel_id=1, replica_groups=mesh['dp'=16,'mp'=8] {'mp'}, dimensions={1}, use_global_device_ids=true | all-gather | bytes 589824 | tf_op jit(solution)/shard_map/all_gather | solution.py:154
  1322.5 72.0 %psum.84 = f32[]{:T(128)} all-reduce(f32[]{:T(128)} %get-tuple-element.63), channel_id=1, replica_groups=mesh['dp'=16,'mp'=8] {'dp','mp'}, use_global_device_ids=true, to_apply=%region_22.0 | all-reduce | flops 1 | bytes 8 | tf_op jit(solution)/shard_map/psum | solution.py:175
  (181 shorter events, 387.2 us)
Async XLA Ops:
  7.2 525.2 %copy-start = (bf16[1024,1024]{1,0:T(8,128)(2,1)S(1)}, bf16[1024,1024]{1,0:T(8,128)(2,1)}, u32[]{:S(2)}) copy-start(bf16[1024,1024]{1,0:T(8,128)(2,1)} %param.13) | copy-start | bytes 6291460
  7.2 90.5 %all-gather.6.cloned.1.call-start = ((), (), s32[]{:S(2)}) async-start(), calls=%async_computation.16 | async-start | bytes 3342336 | tf_op jit(solution)/shard_map/all_gather | solution.py:73
  62.7 113.3 %reduce-scatter.8.cloned.1.call-start = ((), (), s32[]{:S(2)}) async-start(), calls=%async_computation.17 | async-start | bytes 1179648 | tf_op jit(solution)/shard_map/reduce_scatter | solution.py:92
  102.2 103.9 %copy-start.20 = (f32[512]{0:T(512)S(1)}, f32[512]{0:T(512)}, u32[]{:S(2)}) copy-start(f32[512]{0:T(512)} %param.11) | copy-start | bytes 6148
  105.7 226.3 %all-gather.8.cloned.1.call-start = ((), (), s32[]{:S(2)}) async-start(), calls=%async_computation.18 | async-start | bytes 1114112 | tf_op jit(solution)/shard_map/all_gather | solution.py:105
  302.6 104.0 %reduce-scatter.10.cloned.1.call-start = ((), (), s32[]{:S(2)}) async-start(), calls=%async_computation.19 | async-start | bytes 1179648 | tf_op jit(solution)/shard_map/reduce_scatter | solution.py:92
  335.9 225.9 %all-gather.10.cloned.1.call-start = ((), (), s32[]{:S(2)}) async-start(), calls=%async_computation.20 | async-start | bytes 1114112 | tf_op jit(solution)/shard_map/all_gather | solution.py:105
  532.3 107.3 %reduce-scatter.16.cloned.1.call-start = ((), (), s32[]{:S(2)}) async-start(), calls=%async_computation.24 | async-start | bytes 2359296 | tf_op jit(solution)/shard_map/reduce_scatter | solution.py:107
  536.2 182.2 %reduce-scatter.12.cloned.1.call-start = ((), (), s32[]{:S(2)}) async-start(), calls=%async_computation.21 | async-start | bytes 2359296 | tf_op jit(solution)/shard_map/reduce_scatter | solution.py:107
  564.3 23.6 %copy-start.22 = (s32[2,16,4]{1,2,0:T(4,128)S(1)}, s32[2,16,4]{1,2,0:T(4,128)}, u32[]{:S(2)}) copy-start(s32[2,16,4]{1,2,0:T(4,128)} %param.14) | copy-start | bytes 1540
  566.8 227.4 %all-gather.12.cloned.1.call-start = ((), (), s32[]{:S(2)}) async-start(), calls=%async_computation.22 | async-start | bytes 1179648 | tf_op jit(solution)/shard_map/all_gather | solution.py:126
  750.1 108.6 %reduce-scatter.14.cloned.1.call-start = ((), (), s32[]{:S(2)}) async-start(), calls=%async_computation.23 | async-start | bytes 2228224 | tf_op jit(solution)/shard_map/reduce_scatter | solution.py:131
  798.7 216.9 %all-gather.14.cloned.1.call-start = ((), (), s32[]{:S(2)}) async-start(), calls=%async_computation.25 | async-start | bytes 1179648 | tf_op jit(solution)/shard_map/all_gather | solution.py:126
  943.1 30.0 %copy-start.15 = (f32[16,4,1024]{2,0,1:T(8,128)S(1)}, f32[16,4,1024]{2,0,1:T(8,128)}, u32[]{:S(2)}) copy-start(f32[16,4,1024]{2,0,1:T(8,128)} %reduce-scatter.16.cloned.1.call-done) | copy-start | bytes 786436
  973.9 102.3 %reduce-scatter.20.cloned.1.call-start = ((), (), s32[]{:S(2)}) async-start(), calls=%async_computation.27 | async-start | bytes 1114112 | tf_op jit(solution)/shard_map/reduce_scatter | solution.py:167
  1006.7 134.1 %reduce-scatter.18.cloned.1.call-start = ((), (), s32[]{:S(2)}) async-start(), calls=%async_computation.26 | async-start | bytes 2228224 | tf_op jit(solution)/shard_map/reduce_scatter | solution.py:131
  1142.6 14.0 all-to-all-start.7
  1203.2 15.1 %all-to-all-start.8 = ((f32[16,1,2048]{2,1,0:T(1,128)}), f32[16,1,2048]{2,1,0:T(1,128)S(1)}, u32[]{:S(2)}, u32[]{:S(2)}) async-start(f32[16,1,2048]{2,1,0:T(1,128)} %reshape.164), calls=%async_computation.15 | async-start | bytes 262144 | tf_op jit(solution)/shard_map/all_to_all | solution.py:139
  1281.5 32.4 %copy-start.11 = (bf16[3,512,1024]{2,1,0:T(8,128)(2,1)S(1)}, bf16[3,512,1024]{2,1,0:T(8,128)(2,1)}, u32[]{:S(2)}) copy-start(bf16[3,512,1024]{2,1,0:T(8,128)(2,1)} %all-gather.6.cloned.1.call-done) | copy-start | bytes 9437188
  1318.4 76.8 %copy-start.18 = (f32[3,1024,2]{1,2,0:T(2,128)S(1)}, f32[3,1024,2]{1,2,0:T(2,128)}, u32[]{:S(2)}) copy-start(f32[3,1024,2]{1,2,0:T(2,128)} %param.19) | copy-start | bytes 73732
  1318.4 76.8 %copy-start.19 = (f32[3,1024,2]{1,2,0:T(2,128)S(1)}, f32[3,1024,2]{1,2,0:T(2,128)}, u32[]{:S(2)}) copy-start(f32[3,1024,2]{1,2,0:T(2,128)} %param.17) | copy-start | bytes 73732
  1395.3 10.4 copy-start.9
  1403.0 13.3 copy-start.16
  1403.1 13.3 copy-start.17
  (15 other events, 82.9 us)
Sparse Core Ops, SparseCore 0:
  62.8 34.8 all-gather.5
  105.8 70.1 reduce-scatter.7
  302.7 29.3 all-gather.7
  336.5 69.9 reduce-scatter.9
  532.4 29.3 all-gather.9
  566.0 73.5 reduce-scatter.15
  644.4 74.0 reduce-scatter.11
  750.2 43.9 all-gather.11
  798.8 59.7 reduce-scatter.13
  974.0 41.5 all-gather.13
  1017.9 58.1 reduce-scatter.19
  1078.6 62.2 reduce-scatter.17
where the time goes:
time: 1440 us
  waiting for transfers between devices  588 us (41%)
  blocking collectives  396 us (28%)
  other arithmetic  207 us (14%)
  local copies, waits for them, and re-layouts  181 us (13%)
  matrix products  32.5 us (2%)
  between operations  17 us (1%)
  starting transfers between devices  16.6 us (1%)
    unnamed x5, other arithmetic  170 us
    reduce_scatter x2, waiting for transfers between devices, shards(): lax.psum_scatter(partial_sum.reshape(dp_count, own_rows, -1), 'mp', scatt...  141 us
    reduce_scatter x2, waiting for transfers between devices, shards(): lax.psum_scatter(logit_part.reshape(dp_count, own_rows, -1), 'mp', scatte...  129 us
    reduce_scatter x2, waiting for transfers between devices, shards(): lax.psum_scatter(head_term(jnp.int32(0), own_rows * lax.axis_size('dp')),...  125 us
    unnamed x71, local copies, waits for them, and re-layouts  112 us
    psum x1, blocking collectives, shards(): norm_sq = lax.psum(square_sum, ('dp', 'mp'))  72 us
    all_gather x2, blocking collectives, shards(): lax.all_gather(joining_grad, 'mp', axis=1, tiled=True).reshape(all_rows, -1)  59.5 us
    psum x2, blocking collectives, shards(): squares = lax.psum(jnp.sum(joining * joining, -1), 'dp')  58 us
  transfers between devices with their start and end apart: 14, of which 14 were waited for; matrix products, arithmetic and copies ran while one was open for 3% of the time, Pallas kernels for 0%

commit v1 on v0

v1 whole, which is shorter than its diff:
```python
import jax
import jax.numpy as jnp
from jax import lax
from jax.experimental import pallas as pl
from jax.experimental.pallas import tpu as pltpu
from jax.sharding import Mesh, PartitionSpec as P

D = 8192
STEPS = 2
BLOCK = 256
LANES = 128

norm_eps = 1e-05
clip_norm = 1.0
learn_rate = 0.0003
weight_decay = 0.1
beta_first = 0.9
beta_second = 0.999
step_count = 10.0
adam_eps = 1e-08
scale_eps = 1e-12

bf16 = jnp.bfloat16
f32 = jnp.float32
AXES = ("p", "b", "m")
VMEM = pl.BlockSpec(memory_space=pltpu.VMEM)
SMEM = pl.BlockSpec(memory_space=pltpu.SMEM)


def dot(left, right):
    return jnp.dot(left, right, preferred_element_type=f32)


def contract_last(left, right):
    return lax.dot_general(
        left, right, (((1,), (1,)), ((), ())), preferred_element_type=f32
    )


def contract_first(left, right):
    return lax.dot_general(
        left, right, (((0,), (0,)), ((), ())), preferred_element_type=f32
    )


def halves(value):
    high = lax.reduce_precision(value, 8, 7)
    return high.astype(bf16), (value - high).astype(bf16)


def side_lanes(*columns):
    shape = columns[0].shape[:-1] + (LANES,)
    lane = lax.broadcasted_iota(jnp.int32, shape, len(shape) - 1)
    block = jnp.zeros(shape, bf16)
    for place, column in enumerate(columns):
        block = jnp.where(lane == place, column, block)
    return block


def read_lanes(block, first, last):
    wide = block.astype(f32)
    lane = lax.broadcasted_iota(jnp.int32, wide.shape, wide.ndim - 1)
    inside = (lane >= first) & (lane <= last)
    return jnp.sum(jnp.where(inside, wide, 0.0), -1, keepdims=True)


def half_out_kernel(core, taps, out):
    sets, _, width = taps.shape
    chunks = width // 1024
    other = (1 - core[0]) * 512
    for s in range(sets):
        for chunk in range(chunks):
            start = pl.multiple_of(chunk * 1024 + other, 512)
            out[s, :, chunk * 512 : (chunk + 1) * 512] = taps[s, :, pl.ds(start, 512)]


def half_join_kernel(core, taps, received, out):
    sets, _, width = taps.shape
    chunks = width // 1024
    copies = out.shape[0] // chunks
    own = core[0] * 512
    first = core[0] == 0
    for chunk in range(chunks):
        rows = []
        for s in range(sets):
            start = pl.multiple_of(chunk * 1024 + own, 512)
            mine = taps[s, :, pl.ds(start, 512)].astype(f32)
            theirs = received[s, :, chunk * 512 : (chunk + 1) * 512].astype(f32)
            rows.append(jnp.where(first, mine, theirs))
            rows.append(jnp.where(first, theirs, mine))
        block = jnp.concatenate(rows, axis=0).astype(bf16)
        for copy in range(copies):
            out[chunk * copies + copy] = block


def grad_kernel(core, left, left_later, right, right_later, grad, squares):
    value = contract_first(left[0, 0], right[0]) + contract_first(
        left_later[0, 0], right_later[0]
    )
    grad[0] = value
    total = jnp.sum((value * value).reshape(-1, 8, 512), 0)
    folded = total[:, :128] + total[:, 128:256] + total[:, 256:384] + total[:, 384:]
    start = (pl.program_id(0) == 0) & (pl.program_id(1) == 0)

    @pl.when(start)
    def _():
        squares[...] = folded

    @pl.when(jnp.logical_not(start))
    def _():
        squares[...] += folded


def gradients(core, left, right):
    tokens = left.shape[2]

    def left_block(s, h, core):
        return (h ^ core[0], s, 0, 0)

    def left_later_block(s, h, core):
        return (h ^ core[0], jnp.where(s == 2, 3, s), 0, 0)

    return pl.pallas_call(
        grad_kernel,
        grid_spec=pltpu.PrefetchScalarGridSpec(
            num_scalar_prefetch=1,
            grid=(3, 2),
            in_specs=[
                pl.BlockSpec((1, 1, tokens, 512), left_block),
                pl.BlockSpec((1, 1, tokens, 512), left_later_block),
                pl.BlockSpec((1, tokens, 512), lambda s, h, core: (0, 0, 0)),
                pl.BlockSpec(
                    (1, tokens, 512), lambda s, h, core: (jnp.where(s == 2, 2, 1), 0, 0)
                ),
            ],
            out_specs=[
                pl.BlockSpec((1, 512, 512), lambda s, h, core: (s, h, 0)),
                pl.BlockSpec((8, 128), lambda s, h, core: (0, 0)),
            ],
        ),
        out_shape=[
            jax.ShapeDtypeStruct((3, 1024, 512), f32),
            jax.ShapeDtypeStruct((8, 128), f32),
        ],
        compiler_params=pltpu.CompilerParams(vmem_limit_bytes=40 * 2**20),
        cost_estimate=pl.CostEstimate(
            flops=6 * 4 * 512 * 512 * 512, bytes_accessed=10 * 2**20, transcendentals=0
        ),
        name="gradients",
    )(core, left, left, right, right)


def adam_kernel(
    clip, weight, grad, first, second, first_scale, second_scale,
    new_weight, new_first, new_second, new_first_scale, new_second_scale,
):
    rows = weight.shape[1]
    clip_value = clip[0]
    old_scales = jnp.concatenate(
        [first_scale[0], second_scale[0], jnp.zeros((4, rows), f32)], axis=0
    ).T
    new_columns = []
    for block in range(2):
        span = slice(block * BLOCK, (block + 1) * BLOCK)
        clipped = grad[0, :, span] * clip_value
        first_new = (
            first[0, :, span].astype(f32) * (beta_first * old_scales[:, block : block + 1])
            + (1.0 - beta_first) * clipped
        )
        second_new = (
            second[0, :, span].astype(f32)
            * (beta_second * old_scales[:, 2 + block : 3 + block])
            + (1.0 - beta_second) * clipped * clipped
        )
        current = weight[0, :, span].astype(f32)
        update = (
            first_new
            * (1.0 / (1.0 - beta_first**step_count))
            / (jnp.sqrt(second_new * (1.0 / (1.0 - beta_second**step_count))) + adam_eps)
            + weight_decay * current
        )
        new_weight[0, :, span] = (current - learn_rate * update).astype(bf16)
        first_top = jnp.max(jnp.abs(first_new), -1, keepdims=True) + scale_eps
        second_top = jnp.max(jnp.abs(second_new), -1, keepdims=True) + scale_eps
        new_first[0, :, span] = (first_new * (1.0 / first_top)).astype(bf16)
        new_second[0, :, span] = (second_new * (1.0 / second_top)).astype(bf16)
        new_columns.append((first_top, second_top))
    lane = lax.broadcasted_iota(jnp.int32, (rows, LANES), 1)
    table = jnp.zeros((rows, LANES), f32)
    for block, (first_top, second_top) in enumerate(new_columns):
        table = jnp.where(lane == block, first_top, table)
        table = jnp.where(lane == 2 + block, second_top, table)
    turned = table.T
    new_first_scale[0] = turned[0:2]
    new_second_scale[0] = turned[2:4]


def adam(clip, weight, grad, first, second, first_scale, second_scale):
    rows = 256
    wide = pl.BlockSpec((1, rows, 512), lambda s, i: (s, i, 0))
    thin = pl.BlockSpec((1, 2, rows), lambda s, i: (s, 0, i))
    return pl.pallas_call(
        adam_kernel,
        grid=(3, 1024 // rows),
        in_specs=[SMEM, wide, wide, wide, wide, thin, thin],
        out_specs=[wide, wide, wide, thin, thin],
        out_shape=[
            jax.ShapeDtypeStruct((3, 1024, 512), bf16),
            jax.ShapeDtypeStruct((3, 1024, 512), bf16),
            jax.ShapeDtypeStruct((3, 1024, 512), bf16),
            jax.ShapeDtypeStruct((3, 2, 1024), f32),
            jax.ShapeDtypeStruct((3, 2, 1024), f32),
        ],
        compiler_params=pltpu.CompilerParams(vmem_limit_bytes=40 * 2**20),
        name="update",
    )(clip, weight, grad, first, second, first_scale, second_scale)


def shards(
    taps, gain, join_weight, head_weight, targets, masks,
    first_codes, first_scales, second_codes, second_scales,
):
    row_count = lax.axis_size("p")
    column_count = lax.axis_size("m")
    core_count = lax.axis_size("b")
    core = lax.axis_index("b")
    core_array = core.reshape(1).astype(jnp.int32)
    turn_pairs = [
        ((p * core_count + b) * column_count + m, (m * core_count + b) * column_count + p)
        for p in range(row_count)
        for b in range(core_count)
        for m in range(column_count)
    ]

    def turn(value):
        return lax.ppermute(value, AXES, turn_pairs)

    def swap(value):
        return lax.ppermute(value, "b", [(0, 1), (1, 0)])

    def exchange(value, axis):
        return lax.all_to_all(value, axis, 0, 0, tiled=False)

    def spread(value, axis):
        copies = lax.axis_size(axis)
        return exchange(jnp.broadcast_to(value, (copies,) + value.shape), axis)

    def own_rows(weight):
        return lax.dynamic_slice_in_dim(weight, core * 512, 512, weight.ndim - 2)

    def other_rows(weight):
        return lax.dynamic_slice_in_dim(weight, (1 - core) * 512, 512, weight.ndim - 2)

    join_own, join_other = own_rows(join_weight), other_rows(join_weight)
    head_own, head_other = own_rows(head_weight), other_rows(head_weight)
    target_ids = targets.reshape(STEPS, 64, 1)
    mask_float = masks.astype(f32).reshape(STEPS, 64, 1)
    live = jnp.sum(mask_float, axis=1, keepdims=True)
    gain_row = gain.reshape(1, 512)

    with jax.named_scope("taps_in"):
        outgoing = pl.pallas_call(
            half_out_kernel,
            in_specs=[SMEM, VMEM],
            out_specs=VMEM,
            out_shape=jax.ShapeDtypeStruct((3, 4, D // 2), bf16),
            name="half_out",
        )(core_array, taps)
        incoming = swap(outgoing)
        packed = pl.pallas_call(
            half_join_kernel,
            in_specs=[SMEM, VMEM, VMEM],
            out_specs=VMEM,
            out_shape=jax.ShapeDtypeStruct((64, 24, 512), bf16),
            compiler_params=pltpu.CompilerParams(vmem_limit_bytes=24 * 2**20),
            name="half_join",
        )(core_array, taps, incoming)
        landed = exchange(packed, ("m", "p"))
        taps_own = landed.reshape(64, 3, 8, 512).transpose(1, 0, 2, 3).reshape(3, 512, 512)
        taps_other = swap(taps_own)

    with jax.named_scope("join_first"):
        constant_part = (
            dot(taps_own[0], join_own[0])
            + dot(taps_own[1], join_own[1])
            + dot(taps_other[0], join_other[0])
            + dot(taps_other[1], join_other[1])
        )
        top_part = dot(taps_own[2], join_own[2]) + dot(taps_other[2], join_other[2])
        parts = jnp.concatenate(
            [constant_part.astype(bf16), top_part.astype(bf16)], axis=1
        ).reshape(8, 64, 1024)
        sums = jnp.sum(exchange(parts, "m").astype(f32), 0)
        constant = sums[:, :512]
        joining_first = constant + sums[:, 512:]

    def to_columns(joining):
        squares = jnp.sum(joining * joining, -1, keepdims=True)
        payload = jnp.concatenate(
            [(joining * gain_row).astype(bf16), side_lanes(*halves(squares))], axis=1
        )
        mine = spread(turn(payload), "p").reshape(512, 640)
        theirs = swap(mine)
        both = read_lanes(mine[:, 512:], 0, 1) + read_lanes(theirs[:, 512:], 0, 1)
        return mine[:, :512], theirs[:, :512], both

    with jax.named_scope("hidden_first"):
        hidden_own, hidden_other, squares_first = to_columns(joining_first)

    with jax.named_scope("join_second"):
        part = dot(hidden_own, join_own[2]) + dot(hidden_other, join_other[2])
        live_rows = jnp.broadcast_to(live, (STEPS, 512, 1)).astype(bf16)
        payload = jnp.concatenate(
            [part.astype(bf16), side_lanes(*halves(squares_first), live_rows[0], live_rows[1])],
            axis=1,
        )
        got = exchange(payload.reshape(8, 64, 640), "m")
        sums = jnp.sum(got.astype(f32), 0)
        inverse_first = lax.rsqrt(read_lanes(sums[:, 512:], 0, 1) / D + norm_eps)
        counts = [read_lanes(sums[:, 512:], 2, 2), read_lanes(sums[:, 512:], 3, 3)]
        fed_back = inverse_first * sums[:, :512]
        joining_second = constant + fed_back
        logit_part_first = dot(hidden_own, head_own) + dot(hidden_other, head_other)

    with jax.named_scope("hidden_second"):
        later_own, later_other, squares_second = to_columns(joining_second)

    with jax.named_scope("logits"):
        logit_part_second = dot(later_own, head_own) + dot(later_other, head_other)
        payload = jnp.concatenate(
            [
                logit_part_second.astype(bf16),
                logit_part_first.astype(bf16),
                side_lanes(*halves(squares_second)),
            ],
            axis=1,
        )
        got = exchange(payload.reshape(8, 64, 2176), "m")
        sums = jnp.sum(got.astype(f32), 0)
        inverse_second = lax.rsqrt(read_lanes(sums[:, 2048:], 0, 1) / D + norm_eps)
        logits = [inverse_first * sums[:, 1024:2048], inverse_second * sums[:, :1024]]

    with jax.named_scope("softmax"):
        vocab = lax.broadcasted_iota(jnp.int32, (64, 1024), 1) + (
            lax.axis_index("p") * core_count + core
        ) * 1024
        hits = [vocab == target_ids[k] for k in range(STEPS)]
        stats = []
        for k in range(STEPS):
            top = jnp.max(logits[k], -1)
            weights = jnp.exp(logits[k] - top[:, None])
            stats += [
                top,
                jnp.sum(weights, -1),
                jnp.sum(weights * logits[k], -1),
                jnp.sum(jnp.where(hits[k], logits[k], 0.0), -1),
            ]
        shared = spread(jnp.stack(stats), ("p", "b"))
        loss_local = jnp.zeros((1, 1), f32)
        grad_rows, turns = [], []
        for k in range(STEPS):
            tops = shared[:, 4 * k]
            top = jnp.max(tops, 0)
            factor = jnp.exp(tops - top)
            total = jnp.sum(shared[:, 4 * k + 1] * factor, 0)
            mean = jnp.sum(shared[:, 4 * k + 2] * factor, 0) / total
            picked = jnp.sum(shared[:, 4 * k + 3], 0)
            log_total = top + jnp.log(total)
            columns = jnp.stack([log_total, log_total - picked, mean - picked], 1)
            token_weight = mask_float[k] / counts[k]
            loss_local += jnp.sum(token_weight * columns[:, 1:2], 0, keepdims=True)
            turns.append(token_weight * columns[:, 2:3])
            probs = jnp.exp(logits[k] - columns[:, 0:1])
            grad_rows.append(
                (token_weight * (probs - hits[k].astype(f32))).astype(bf16)
            )

    with jax.named_scope("logit_grads"):
        all_grads = spread(jnp.concatenate(grad_rows, 1), "m").reshape(512, 2048)
        grads_first, grads_second = all_grads[:, :1024], all_grads[:, 1024:]

    with jax.named_scope("back_second"):
        away = swap(contract_last(grads_second, head_other).astype(bf16))
        kept = contract_last(grads_second, head_own) + away.astype(f32)
        landed = exchange(kept.astype(bf16).reshape(8, 64, 512), "p")
        row_grad = turn(jnp.sum(landed.astype(f32), 0).astype(bf16)).astype(f32)
        back_second = (
            inverse_second * gain_row * row_grad
            - (inverse_second * inverse_second * turns[1] / D) * joining_second
        ).astype(bf16)
        inner = jnp.sum(back_second.astype(f32) * fed_back, -1, keepdims=True)
        loss_rows = jnp.broadcast_to(loss_local, (64, 1))
        payload = jnp.concatenate(
            [back_second, side_lanes(*halves(inner), *halves(inverse_first), *halves(loss_rows))],
            axis=1,
        )
        got = spread(payload, "m")
        loss = jnp.sum(read_lanes(got[:, 0, 512:], 4, 5))
        got = got.reshape(512, 640)
        second_all = got[:, :512]
        inner_all = read_lanes(got[:, 512:], 0, 1)
        second_scaled = (
            second_all.astype(f32) * read_lanes(got[:, 512:], 2, 3)
        ).astype(bf16)

    with jax.named_scope("back_first"):
        away = contract_last(second_all, join_other[2]) + contract_last(grads_first, head_other)
        away = swap(
            jnp.concatenate([away.astype(bf16), side_lanes(*halves(inner_all))], axis=1)
        )
        kept = (
            contract_last(second_all, join_own[2])
            + contract_last(grads_first, head_own)
            + away[:, :512].astype(f32)
        )
        inner_chip = inner_all + read_lanes(away[:, 512:], 0, 1)
        payload = jnp.concatenate([kept.astype(bf16), side_lanes(*halves(inner_chip))], axis=1)
        landed = jnp.sum(exchange(payload.reshape(8, 64, 640), "p").astype(f32), 0)
        payload = jnp.concatenate(
            [
                landed[:, :512].astype(bf16),
                side_lanes(*halves(read_lanes(landed[:, 512:], 0, 1))),
            ],
            axis=1,
        )
        row_grad = turn(payload)
        inner = turns[0] + read_lanes(row_grad[:, 512:], 0, 1)
        back_first = (
            inverse_first * gain_row * row_grad[:, :512].astype(f32)
            - (inverse_first * inverse_first * inner / D) * joining_first
        ).astype(bf16)
        first_all = spread(back_first, "m").reshape(512, 512)

    with jax.named_scope("gradients"):
        left = jnp.stack(
            [
                jnp.concatenate([taps_own, hidden_own[None]], 0),
                jnp.concatenate([taps_other, hidden_other[None]], 0),
            ]
        )
        right = jnp.stack([first_all, second_all, second_scaled])
        grads, squares = gradients(core_array, left, right)
        square_sum = jnp.broadcast_to(jnp.sum(squares), (1, LANES))
        norm_sq = jnp.sum(spread(square_sum, AXES)[:, 0, 0])
        clip = jnp.minimum(1.0, clip_norm / (jnp.sqrt(norm_sq) + 1e-06))

    with jax.named_scope("update"):
        new_join, new_first, new_second, first_scale, second_scale = adam(
            clip.reshape(1),
            join_weight,
            grads,
            first_codes,
            second_codes,
            jnp.swapaxes(first_scales, 1, 2),
            jnp.swapaxes(second_scales, 1, 2),
        )
    return (
        new_join,
        new_first,
        jnp.swapaxes(first_scale, 1, 2),
        new_second,
        jnp.swapaxes(second_scale, 1, 2),
        loss,
    )


def solution(mesh):
    rows = mesh.shape["dp"] // 2
    fine = Mesh(mesh.devices.reshape(rows, 2, mesh.shape["mp"]), AXES)
    dp, mp = ("p", "b"), "m"
    return jax.shard_map(
        shards,
        mesh=fine,
        in_specs=(
            P(None, ("p", "b", "m"), None),
            P(dp),
            P(None, mp, dp),
            P(mp, dp),
            P(None, None, mp),
            P(None, None, mp),
            P(None, mp, dp),
            P(None, mp, dp),
            P(None, mp, dp),
            P(None, mp, dp),
        ),
        out_specs=(
            P(None, mp, dp),
            P(None, mp, dp),
            P(None, mp, dp),
            P(None, mp, dp),
            P(None, mp, dp),
            P(),
        ),
        check_vma=False,
    )
```

time: 1440 us -> 419 us (0.29)
  waiting for transfers between devices: 588 us -> 118 us
  blocking collectives: 396 us -> 115 us
  other arithmetic: 207 us -> 34.9 us
  local copies, waits for them, and re-layouts: 181 us -> 26.6 us
  starting transfers between devices: 16.6 us -> 72.3 us
  Pallas kernels: 0 us -> 21.4 us
    reduce_scatter x7 -> x0, waiting for transfers between devices: 437 us -> none  [the longest x2 141 us: shards(): lax.psum_scatter(partial_sum.reshape(dp_count, own_rows, -1), 'mp', scatt...]
    psum x8 -> x0, blocking collectives: 250 us -> none  [the longest x1 72 us: shards(): norm_sq = lax.psum(square_sum, ('dp', 'mp'))]
    unnamed x5 -> x0, other arithmetic: 170 us -> none
    all_gather x5 -> x0, waiting for transfers between devices: 143 us -> none  [the longest x2 54.7 us: shards(): lax.all_gather(moved.reshape(own_rows, -1), 'dp', axis=0, tiled=True)]
    all_to_all x2 -> x9, waiting for transfers between devices: 7.87 us -> 115 us  [exchange(): return lax.all_to_all(value, axis, 0, 0, tiled=False)]
    unnamed x71 -> x81, local copies, waits for them, and re-layouts: 112 us -> 12.8 us
    all_gather x2 -> x0, blocking collectives: 59.5 us -> none  [shards(): lax.all_gather(joining_grad, 'mp', axis=1, tiled=True).reshape(all_rows, -1)]
    all_to_all x12 -> x1, local copies, waits for them, and re-layouts: 53 us -> 0.51 us  [exchange(): return lax.all_to_all(value, axis, 0, 0, tiled=False)]
  transfers between devices with their start and end apart: 14 -> 19, of which waited for: 14 -> 13; matrix products, arithmetic and copies ran while one was open for 3% -> 5% of each run, Pallas kernels for 0% -> 0%
where the time goes in v1:
time: 419 us; the launch traced here: 417 us
  waiting for transfers between devices  118 us (28%)
  blocking collectives  115 us (27%)
  starting transfers between devices  72.3 us (17%)
  other arithmetic  34.9 us (8%)
  local copies, waits for them, and re-layouts  26.6 us (6%)
  matrix products  22.6 us (5%)
  Pallas kernels  21.4 us (5%)
  between operations  5.46 us (1%)
    all_to_all x4, blocking collectives, exchange(): return lax.all_to_all(value, axis, 0, 0, tiled=False)  115 us
    all_to_all x9, waiting for transfers between devices, exchange(): return lax.all_to_all(value, axis, 0, 0, tiled=False)  115 us
    all_to_all x9, starting transfers between devices, exchange(): return lax.all_to_all(value, axis, 0, 0, tiled=False)  56.8 us
    dot_general x12, matrix products, dot(): return jnp.dot(left, right, preferred_element_type=f32)  15.6 us
    pallas_call x1, Pallas kernels, adam(): pl.pallas_call(adam_kernel, grid=(3, 1024 // rows), in_specs=[SMEM, wide,...  15.1 us
    ppermute x6, starting transfers between devices, swap(): return lax.ppermute(value, 'b', [(0, 1), (1, 0)])  12.8 us
    unnamed x81, local copies, waits for them, and re-layouts  12.8 us
  transfers between devices with their start and end apart: 19, of which 13 were waited for; matrix products, arithmetic and copies ran while one was open for 5% of the time, Pallas kernels for 0%

profile of v1, /device:TPU:1, one launch (start us, length us, event | category | flops | bytes accessed | tf_op | source)
XLA Modules:
  0.0 416.6 jit_solution(650183155416839873)
XLA Ops:
  6.0 33.6 %all_to_all.65 = bf16[64,24,512]{2,1,0:T(8,128)(2,1)S(1)} all-to-all(bf16[64,24,512]{2,1,0:T(8,128)(2,1)S(1)} %half_join.1), channel_id=1, replica_groups=mesh['p'=8,'b'=2,'m'=8] {'m','p'}, dimensions={0} | all-to-all | bytes 3145728 | tf_op jit(solution)/shard_map/taps_in/all_to_all | solution.py:242
  56.5 4.4 %all-to-all-start.1 = ((bf16[8,64,1024]{2,1,0:T(8,128)(2,1)}), bf16[8,64,1024]{2,1,0:T(8,128)(2,1)}, u32[]{:S(2)}, u32[]{:S(2)}) async-start(bf16[8,64,1024]{2,1,0:T(8,128)(2,1)} %bitcast.119), calls=%async_computation.1 | async-start | bytes 2097152 | tf_op jit(solution)/shard_map/join_first/all_to_all | solution.py:242
  60.9 17.4 %all-to-all-done.1 = bf16[8,64,1024]{2,1,0:T(8,128)(2,1)} async-done(((bf16[8,64,1024]{2,1,0:T(8,128)(2,1)}), bf16[8,64,1024]{2,1,0:T(8,128)(2,1)}, u32[]{:S(2)}, u32[]{:S(2)}) %all-to-all-start.1) | async-done | bytes 1048608 | tf_op jit(solution)/shard_map/join_first/all_to_all | solution.py:242
  80.7 23.9 %all_to_all.66 = bf16[8,64,640]{2,1,0:T(8,128)(2,1)S(1)} all-to-all(bf16[8,64,640]{2,1,0:T(8,128)(2,1)S(1)} %broadcast_in_dim.209), channel_id=1, replica_groups=mesh['p'=8,'b'=2,'m'=8] {'p'}, dimensions={0} | all-to-all | bytes 1310720 | tf_op jit(solution)/shard_map/hidden_first/all_to_all | solution.py:242
  119.0 4.2 %all-to-all-start.3 = ((bf16[8,64,640]{2,1,0:T(8,128)(2,1)}), bf16[8,64,640]{2,1,0:T(8,128)(2,1)}, u32[]{:S(2)}, u32[]{:S(2)}) async-start(bf16[8,64,640]{2,1,0:T(8,128)(2,1)} %bitcast.124), calls=%async_computation.3 | async-start | bytes 1310720 | tf_op jit(solution)/shard_map/join_second/all_to_all | solution.py:242
  123.3 13.2 %all-to-all-done.3 = bf16[8,64,640]{2,1,0:T(8,128)(2,1)} async-done(((bf16[8,64,640]{2,1,0:T(8,128)(2,1)}), bf16[8,64,640]{2,1,0:T(8,128)(2,1)}, u32[]{:S(2)}, u32[]{:S(2)}) %all-to-all-start.3) | async-done | bytes 655392 | tf_op jit(solution)/shard_map/join_second/all_to_all | solution.py:242
  140.9 22.1 %all_to_all.67 = bf16[8,64,640]{2,1,0:T(8,128)(2,1)S(1)} all-to-all(bf16[8,64,640]{2,1,0:T(8,128)(2,1)S(1)} %broadcast_in_dim.222), channel_id=1, replica_groups=mesh['p'=8,'b'=2,'m'=8] {'p'}, dimensions={0} | all-to-all | bytes 1310720 | tf_op jit(solution)/shard_map/hidden_second/all_to_all | solution.py:242
  163.0 3.7 collective-permute-start.5
  171.8 5.3 %all-to-all-start.5 = ((bf16[8,64,2176]{2,1,0:T(8,128)(2,1)}), bf16[8,64,2176]{2,1,0:T(8,128)(2,1)}, u32[]{:S(2)}, u32[]{:S(2)}) async-start(bf16[8,64,2176]{2,1,0:T(8,128)(2,1)} %bitcast.113), calls=%async_computation.5 | async-start | bytes 4456448 | tf_op jit(solution)/shard_map/logits/all_to_all | solution.py:242
  177.5 29.7 %all-to-all-done.5 = bf16[8,64,2176]{2,1,0:T(8,128)(2,1)} async-done(((bf16[8,64,2176]{2,1,0:T(8,128)(2,1)}), bf16[8,64,2176]{2,1,0:T(8,128)(2,1)}, u32[]{:S(2)}, u32[]{:S(2)}) %all-to-all-start.5) | async-done | bytes 2228256 | tf_op jit(solution)/shard_map/logits/all_to_all | solution.py:242
  210.7 4.1 all-to-all-start.6
  214.9 5.7 %all-to-all-done.6 = f32[16,1,512]{2,1,0:T(1,128)S(1)} async-done(((f32[16,1,512]{2,1,0:T(1,128)}), f32[16,1,512]{2,1,0:T(1,128)S(1)}, u32[]{:S(2)}, u32[]{:S(2)}) %all-to-all-start.6) | async-done | bytes 32800 | tf_op jit(solution)/shard_map/softmax/all_to_all | solution.py:242
  225.6 35.3 %all_to_all.68 = bf16[8,64,2048]{2,1,0:T(8,128)(2,1)S(1)} all-to-all(bf16[8,64,2048]{2,1,0:T(8,128)(2,1)S(1)} %broadcast_in_dim.227), channel_id=1, replica_groups=mesh['p'=8,'b'=2,'m'=8] {'m'}, dimensions={0} | all-to-all | bytes 4194304 | tf_op jit(solution)/shard_map/logit_grads/all_to_all | solution.py:242
  270.5 8.6 %all-to-all-done.8 = bf16[8,64,512]{2,1,0:T(8,128)(2,1)S(1)} async-done(((bf16[8,64,512]{2,1,0:T(8,128)(2,1)}), bf16[8,64,512]{2,1,0:T(8,128)(2,1)S(1)}, u32[]{:S(2)}, u32[]{:S(2)}) %all-to-all-start.8) | async-done | bytes 524320 | tf_op jit(solution)/shard_map/back_second/all_to_all | solution.py:242
  285.8 11.5 %all-to-all-start.9 = ((bf16[8,64,640]{2,1,0:T(8,128)(2,1)}), bf16[8,64,640]{2,1,0:T(8,128)(2,1)S(1)}, u32[]{:S(2)}, u32[]{:S(2)}) async-start(bf16[8,64,640]{2,1,0:T(8,128)(2,1)} %broadcast_in_dim.235), calls=%async_computation.9 | async-start | bytes 1310720 | tf_op jit(solution)/shard_map/back_second/all_to_all | solution.py:242
  297.4 13.1 %all-to-all-done.9 = bf16[8,64,640]{2,1,0:T(8,128)(2,1)S(1)} async-done(((bf16[8,64,640]{2,1,0:T(8,128)(2,1)}), bf16[8,64,640]{2,1,0:T(8,128)(2,1)S(1)}, u32[]{:S(2)}, u32[]{:S(2)}) %all-to-all-start.9) | async-done | bytes 655392 | tf_op jit(solution)/shard_map/back_second/all_to_all | solution.py:242
  320.7 4.2 %all-to-all-start.10 = ((bf16[8,64,640]{2,1,0:T(8,128)(2,1)}), bf16[8,64,640]{2,1,0:T(8,128)(2,1)}, u32[]{:S(2)}, u32[]{:S(2)}) async-start(bf16[8,64,640]{2,1,0:T(8,128)(2,1)} %bitcast.123), calls=%async_computation.10 | async-start | bytes 1310720 | tf_op jit(solution)/shard_map/back_first/all_to_all | solution.py:242
  329.4 7.1 %all-to-all-done.10 = bf16[8,64,640]{2,1,0:T(8,128)(2,1)} async-done(((bf16[8,64,640]{2,1,0:T(8,128)(2,1)}), bf16[8,64,640]{2,1,0:T(8,128)(2,1)}, u32[]{:S(2)}, u32[]{:S(2)}) %all-to-all-start.10) | async-done | bytes 655392 | tf_op jit(solution)/shard_map/back_first/all_to_all | solution.py:242
  340.5 15.2 %all-to-all-start.11 = ((bf16[8,64,512]{2,1,0:T(8,128)(2,1)}), bf16[8,64,512]{2,1,0:T(8,128)(2,1)}, u32[]{:S(2)}, u32[]{:S(2)}) async-start(bf16[8,64,512]{2,1,0:T(8,128)(2,1)} %broadcast_in_dim.242), calls=%async_computation.11 | async-start | bytes 1048576 | tf_op jit(solution)/shard_map/back_first/all_to_all | solution.py:242
  356.7 10.8 %all-to-all-done.11 = bf16[8,64,512]{2,1,0:T(8,128)(2,1)} async-done(((bf16[8,64,512]{2,1,0:T(8,128)(2,1)}), bf16[8,64,512]{2,1,0:T(8,128)(2,1)}, u32[]{:S(2)}, u32[]{:S(2)}) %all-to-all-start.11) | async-done | bytes 524320 | tf_op jit(solution)/shard_map/back_first/all_to_all | solution.py:242
  371.0 4.5 %gradients.1 = (f32[3,1024,512]{2,1,0:T(8,128)S(1)}, f32[8,128]{1,0:T(8,128)S(1)}) custom-call(s32[1]{0:T(128)} %bitcast.core, bf16[2,4,512,512]{3,2,1,0:T(8,128)(2,1)S(1)} %copy-done.4, bf16[2,4,512,512]{3,2,1,0:T(8,128)(2,1)S(1)} %copy-done.4, bf16[3,512,512]{2,1,0:T(8,128)(2,1)S(1)} %pad_maximum_fusion.2.right.right_later, ...), custom_call_target="tpu_custom_call" | custom-call | flops 3221225472 | bytes 10485760 | tf_op jit(solution)/shard_map/gradients/gradients/pallas_call | solution.py:123
  380.2 4.4 %all-to-all-start.12 = ((f32[128,1,128]{2,1,0:T(1,128)}), f32[128,1,128]{2,1,0:T(1,128)S(1)}, u32[]{:S(2)}, u32[]{:S(2)}) async-start(f32[128,1,128]{2,1,0:T(1,128)} %broadcast_in_dim.243), calls=%async_computation.12 | async-start | bytes 131072 | tf_op jit(solution)/shard_map/gradients/all_to_all | solution.py:242
  385.2 9.1 %all-to-all-done.12 = f32[128,1,128]{2,1,0:T(1,128)S(1)} async-done(((f32[128,1,128]{2,1,0:T(1,128)}), f32[128,1,128]{2,1,0:T(1,128)S(1)}, u32[]{:S(2)}, u32[]{:S(2)}) %all-to-all-start.12) | async-done | bytes 65568 | tf_op jit(solution)/shard_map/gradients/all_to_all | solution.py:242
  401.5 15.1 %update.1 = (bf16[3,1024,512]{2,1,0:T(8,128)(2,1)}, bf16[3,1024,512]{2,1,0:T(8,128)(2,1)}, bf16[3,1024,512]{2,1,0:T(8,128)(2,1)}, f32[3,2,1024]{2,1,0:T(2,128)}, f32[3,2,1024]{2,1,0:T(2,128)}) custom-call(f32[1]{0:T(128)} %bitcast.54.clip, bf16[3,1024,512]{2,1,0:T(8,128)(2,1)S(1)} %copy-done.2, f32[3,1024,512]{2,1,0:T(8,128)} %copy-done.3, ...), custom_call_target="tpu_custom_call" | custom-call | tf_op jit(solution)/shard_map/update/update/pallas_call | solution.py:202
  (233 shorter events, 105.0 us)
Async XLA Ops:
  0.6 166.1 %copy-start = (bf16[1024,1024]{1,0:T(8,128)(2,1)S(1)}, bf16[1024,1024]{1,0:T(8,128)(2,1)}, u32[]{:S(2)}) copy-start(bf16[1024,1024]{1,0:T(8,128)(2,1)} %param.13) | copy-start | bytes 6291460
  2.4 2.6 collective-permute-start
  41.5 7.0 %collective-permute-start.1 = (bf16[3,512,512]{2,1,0:T(8,128)(2,1)}, bf16[3,512,512]{2,1,0:T(8,128)(2,1)}, u32[]{:S(2)}, u32[]{:S(2)}) collective-permute-start(bf16[3,512,512]{2,1,0:T(8,128)(2,1)} %get-tuple-element.59), channel_id=1, source_target_pairs={{0,8},{8,0},{1,9},{9,1},{2,10},{10,2},{3,11},{11,3},{4,12},{12,4},... | collective-permute-start | bytes 4718600 | tf_op jit(solution)/shard_map/taps_in/ppermute | solution.py:239
  56.5 21.8 %all-to-all-start.1 = ((bf16[8,64,1024]{2,1,0:T(8,128)(2,1)}), bf16[8,64,1024]{2,1,0:T(8,128)(2,1)}, u32[]{:S(2)}, u32[]{:S(2)}) async-start(bf16[8,64,1024]{2,1,0:T(8,128)(2,1)} %bitcast.119), calls=%async_computation.1 | async-start | bytes 2097152 | tf_op jit(solution)/shard_map/join_first/all_to_all | solution.py:242
  60.8 46.9 %copy-start.30 = (s32[2,16,4]{1,2,0:T(4,128)S(1)}, s32[2,16,4]{1,2,0:T(4,128)}, u32[]{:S(2)}) copy-start(s32[2,16,4]{1,2,0:T(4,128)} %param.15) | copy-start | bytes 1540
  60.9 48.8 %copy-start.25 = (pred[128]{0:T(512)(128)(4,1)}, pred[128]{0:T(512)(128)(4,1)S(1)}, u32[]{:S(2)}) copy-start(pred[128]{0:T(512)(128)(4,1)S(1)} %get-tuple-element.95) | copy-start | bytes 388
  60.9 48.8 %copy-start.27 = (pred[128]{0:T(512)(128)(4,1)}, pred[128]{0:T(512)(128)(4,1)S(1)}, u32[]{:S(2)}) copy-start(pred[128]{0:T(512)(128)(4,1)S(1)} %get-tuple-element.96) | copy-start | bytes 388
  80.0 0.7 collective-permute-start.2
  104.6 4.8 %collective-permute-start.3 = (bf16[512,640]{1,0:T(8,128)(2,1)S(1)}, bf16[512,640]{1,0:T(8,128)(2,1)S(1)}, u32[]{:S(2)}, u32[]{:S(2)}) collective-permute-start(bf16[512,640]{1,0:T(8,128)(2,1)S(1)} %bitcast.114), channel_id=1, source_target_pairs={{0,8},{8,0},{1,9},{9,1},{2,10},{10,2},{3,11},{11,3},{4,12},{12,4},... | collective-permute-start | bytes 1966088 | tf_op jit(solution)/shard_map/hidden_first/ppermute | solution.py:239
  109.5 57.2 %copy-start.11 = (bf16[512,640]{1,0:T(8,128)(2,1)}, bf16[512,640]{1,0:T(8,128)(2,1)S(1)}, u32[]{:S(2)}) copy-start(bf16[512,640]{1,0:T(8,128)(2,1)S(1)} %collective-permute-done.3) | copy-start | bytes 1966084
  119.0 17.4 %all-to-all-start.3 = ((bf16[8,64,640]{2,1,0:T(8,128)(2,1)}), bf16[8,64,640]{2,1,0:T(8,128)(2,1)}, u32[]{:S(2)}, u32[]{:S(2)}) async-start(bf16[8,64,640]{2,1,0:T(8,128)(2,1)} %bitcast.124), calls=%async_computation.3 | async-start | bytes 1310720 | tf_op jit(solution)/shard_map/join_second/all_to_all | solution.py:242
  140.2 0.7 collective-permute-start.4
  163.0 5.4 %collective-permute-start.5 = (bf16[512,640]{1,0:T(8,128)(2,1)S(1)}, bf16[512,640]{1,0:T(8,128)(2,1)S(1)}, u32[]{:S(2)}, u32[]{:S(2)}) collective-permute-start(bf16[512,640]{1,0:T(8,128)(2,1)S(1)} %bitcast.120), channel_id=1, source_target_pairs={{0,8},{8,0},{1,9},{9,1},{2,10},{10,2},{3,11},{11,3},{4,12},{12,4},... | collective-permute-start | bytes 1966088 | tf_op jit(solution)/shard_map/hidden_second/ppermute | solution.py:239
  171.8 35.4 %all-to-all-start.5 = ((bf16[8,64,2176]{2,1,0:T(8,128)(2,1)}), bf16[8,64,2176]{2,1,0:T(8,128)(2,1)}, u32[]{:S(2)}, u32[]{:S(2)}) async-start(bf16[8,64,2176]{2,1,0:T(8,128)(2,1)} %bitcast.113), calls=%async_computation.5 | async-start | bytes 4456448 | tf_op jit(solution)/shard_map/logits/all_to_all | solution.py:242
  210.7 10.0 %all-to-all-start.6 = ((f32[16,1,512]{2,1,0:T(1,128)}), f32[16,1,512]{2,1,0:T(1,128)S(1)}, u32[]{:S(2)}, u32[]{:S(2)}) async-start(f32[16,1,512]{2,1,0:T(1,128)} %reshape.431), calls=%async_computation.6 | async-start | bytes 65536 | tf_op jit(solution)/shard_map/softmax/all_to_all | solution.py:242
  261.7 3.2 collective-permute-start.6
  266.5 12.6 %all-to-all-start.8 = ((bf16[8,64,512]{2,1,0:T(8,128)(2,1)}), bf16[8,64,512]{2,1,0:T(8,128)(2,1)S(1)}, u32[]{:S(2)}, u32[]{:S(2)}) async-start(bf16[8,64,512]{2,1,0:T(8,128)(2,1)} %bitcast.129), calls=%async_computation.8 | async-start | bytes 1048576 | tf_op jit(solution)/shard_map/back_second/all_to_all | solution.py:242
  279.2 3.8 collective-permute-start.7
  285.8 24.6 %all-to-all-start.9 = ((bf16[8,64,640]{2,1,0:T(8,128)(2,1)}), bf16[8,64,640]{2,1,0:T(8,128)(2,1)S(1)}, u32[]{:S(2)}, u32[]{:S(2)}) async-start(bf16[8,64,640]{2,1,0:T(8,128)(2,1)} %broadcast_in_dim.235), calls=%async_computation.9 | async-start | bytes 1310720 | tf_op jit(solution)/shard_map/back_second/all_to_all | solution.py:242
  313.3 5.4 %collective-permute-start.8 = (bf16[512,640]{1,0:T(8,128)(2,1)S(1)}, bf16[512,640]{1,0:T(8,128)(2,1)S(1)}, u32[]{:S(2)}, u32[]{:S(2)}) collective-permute-start(bf16[512,640]{1,0:T(8,128)(2,1)S(1)} %pad_maximum_fusion.5), channel_id=1, source_target_pairs={{0,8},{8,0},{1,9},{9,1},{2,10},{10,2},{3,11},{11,3},{4,12},{12,4},... | collective-permute-start | bytes 1966088 | tf_op jit(solution)/shard_map/back_first/ppermute | solution.py:239
  320.7 15.7 %all-to-all-start.10 = ((bf16[8,64,640]{2,1,0:T(8,128)(2,1)}), bf16[8,64,640]{2,1,0:T(8,128)(2,1)}, u32[]{:S(2)}, u32[]{:S(2)}) async-start(bf16[8,64,640]{2,1,0:T(8,128)(2,1)} %bitcast.123), calls=%async_computation.10 | async-start | bytes 1310720 | tf_op jit(solution)/shard_map/back_first/all_to_all | solution.py:242
  337.9 1.5 collective-permute-start.9
  340.5 27.0 %all-to-all-start.11 = ((bf16[8,64,512]{2,1,0:T(8,128)(2,1)}), bf16[8,64,512]{2,1,0:T(8,128)(2,1)}, u32[]{:S(2)}, u32[]{:S(2)}) async-start(bf16[8,64,512]{2,1,0:T(8,128)(2,1)} %broadcast_in_dim.242), calls=%async_computation.11 | async-start | bytes 1048576 | tf_op jit(solution)/shard_map/back_first/all_to_all | solution.py:242
  380.2 14.2 %all-to-all-start.12 = ((f32[128,1,128]{2,1,0:T(1,128)}), f32[128,1,128]{2,1,0:T(1,128)S(1)}, u32[]{:S(2)}, u32[]{:S(2)}) async-start(f32[128,1,128]{2,1,0:T(1,128)} %broadcast_in_dim.243), calls=%async_computation.12 | async-start | bytes 131072 | tf_op jit(solution)/shard_map/gradients/all_to_all | solution.py:242
  (34 other events, 397.1 us)

commit v2 on v1

v2 whole, which is shorter than its diff:
```python
import jax
import jax.numpy as jnp
from jax import lax
from jax.experimental import pallas as pl
from jax.experimental.pallas import tpu as pltpu
from jax.sharding import Mesh, PartitionSpec as P

D = 8192
STEPS = 2
BLOCK = 256
LANES = 128

norm_eps = 1e-05
clip_norm = 1.0
learn_rate = 0.0003
weight_decay = 0.1
beta_first = 0.9
beta_second = 0.999
step_count = 10.0
adam_eps = 1e-08
scale_eps = 1e-12

bf16 = jnp.bfloat16
f32 = jnp.float32
AXES = ("p", "b", "m")
VMEM = pl.BlockSpec(memory_space=pltpu.VMEM)
SMEM = pl.BlockSpec(memory_space=pltpu.SMEM)


def dot(left, right):
    return jnp.dot(left, right, preferred_element_type=f32)


def contract_last(left, right):
    return lax.dot_general(
        left, right, (((1,), (1,)), ((), ())), preferred_element_type=f32
    )


def contract_first(left, right):
    return lax.dot_general(
        left, right, (((0,), (0,)), ((), ())), preferred_element_type=f32
    )


def lane_of(shape):
    return lax.broadcasted_iota(jnp.int32, shape, len(shape) - 1)


def put_lanes(rows, columns, first=0):
    lane = lane_of((rows, LANES))
    block = jnp.zeros((rows, LANES), f32)
    for place, column in enumerate(columns):
        block = jnp.where(lane == first + place, column, block)
    return block


def halves(value):
    high = value.astype(bf16).astype(f32)
    return high, (value - high).astype(bf16).astype(f32)


def read_lanes(block, first, last):
    lane = lane_of(block.shape)
    inside = (lane >= first) & (lane <= last)
    return jnp.sum(jnp.where(inside, block, 0.0), -1, keepdims=True)


def sum_chunks(parts, start, stop):
    total = parts[0, :, start:stop].astype(f32)
    for chunk in range(1, parts.shape[0]):
        total += parts[chunk, :, start:stop].astype(f32)
    return total


def flat(ref, start, stop):
    return ref[:, :, start:stop].reshape(-1, stop - start)


def own_half(core):
    return pl.ds(pl.multiple_of(core * 512, 512), 512)


def call(kernel, name, outs, *operands, grid_spec=None):
    options = {}
    if grid_spec is None:
        options["in_specs"] = [
            SMEM if space == "s" else VMEM for space, _ in operands
        ]
        options["out_specs"] = [VMEM] * len(outs)
    else:
        options["grid_spec"] = grid_spec
    result = pl.pallas_call(
        kernel,
        out_shape=[jax.ShapeDtypeStruct(shape, dtype) for shape, dtype in outs],
        compiler_params=pltpu.CompilerParams(vmem_limit_bytes=40 * 2**20),
        name=name,
        **options,
    )(*[operand for _, operand in operands])
    return result[0] if len(outs) == 1 else result


def half_out_kernel(core, taps, out):
    sets, _, width = taps.shape
    chunks = width // 1024
    other = (1 - core[0]) * 512
    for s in range(sets):
        for chunk in range(chunks):
            start = pl.multiple_of(chunk * 1024 + other, 512)
            out[s, :, chunk * 512 : (chunk + 1) * 512] = taps[s, :, pl.ds(start, 512)]


def half_join_kernel(core, taps, received, out):
    sets, _, width = taps.shape
    chunks = width // 1024
    copies = out.shape[0] // chunks
    own = core[0] * 512
    first = core[0] == 0
    for chunk in range(chunks):
        rows = []
        for s in range(sets):
            start = pl.multiple_of(chunk * 1024 + own, 512)
            mine = taps[s, :, pl.ds(start, 512)].astype(f32)
            theirs = received[s, :, chunk * 512 : (chunk + 1) * 512].astype(f32)
            rows.append(jnp.where(first, mine, theirs))
            rows.append(jnp.where(first, theirs, mine))
        block = jnp.concatenate(rows, axis=0).astype(bf16)
        for copy in range(copies):
            out[chunk * copies + copy] = block


def join_own_kernel(core, taps, weight, out):
    out[0] = dot(taps[0], weight[0]) + dot(taps[1], weight[1])
    out[1] = dot(taps[2], weight[2])


def join_other_kernel(core, taps, weight, begun, out):
    constant = begun[0] + dot(taps[0], weight[0]) + dot(taps[1], weight[1])
    out[:, :, :512] = constant.astype(bf16).reshape(8, 64, 512)
    top = begun[1] + dot(taps[2], weight[2])
    out[:, :, 512:] = top.astype(bf16).reshape(8, 64, 512)


def join_half(kernel, name, out, core, taps, weight, begun, other):
    whole = lambda i, core: (0, 0, 0)
    half = lambda i, core: (0, (1 - core[0]) if other else core[0], 0)
    specs = [pl.BlockSpec((3, 512, 512), whole), pl.BlockSpec((3, 512, 512), half)]
    operands = [taps, weight]
    if other:
        specs.append(pl.BlockSpec((2, 512, 512), whole))
        operands.append(begun)
    shape, dtype = out
    return pl.pallas_call(
        kernel,
        grid_spec=pltpu.PrefetchScalarGridSpec(
            num_scalar_prefetch=1,
            grid=(1,),
            in_specs=specs,
            out_specs=pl.BlockSpec(shape, whole),
        ),
        out_shape=jax.ShapeDtypeStruct(shape, dtype),
        compiler_params=pltpu.CompilerParams(vmem_limit_bytes=40 * 2**20),
        cost_estimate=pl.CostEstimate(
            flops=2 * 3 * 512**3, bytes_accessed=5 * 2**20, transcendentals=0
        ),
        name=name,
    )(core, *operands)


def write_row_payload(core, joining, gain, payload):
    squares = jnp.sum(joining * joining, -1, keepdims=True)
    payload[:, :512] = (joining * gain[...]).astype(bf16)
    payload[:, 512:] = put_lanes(64, halves(squares), 2 * core[0]).astype(bf16)


def first_rows_kernel(core, got, gain, constant, joining, payload):
    fixed = sum_chunks(got, 0, 512)
    total = fixed + sum_chunks(got, 512, 1024)
    constant[...] = fixed
    joining[...] = total
    write_row_payload(core, total, gain, payload)


def second_rows_kernel(
    core, got, constant, gain, joining, fed_back, logits_first, table, payload
):
    side = sum_chunks(got, 1536, 1664)
    inverse = lax.rsqrt(read_lanes(side, 0, 3) / D + norm_eps)
    fed = inverse * sum_chunks(got, 0, 512)
    total = constant[...] + fed
    fed_back[...] = fed
    joining[...] = total
    write_row_payload(core, total, gain, payload)
    logits_first[...] = inverse * sum_chunks(got, 512, 1536)
    table[...] = put_lanes(64, [inverse, side[:, 4:5], side[:, 5:6]])


def both_halves(core, mine, theirs, weight):
    return dot(flat(mine, 0, 512), weight[own_half(core[0])]) + dot(
        flat(theirs, 0, 512), weight[own_half(1 - core[0])]
    )


def join_second_kernel(core, live, mine, theirs, weight, head, out):
    joined = both_halves(core, mine, theirs, weight.at[0])
    out[:, :, :512] = joined.astype(bf16).reshape(8, 64, 512)
    logits = both_halves(core, mine, theirs, head)
    out[:, :, 512:1536] = logits.astype(bf16).reshape(8, 64, 1024)
    lane = lane_of((8, 64, LANES))
    side = mine[:, :, 512:].astype(f32) + theirs[:, :, 512:].astype(f32)
    side = jnp.where(lane == 4, live[0], jnp.where(lane == 5, live[1], side))
    out[:, :, 1536:] = side.astype(bf16)


def logits_kernel(core, mine, theirs, head, out):
    logits = both_halves(core, mine, theirs, head)
    out[:, :, :1024] = logits.astype(bf16).reshape(8, 64, 1024)
    side = mine[:, :, 512:].astype(f32) + theirs[:, :, 512:].astype(f32)
    out[:, :, 1024:] = side.astype(bf16)


def stats_kernel(base, got, logits_first, targets, logits_second, table, out):
    side = sum_chunks(got, 1024, 1152)
    inverse = lax.rsqrt(read_lanes(side, 0, 3) / D + norm_eps)
    second = inverse * sum_chunks(got, 0, 1024)
    logits_second[...] = second
    table[...] = put_lanes(64, [inverse])
    vocab = lane_of((64, 1024)) + base[0]
    columns = []
    for step, logits in enumerate((logits_first[...], second)):
        top = jnp.max(logits, -1, keepdims=True)
        weights = jnp.exp(logits - top)
        columns += [
            top,
            jnp.sum(weights, -1, keepdims=True),
            jnp.sum(weights * logits, -1, keepdims=True),
            jnp.sum(jnp.where(vocab == targets[step], logits, 0.0), -1, keepdims=True),
        ]
    square = jnp.concatenate([put_lanes(64, columns), jnp.zeros((64, LANES), f32)], 0)
    rows = square.T[:8]
    for copy in range(out.shape[0]):
        out[copy] = rows


def logit_grad_kernel(
    base, shared, logits_first, logits_second, table, targets, masks,
    grads_first, grads_second, turns,
):
    rows = []
    for step in range(STEPS):
        tops = shared[:, 4 * step, :]
        top = jnp.max(tops, 0, keepdims=True)
        factor = jnp.exp(tops - top)
        total = jnp.sum(shared[:, 4 * step + 1, :] * factor, 0, keepdims=True)
        total = jnp.where(total > 0.0, total, 1.0)
        mean = jnp.sum(shared[:, 4 * step + 2, :] * factor, 0, keepdims=True) / total
        picked = jnp.sum(shared[:, 4 * step + 3, :], 0, keepdims=True)
        log_total = top + jnp.log(total)
        rows += [log_total, log_total - picked, mean - picked]
    square = jnp.concatenate(rows + [jnp.zeros((LANES - len(rows), LANES), f32)], 0)
    columns = square.T[:64]
    vocab = lane_of((64, 1024)) + base[0]
    found, loss = [], jnp.zeros((1, 1), f32)
    for step, logits in enumerate((logits_first, logits_second)):
        log_total, entropy, turn = [
            columns[:, 3 * step + i : 3 * step + i + 1] for i in range(3)
        ]
        token_weight = masks[step] / table[:, 1 + step : 2 + step]
        loss += jnp.sum(token_weight * entropy, 0, keepdims=True)
        found.append(token_weight * turn)
        probs = jnp.exp(logits[...] - log_total)
        hit = jnp.where(vocab == targets[step], 1.0, 0.0)
        grad = (token_weight * (probs - hit)).astype(bf16)
        if step == 0:
            grads_first[...] = grad
        else:
            for copy in range(grads_second.shape[0]):
                grads_second[copy] = grad
    turns[...] = put_lanes(64, found + [jnp.broadcast_to(loss, (64, 1))])


def back_second_kernel(
    row_grad, gain, joining, fed_back, table_first, table_second, turns, grads_first, out
):
    inverse = table_second[:, 0:1]
    grad = (
        (inverse * gain[...]) * row_grad[...].astype(f32)
        - (inverse * inverse * turns[:, 1:2] / D) * joining[...]
    ).astype(bf16)
    inner = jnp.sum(grad.astype(f32) * fed_back[...], -1, keepdims=True)
    side = put_lanes(
        64, [*halves(inner), *halves(table_first[:, 0:1]), *halves(turns[:, 2:3])]
    ).astype(bf16)
    logit_grad = grads_first[...]
    for copy in range(out.shape[0]):
        out[copy, :, :512] = grad
        out[copy, :, 512:1536] = logit_grad
        out[copy, :, 1536:] = side


def inner_lanes(core, got):
    side = flat(got, 1536, 1664).astype(f32)
    return put_lanes(512, [side[:, 0:1], side[:, 1:2]], 2 * core[0])


def feed_away_kernel(core, got, weight, head, out):
    rows = own_half(1 - core[0])
    value = contract_last(flat(got, 0, 512), weight[0, rows]) + contract_last(
        flat(got, 512, 1536), head[rows]
    )
    out[:, :, :512] = value.astype(bf16).reshape(8, 64, 512)
    out[:, :, 512:] = inner_lanes(core, got).astype(bf16).reshape(8, 64, LANES)


def feed_keep_kernel(core, got, weight, head, away, out):
    rows = own_half(core[0])
    value = (
        contract_last(flat(got, 0, 512), weight[0, rows])
        + contract_last(flat(got, 512, 1536), head[rows])
        + flat(away, 0, 512).astype(f32)
    )
    out[:, :, :512] = value.astype(bf16).reshape(8, 64, 512)
    side = inner_lanes(core, got) + flat(away, 512, 640).astype(f32)
    out[:, :, 512:] = side.astype(bf16).reshape(8, 64, LANES)


def feed_sum_kernel(landed, out):
    out[:, :512] = sum_chunks(landed, 0, 512).astype(bf16)
    inner = read_lanes(sum_chunks(landed, 512, 640), 0, 3)
    out[:, 512:] = put_lanes(64, halves(inner)).astype(bf16)


def back_first_kernel(row_grad, gain, joining, table, turns, out):
    inverse = table[:, 0:1]
    inner = turns[:, 0:1] + read_lanes(row_grad[:, 512:].astype(f32), 0, 1)
    grad = (
        (inverse * gain[...]) * row_grad[:, :512].astype(f32)
        - (inverse * inverse * inner / D) * joining[...]
    ).astype(bf16)
    for copy in range(out.shape[0]):
        out[copy] = grad


def grad_kernel(
    core, own, other, mine, theirs, first, second, side, grad, squares, folded
):
    tap = pl.program_id(0)
    later = flat(second, 0, 512)

    def both(lefts, rights):
        for half, columns in enumerate(lefts):
            value = sum(contract_first(x, y) for x, y in zip(columns, rights))
            place = core[0] if half == 0 else 1 - core[0]
            grad[0, own_half(place)] = value
            total = jnp.sum((value * value).reshape(-1, 8, 512), 0)
            total = total[:, :128] + total[:, 128:256] + total[:, 256:384] + total[:, 384:]
            folded[...] = total if half == 0 else folded[...] + total

    @pl.when(tap < 2)
    def _():
        both([(own[0], own[0]), (other[0], other[0])], (flat(first, 0, 512), later))

    @pl.when(tap == 2)
    def _():
        inverse = read_lanes(flat(side, 0, LANES).astype(f32), 2, 3)
        scaled = (later.astype(f32) * inverse).astype(bf16)
        both(
            [(own[0], flat(mine, 0, 512)), (other[0], flat(theirs, 0, 512))],
            (flat(first, 0, 512), scaled),
        )

    @pl.when(tap == 0)
    def _():
        squares[...] = folded[...]

    @pl.when(tap > 0)
    def _():
        squares[...] += folded[...]


def gradients(core, own, other, mine, theirs, first, got):
    tap = lambda s, core: (s, 0, 0)
    whole = lambda s, core: (0, 0, 0)
    return pl.pallas_call(
        grad_kernel,
        grid_spec=pltpu.PrefetchScalarGridSpec(
            num_scalar_prefetch=1,
            grid=(3,),
            in_specs=[
                pl.BlockSpec((1, 512, 512), tap),
                pl.BlockSpec((1, 512, 512), tap),
                pl.BlockSpec((8, 64, 512), whole),
                pl.BlockSpec((8, 64, 512), whole),
                pl.BlockSpec((8, 64, 512), whole),
                pl.BlockSpec((8, 64, 512), whole),
                pl.BlockSpec((8, 64, LANES), lambda s, core: (0, 0, 1536 // LANES)),
            ],
            out_specs=[
                pl.BlockSpec((1, 1024, 512), tap),
                pl.BlockSpec((8, LANES), lambda s, core: (0, 0)),
            ],
            scratch_shapes=[pltpu.VMEM((8, LANES), f32)],
        ),
        out_shape=[
            jax.ShapeDtypeStruct((3, 1024, 512), f32),
            jax.ShapeDtypeStruct((8, LANES), f32),
        ],
        compiler_params=pltpu.CompilerParams(vmem_limit_bytes=40 * 2**20),
        cost_estimate=pl.CostEstimate(
            flops=6 * 4 * 512 * 512 * 512, bytes_accessed=10 * 2**20, transcendentals=0
        ),
        name="gradients",
    )(core, own, other, mine, theirs, first, got, got)


def adam_kernel(
    clip, weight, grad, first, second, first_scale, second_scale,
    new_weight, new_first, new_second, new_first_scale, new_second_scale,
):
    rows = weight.shape[1]
    clip_value = clip[0]
    old_scales = jnp.concatenate(
        [first_scale[0], second_scale[0], jnp.zeros((4, rows), f32)], axis=0
    ).T
    new_columns = []
    for block in range(2):
        span = slice(block * BLOCK, (block + 1) * BLOCK)
        clipped = grad[0, :, span] * clip_value
        first_new = (
            first[0, :, span].astype(f32) * (beta_first * old_scales[:, block : block + 1])
            + (1.0 - beta_first) * clipped
        )
        second_new = (
            second[0, :, span].astype(f32)
            * (beta_second * old_scales[:, 2 + block : 3 + block])
            + (1.0 - beta_second) * clipped * clipped
        )
        current = weight[0, :, span].astype(f32)
        spread_sq = second_new * (1.0 / (1.0 - beta_second**step_count))
        spread = spread_sq * lax.rsqrt(spread_sq) + adam_eps
        turned = pl.reciprocal(spread, approx=True)
        turned = turned * (2.0 - spread * turned)
        step = first_new * turned * (learn_rate / (1.0 - beta_first**step_count))
        new_weight[0, :, span] = (
            current * (1.0 - learn_rate * weight_decay) - step
        ).astype(bf16)
        first_top = jnp.max(jnp.abs(first_new), -1, keepdims=True) + scale_eps
        second_top = jnp.max(jnp.abs(second_new), -1, keepdims=True) + scale_eps
        new_first[0, :, span] = (first_new * (1.0 / first_top)).astype(bf16)
        new_second[0, :, span] = (second_new * (1.0 / second_top)).astype(bf16)
        new_columns.append((first_top, second_top))
    lane = lax.broadcasted_iota(jnp.int32, (rows, LANES), 1)
    table = jnp.zeros((rows, LANES), f32)
    for block, (first_top, second_top) in enumerate(new_columns):
        table = jnp.where(lane == block, first_top, table)
        table = jnp.where(lane == 2 + block, second_top, table)
    turned = table.T
    new_first_scale[0] = turned[0:2]
    new_second_scale[0] = turned[2:4]


def adam(clip, weight, grad, first, second, first_scale, second_scale):
    rows = 256
    wide = pl.BlockSpec((1, rows, 512), lambda s, i: (s, i, 0))
    thin = pl.BlockSpec((1, 2, rows), lambda s, i: (s, 0, i))
    return pl.pallas_call(
        adam_kernel,
        grid=(3, 1024 // rows),
        in_specs=[SMEM, wide, wide, wide, wide, thin, thin],
        out_specs=[wide, wide, wide, thin, thin],
        out_shape=[
            jax.ShapeDtypeStruct((3, 1024, 512), bf16),
            jax.ShapeDtypeStruct((3, 1024, 512), bf16),
            jax.ShapeDtypeStruct((3, 1024, 512), bf16),
            jax.ShapeDtypeStruct((3, 2, 1024), f32),
            jax.ShapeDtypeStruct((3, 2, 1024), f32),
        ],
        compiler_params=pltpu.CompilerParams(vmem_limit_bytes=60 * 2**20),
        name="update",
    )(clip, weight, grad, first, second, first_scale, second_scale)


def shards(
    taps, gain, join_weight, head_weight, targets, masks,
    first_codes, first_scales, second_codes, second_scales,
):
    row_count = lax.axis_size("p")
    column_count = lax.axis_size("m")
    core_count = lax.axis_size("b")
    core = lax.axis_index("b")
    core_array = core.reshape(1).astype(jnp.int32)
    turn_pairs = [
        ((p * core_count + b) * column_count + m, (m * core_count + b) * column_count + p)
        for p in range(row_count)
        for b in range(core_count)
        for m in range(column_count)
    ]

    def turn(value):
        return lax.ppermute(value, AXES, turn_pairs)

    def swap(value):
        return lax.ppermute(value, "b", [(0, 1), (1, 0)])

    def exchange(value, axis):
        return lax.all_to_all(value, axis, 0, 0, tiled=False)

    def spread(value, axis):
        copies = lax.axis_size(axis)
        return exchange(jnp.broadcast_to(value, (copies,) + value.shape), axis)

    def own_rows(weight):
        return lax.dynamic_slice_in_dim(weight, core * 512, 512, weight.ndim - 2)

    def other_rows(weight):
        return lax.dynamic_slice_in_dim(weight, (1 - core) * 512, 512, weight.ndim - 2)

    base = (lax.axis_index("p") * core_count + core).reshape(1).astype(jnp.int32) * 1024
    target_ids = targets.reshape(STEPS, 64, 1)
    mask_float = masks.astype(f32).reshape(STEPS, 64, 1)
    live = jnp.sum(masks.astype(f32), axis=(1, 2))
    gain_row = gain.reshape(1, 512)
    row_f32, row_payload = ((64, 512), f32), ((64, 640), bf16)
    table_shape = ((64, LANES), f32)
    last_join = pl.BlockSpec((1, 1024, 512), lambda i: (2, 0, 0))
    scalar = pl.BlockSpec(memory_space=pltpu.SMEM)

    def whole(*shape):
        return pl.BlockSpec(shape, lambda i: (0,) * len(shape))

    def one_step(specs, out):
        return pl.GridSpec(grid=(1,), in_specs=specs, out_specs=[out])

    with jax.named_scope("taps_in"):
        outgoing = call(
            half_out_kernel, "half_out", [((3, 4, D // 2), bf16)],
            ("s", core_array), ("v", taps),
        )
        incoming = swap(outgoing)
        packed = call(
            half_join_kernel, "half_join", [((64, 24, 512), bf16)],
            ("s", core_array), ("v", taps), ("v", incoming),
        )
        landed = exchange(packed, ("m", "p"))
        taps_own = landed.reshape(64, 3, 8, 512).transpose(1, 0, 2, 3).reshape(3, 512, 512)
        taps_other = swap(taps_own)

    with jax.named_scope("join_first"):
        begun = join_half(
            join_own_kernel, "join_own", ((2, 512, 512), f32),
            core_array, taps_own, join_weight, None, False,
        )
        parts = join_half(
            join_other_kernel, "join_other", ((8, 64, 1024), bf16),
            core_array, taps_other, join_weight, begun, True,
        )
        constant, joining_first, payload = call(
            first_rows_kernel, "first_rows", [row_f32, row_f32, row_payload],
            ("s", core_array), ("v", exchange(parts, "m")), ("v", gain_row),
        )

    with jax.named_scope("hidden_first"):
        hidden_mine = spread(turn(payload), "p")
        hidden_theirs = swap(hidden_mine)

    with jax.named_scope("join_second"):
        parts = call(
            join_second_kernel, "join_second", [((8, 64, 1664), bf16)],
            ("s", core_array), ("s", live), ("v", hidden_mine), ("v", hidden_theirs),
            ("v", join_weight), ("v", head_weight),
            grid_spec=one_step(
                [
                    scalar, scalar, whole(8, 64, 640), whole(8, 64, 640),
                    last_join, whole(1024, 1024),
                ],
                whole(8, 64, 1664),
            ),
        )
        joining_second, fed_back, logits_first, table_first, payload = call(
            second_rows_kernel, "second_rows",
            [row_f32, row_f32, ((64, 1024), f32), table_shape, row_payload],
            ("s", core_array), ("v", exchange(parts, "m")), ("v", constant),
            ("v", gain_row),
        )

    with jax.named_scope("hidden_second"):
        later_mine = spread(turn(payload), "p")
        later_theirs = swap(later_mine)

    with jax.named_scope("logits"):
        parts = call(
            logits_kernel, "logits", [((8, 64, 1152), bf16)],
            ("s", core_array), ("v", later_mine), ("v", later_theirs), ("v", head_weight),
        )
        got = exchange(parts, "m")

    with jax.named_scope("softmax"):
        logits_second, table_second, stats = call(
            stats_kernel, "stats",
            [((64, 1024), f32), table_shape, ((row_count * core_count, 8, LANES), f32)],
            ("s", base), ("v", got), ("v", logits_first), ("v", target_ids),
        )
        shared = exchange(stats, ("p", "b"))
        grads_first, grad_copies, turns = call(
            logit_grad_kernel, "logit_grad",
            [((64, 1024), bf16), ((column_count, 64, 1024), bf16), table_shape],
            ("s", base), ("v", shared), ("v", logits_first), ("v", logits_second),
            ("v", table_first), ("v", target_ids), ("v", mask_float),
        )
        grads_second = exchange(grad_copies, "m").reshape(512, 1024)

    with jax.named_scope("back_second"):
        away = swap(contract_last(grads_second, other_rows(head_weight)).astype(bf16))
        kept = contract_last(grads_second, own_rows(head_weight)) + away.astype(f32)
        landed = exchange(kept.astype(bf16).reshape(8, 64, 512), "p")
        row_grad = turn(jnp.sum(landed.astype(f32), 0).astype(bf16))
        payload = call(
            back_second_kernel, "back_second", [((column_count, 64, 1664), bf16)],
            ("v", row_grad), ("v", gain_row), ("v", joining_second), ("v", fed_back),
            ("v", table_first), ("v", table_second), ("v", turns), ("v", grads_first),
        )
        got = exchange(payload, "m")

    with jax.named_scope("back_first"):
        weights = (("v", join_weight), ("v", head_weight))
        specs = [scalar, whole(8, 64, 1664), last_join, whole(1024, 1024)]
        away = swap(
            call(
                feed_away_kernel, "feed_away", [((8, 64, 640), bf16)],
                ("s", core_array), ("v", got), *weights,
                grid_spec=one_step(specs, whole(8, 64, 640)),
            )
        )
        parts = call(
            feed_keep_kernel, "feed_keep", [((8, 64, 640), bf16)],
            ("s", core_array), ("v", got), *weights, ("v", away),
            grid_spec=one_step(specs + [whole(8, 64, 640)], whole(8, 64, 640)),
        )
        summed = call(
            feed_sum_kernel, "feed_sum", [row_payload], ("v", exchange(parts, "p"))
        )
        copies = call(
            back_first_kernel, "back_first", [((column_count, 64, 512), bf16)],
            ("v", turn(summed)), ("v", gain_row), ("v", joining_first),
            ("v", table_first), ("v", turns),
        )
        first_all = exchange(copies, "m")

    with jax.named_scope("gradients"):
        grads, squares = gradients(
            core_array, taps_own, taps_other, hidden_mine, hidden_theirs, first_all, got
        )
        square_sum = jnp.broadcast_to(jnp.sum(squares), (1, LANES))
        norm_sq = jnp.sum(spread(square_sum, AXES)[:, 0, 0])
        clip = jnp.minimum(1.0, clip_norm / (jnp.sqrt(norm_sq) + 1e-06))

    with jax.named_scope("update"):
        new_join, new_first, new_second, first_scale, second_scale = adam(
            clip.reshape(1),
            join_weight,
            grads,
            first_codes,
            second_codes,
            jnp.swapaxes(first_scales, 1, 2),
            jnp.swapaxes(second_scales, 1, 2),
        )
        loss = jnp.sum(got[:, 0, 1540:1542].astype(f32))
    return (
        new_join,
        new_first,
        jnp.swapaxes(first_scale, 1, 2),
        new_second,
        jnp.swapaxes(second_scale, 1, 2),
        loss,
    )


def solution(mesh):
    rows = mesh.shape["dp"] // 2
    fine = Mesh(mesh.devices.reshape(rows, 2, mesh.shape["mp"]), AXES)
    dp, mp = ("p", "b"), "m"
    return jax.shard_map(
        shards,
        mesh=fine,
        in_specs=(
            P(None, ("p", "b", "m"), None),
            P(dp),
            P(None, mp, dp),
            P(mp, dp),
            P(None, None, mp),
            P(None, None, mp),
            P(None, mp, dp),
            P(None, mp, dp),
            P(None, mp, dp),
            P(None, mp, dp),
        ),
        out_specs=(
            P(None, mp, dp),
            P(None, mp, dp),
            P(None, mp, dp),
            P(None, mp, dp),
            P(None, mp, dp),
            P(),
        ),
        check_vma=False,
    )
```

time: 419 us -> 375 us (0.89)
  blocking collectives: 115 us -> 215 us
  waiting for transfers between devices: 118 us -> 59.2 us
  starting transfers between devices: 72.3 us -> 36.9 us
  other arithmetic: 34.9 us -> 4.6 us
  matrix products: 22.6 us -> 5.49 us
  Pallas kernels: 21.4 us -> 32.1 us
  local copies, waits for them, and re-layouts: 26.6 us -> 17.7 us
    all_to_all x4 -> x9, blocking collectives: 115 us -> 215 us  [exchange(): return lax.all_to_all(value, axis, 0, 0, tiled=False)]
    all_to_all x9 -> x4, waiting for transfers between devices: 115 us -> 49.6 us  [exchange(): return lax.all_to_all(value, axis, 0, 0, tiled=False)]
    all_to_all x9 -> x4, starting transfers between devices: 56.8 us -> 20 us  [exchange(): return lax.all_to_all(value, axis, 0, 0, tiled=False)]
    dot_general x12 -> x0, matrix products: 15.6 us -> none  [dot(): return jnp.dot(left, right, preferred_element_type=f32)]
    pallas_call x2 -> x15, Pallas kernels: 1.84 us -> 11.9 us  [the longest x13 9.91 us: call(): pl.pallas_call(kernel, out_shape=[jax.ShapeDtypeStruct(shape, dtype) for...]
    another operation x5 -> x0, other arithmetic: 9.27 us -> none  [the longest x3 6.93 us: shards(): jnp.stack([jnp.concatenate([taps_own, hidden_own[None]], 0), jnp.concaten...]
    reduce_sum x23 -> x3, other arithmetic: 11 us -> 3.26 us  [the longest x1 1.76 us: shards(): row_grad = turn(jnp.sum(landed.astype(f32), 0).astype(bf16))]
    ppermute x6, waiting for transfers between devices: 3.78 us -> 9.62 us  [swap(): return lax.ppermute(value, 'b', [(0, 1), (1, 0)])]
  transfers between devices with their start and end apart: 19 -> 14, of which waited for: 13 -> 10; matrix products, arithmetic and copies ran while one was open for 5% -> 1% of each run, Pallas kernels for 0% -> 0%
where the time goes in v2:
time: 375 us; the launch traced here: 373 us
  blocking collectives  215 us (57%)
  waiting for transfers between devices  59.2 us (16%)
  starting transfers between devices  36.9 us (10%)
  Pallas kernels  32.1 us (9%)
  local copies, waits for them, and re-layouts  17.7 us (5%)
  matrix products  5.49 us (1%)
  other arithmetic  4.6 us (1%)
    all_to_all x9, blocking collectives, exchange(): return lax.all_to_all(value, axis, 0, 0, tiled=False)  215 us
    all_to_all x4, waiting for transfers between devices, exchange(): return lax.all_to_all(value, axis, 0, 0, tiled=False)  49.6 us
    all_to_all x4, starting transfers between devices, exchange(): return lax.all_to_all(value, axis, 0, 0, tiled=False)  20 us
    pallas_call x1, Pallas kernels, adam(): pl.pallas_call(adam_kernel, grid=(3, 1024 // rows), in_specs=[SMEM, wide,...  15.9 us
    unnamed x69, local copies, waits for them, and re-layouts  15.3 us
    ppermute x6, starting transfers between devices, swap(): return lax.ppermute(value, 'b', [(0, 1), (1, 0)])  13.3 us
    pallas_call x13, Pallas kernels, call(): pl.pallas_call(kernel, out_shape=[jax.ShapeDtypeStruct(shape, dtype) for...  9.91 us
    ppermute x6, waiting for transfers between devices, swap(): return lax.ppermute(value, 'b', [(0, 1), (1, 0)])  9.62 us
  transfers between devices with their start and end apart: 14, of which 10 were waited for; matrix products, arithmetic and copies ran while one was open for 1% of the time, Pallas kernels for 0%

profile of v2, /device:TPU:1, one launch (start us, length us, event | category | flops | bytes accessed | tf_op | source)
XLA Modules:
  0.0 372.9 jit_solution(15122644437072048018)
XLA Ops:
  5.1 33.6 %all_to_all.65 = bf16[64,24,512]{2,1,0:T(8,128)(2,1)S(1)} all-to-all(bf16[64,24,512]{2,1,0:T(8,128)(2,1)S(1)} %half_join.1), channel_id=1, replica_groups=mesh['p'=8,'b'=2,'m'=8] {'m','p'}, dimensions={0} | all-to-all | bytes 3145728 | tf_op jit(solution)/shard_map/taps_in/all_to_all | solution.py:506
  45.0 19.8 %all_to_all.66.got = bf16[8,64,1024]{2,1,0:T(8,128)(2,1)S(1)} all-to-all(bf16[8,64,1024]{2,1,0:T(8,128)(2,1)S(1)} %join_other.1), channel_id=1, replica_groups=mesh['p'=8,'b'=2,'m'=8] {'m'}, dimensions={0} | all-to-all | bytes 2097152 | tf_op jit(solution)/shard_map/join_first/all_to_all | solution.py:506
  65.8 24.1 %all_to_all.67.mine = bf16[8,64,640]{2,1,0:T(8,128)(2,1)S(1)} all-to-all(bf16[8,64,640]{2,1,0:T(8,128)(2,1)S(1)} %broadcast_in_dim.9), channel_id=1, replica_groups=mesh['p'=8,'b'=2,'m'=8] {'p'}, dimensions={0} | all-to-all | bytes 1310720 | tf_op jit(solution)/shard_map/hidden_first/all_to_all | solution.py:506
  90.0 3.1 collective-permute-start.3
  98.0 27.1 %all_to_all.68.got = bf16[8,64,1664]{2,1,0:T(8,128)(2,1)S(1)} all-to-all(bf16[8,64,1664]{2,1,0:T(8,128)(2,1)S(1)} %join_second.1), channel_id=1, replica_groups=mesh['p'=8,'b'=2,'m'=8] {'m'}, dimensions={0} | all-to-all | bytes 3407872 | tf_op jit(solution)/shard_map/join_second/all_to_all | solution.py:506
  127.5 23.3 %all_to_all.69.mine = bf16[8,64,640]{2,1,0:T(8,128)(2,1)S(1)} all-to-all(bf16[8,64,640]{2,1,0:T(8,128)(2,1)S(1)} %broadcast_in_dim.10), channel_id=1, replica_groups=mesh['p'=8,'b'=2,'m'=8] {'p'}, dimensions={0} | all-to-all | bytes 1310720 | tf_op jit(solution)/shard_map/hidden_second/all_to_all | solution.py:506
  150.8 3.1 collective-permute-start.5
  157.9 4.4 %all-to-all-start.5 = ((bf16[8,64,1152]{2,1,0:T(8,128)(2,1)}), bf16[8,64,1152]{2,1,0:T(8,128)(2,1)}, u32[]{:S(2)}, u32[]{:S(2)}) async-start(bf16[8,64,1152]{2,1,0:T(8,128)(2,1)} %copy-done.7), calls=%async_computation.5 | async-start | bytes 2359296 | tf_op jit(solution)/shard_map/logits/all_to_all | solution.py:506
  162.4 18.6 %all-to-all-done.5.got = bf16[8,64,1152]{2,1,0:T(8,128)(2,1)} async-done(((bf16[8,64,1152]{2,1,0:T(8,128)(2,1)}), bf16[8,64,1152]{2,1,0:T(8,128)(2,1)}, u32[]{:S(2)}, u32[]{:S(2)}) %all-to-all-start.5) | async-done | bytes 1179680 | tf_op jit(solution)/shard_map/logits/all_to_all | solution.py:506
  184.8 4.6 %all-to-all-start.6 = ((f32[16,8,128]{2,1,0:T(8,128)}), f32[16,8,128]{2,1,0:T(8,128)}, u32[]{:S(2)}, u32[]{:S(2)}) async-start(f32[16,8,128]{2,1,0:T(8,128)} %copy-done.28), calls=%async_computation.6 | async-start | bytes 131072 | tf_op jit(solution)/shard_map/softmax/all_to_all | solution.py:506
  190.2 5.2 %all-to-all-done.6.shared = f32[16,8,128]{2,1,0:T(8,128)} async-done(((f32[16,8,128]{2,1,0:T(8,128)}), f32[16,8,128]{2,1,0:T(8,128)}, u32[]{:S(2)}, u32[]{:S(2)}) %all-to-all-start.6) | async-done | bytes 65568 | tf_op jit(solution)/shard_map/softmax/all_to_all | solution.py:506
  200.1 4.2 %all-to-all-start.7 = ((bf16[8,64,1024]{2,1,0:T(8,128)(2,1)}), bf16[8,64,1024]{2,1,0:T(8,128)(2,1)}, u32[]{:S(2)}, u32[]{:S(2)}) async-start(bf16[8,64,1024]{2,1,0:T(8,128)(2,1)} %copy-done.12), calls=%async_computation.7 | async-start | bytes 2097152 | tf_op jit(solution)/shard_map/softmax/all_to_all | solution.py:506
  204.4 17.4 %all-to-all-done.7 = bf16[8,64,1024]{2,1,0:T(8,128)(2,1)} async-done(((bf16[8,64,1024]{2,1,0:T(8,128)(2,1)}), bf16[8,64,1024]{2,1,0:T(8,128)(2,1)}, u32[]{:S(2)}, u32[]{:S(2)}) %all-to-all-start.7) | async-done | bytes 1048608 | tf_op jit(solution)/shard_map/softmax/all_to_all | solution.py:506
  221.8 3.1 convolution_convert_fusion
  229.9 12.5 %all_to_all.70 = bf16[8,64,512]{2,1,0:T(8,128)(2,1)} all-to-all(bf16[8,64,512]{2,1,0:T(8,128)(2,1)S(1)} %bitcast.23), channel_id=1, replica_groups=mesh['p'=8,'b'=2,'m'=8] {'p'}, dimensions={0} | all-to-all | bytes 1048576 | tf_op jit(solution)/shard_map/back_second/all_to_all | solution.py:506
  247.7 36.2 %all_to_all.71.got.second.side = bf16[8,64,1664]{2,1,0:T(8,128)(2,1)S(1)} all-to-all(bf16[8,64,1664]{2,1,0:T(8,128)(2,1)S(1)} %back_second.1), channel_id=1, replica_groups=mesh['p'=8,'b'=2,'m'=8] {'m'}, dimensions={0} | all-to-all | bytes 3407872 | tf_op jit(solution)/shard_map/back_second/all_to_all | solution.py:506
  284.9 2.8 collective-permute-start.8
  290.5 13.4 %all_to_all.72.landed = bf16[8,64,640]{2,1,0:T(8,128)(2,1)S(1)} all-to-all(bf16[8,64,640]{2,1,0:T(8,128)(2,1)S(1)} %feed_keep.1), channel_id=1, replica_groups=mesh['p'=8,'b'=2,'m'=8] {'p'}, dimensions={0} | all-to-all | bytes 1310720 | tf_op jit(solution)/shard_map/back_first/all_to_all | solution.py:506
  304.9 25.1 %all_to_all.73.first = bf16[8,64,512]{2,1,0:T(8,128)(2,1)S(1)} all-to-all(bf16[8,64,512]{2,1,0:T(8,128)(2,1)S(1)} %back_first.1), channel_id=1, replica_groups=mesh['p'=8,'b'=2,'m'=8] {'m'}, dimensions={0} | all-to-all | bytes 1048576 | tf_op jit(solution)/shard_map/back_first/all_to_all | solution.py:506
  330.0 4.3 %gradients.1 = (f32[3,1024,512]{2,1,0:T(8,128)S(1)}, f32[8,128]{1,0:T(8,128)S(1)}) custom-call(s32[1]{0:T(128)} %bitcast.core, bf16[3,512,512]{2,1,0:T(8,128)(2,1)S(1)} %copy-done.5, bf16[3,512,512]{2,1,0:T(8,128)(2,1)S(1)} %copy-done.11, bf16[8,64,640]{2,1,0:T(8,128)(2,1)S(1)} %copy-done.9, bf16[8,64,640]{2,1,0:T(8,128)(2,1)S(1)} %copy-done.16, ...), custom_call_target="tpu_custom_call" | custom-call | flops 3221225472 | bytes 10485760 | tf_op jit(solution)/shard_map/gradients/gradients/pallas_call | solution.py:384
  334.3 2.7 copy-done.6
  338.8 6.8 %all-to-all-start.12 = ((f32[128,1,128]{2,1,0:T(1,128)}), f32[128,1,128]{2,1,0:T(1,128)S(1)}, u32[]{:S(2)}, u32[]{:S(2)}) async-start(f32[128,1,128]{2,1,0:T(1,128)} %broadcast_in_dim.11), calls=%async_computation.12 | async-start | bytes 131072 | tf_op jit(solution)/shard_map/gradients/all_to_all | solution.py:506
  347.0 8.3 %all-to-all-done.12 = f32[128,1,128]{2,1,0:T(1,128)S(1)} async-done(((f32[128,1,128]{2,1,0:T(1,128)}), f32[128,1,128]{2,1,0:T(1,128)S(1)}, u32[]{:S(2)}, u32[]{:S(2)}) %all-to-all-start.12) | async-done | bytes 65568 | tf_op jit(solution)/shard_map/gradients/all_to_all | solution.py:506
  356.8 15.9 %update.1 = (bf16[3,1024,512]{2,1,0:T(8,128)(2,1)}, bf16[3,1024,512]{2,1,0:T(8,128)(2,1)}, bf16[3,1024,512]{2,1,0:T(8,128)(2,1)}, f32[3,2,1024]{2,1,0:T(2,128)}, f32[3,2,1024]{2,1,0:T(2,128)}) custom-call(f32[1]{0:T(128)} %bitcast.9.clip, bf16[3,1024,512]{2,1,0:T(8,128)(2,1)} %weight.11, f32[3,1024,512]{2,1,0:T(8,128)} %copy-done.6, ...), custom_call_target="tpu_custom_call" | custom-call | tf_op jit(solution)/shard_map/update/update/pallas_call | solution.py:466
  (114 shorter events, 51.4 us)
Async XLA Ops:
  1.6 2.4 collective-permute-start
  38.8 5.0 %collective-permute-start.1 = (bf16[3,512,512]{2,1,0:T(8,128)(2,1)S(1)}, bf16[3,512,512]{2,1,0:T(8,128)(2,1)S(1)}, u32[]{:S(2)}, u32[]{:S(2)}) collective-permute-start(bf16[3,512,512]{2,1,0:T(8,128)(2,1)S(1)} %copy_bitcast_fusion.taps.own), channel_id=1, source_target_pairs={{0,8},{8,0},{1,9},{9,1},{2,10},{10,2},{3,11},{11,3},{4,12},{12,4},... | collective-permute-start | bytes 4718600 | tf_op jit(solution)/shard_map/taps_in/ppermute | solution.py:503
  45.0 19.8 %copy-start.31 = (f32[512]{0:T(512)S(1)}, f32[512]{0:T(512)}, u32[]{:S(2)}) copy-start(f32[512]{0:T(512)} %param.11) | copy-start | bytes 6148
  64.7 28.4 %copy-start.32 = (s32[2,16,4]{1,2,0:T(4,128)S(1)}, s32[2,16,4]{1,2,0:T(4,128)}, u32[]{:S(2)}) copy-start(s32[2,16,4]{1,2,0:T(4,128)} %param.15) | copy-start | bytes 1540
  64.7 30.1 %copy-start.1 = (bf16[1024,1024]{1,0:T(8,128)(2,1)S(1)}, bf16[1024,1024]{1,0:T(8,128)(2,1)}, u32[]{:S(2)}) copy-start(bf16[1024,1024]{1,0:T(8,128)(2,1)} %head.7) | copy-start | bytes 6291460
  65.0 29.9 %copy-start.20 = (f32[64,512]{1,0:T(8,128)}, f32[64,512]{1,0:T(8,128)S(1)}, u32[]{:S(2)}) copy-start(f32[64,512]{1,0:T(8,128)S(1)} %get-tuple-element.40.joining) | copy-start | bytes 393220
  65.0 0.8 collective-permute-start.2
  90.0 4.8 %collective-permute-start.3 = (bf16[8,64,640]{2,1,0:T(8,128)(2,1)S(1)}, bf16[8,64,640]{2,1,0:T(8,128)(2,1)S(1)}, u32[]{:S(2)}, u32[]{:S(2)}) collective-permute-start(bf16[8,64,640]{2,1,0:T(8,128)(2,1)S(1)} %all_to_all.67.mine), channel_id=1, source_target_pairs={{0,8},{8,0},{1,9},{9,1},{2,10},{10,2},{3,11},{11,3},{4,12},{12,4},... | collective-permute-start | bytes 1966088 | tf_op jit(solution)/shard_map/hidden_first/ppermute | solution.py:503
  126.7 0.7 collective-permute-start.4
  150.8 4.8 %collective-permute-start.5 = (bf16[8,64,640]{2,1,0:T(8,128)(2,1)S(1)}, bf16[8,64,640]{2,1,0:T(8,128)(2,1)S(1)}, u32[]{:S(2)}, u32[]{:S(2)}) collective-permute-start(bf16[8,64,640]{2,1,0:T(8,128)(2,1)S(1)} %all_to_all.69.mine), channel_id=1, source_target_pairs={{0,8},{8,0},{1,9},{9,1},{2,10},{10,2},{3,11},{11,3},{4,12},{12,4},... | collective-permute-start | bytes 1966088 | tf_op jit(solution)/shard_map/hidden_second/ppermute | solution.py:503
  157.9 23.2 %all-to-all-start.5 = ((bf16[8,64,1152]{2,1,0:T(8,128)(2,1)}), bf16[8,64,1152]{2,1,0:T(8,128)(2,1)}, u32[]{:S(2)}, u32[]{:S(2)}) async-start(bf16[8,64,1152]{2,1,0:T(8,128)(2,1)} %copy-done.7), calls=%async_computation.5 | async-start | bytes 2359296 | tf_op jit(solution)/shard_map/logits/all_to_all | solution.py:506
  184.8 10.7 %all-to-all-start.6 = ((f32[16,8,128]{2,1,0:T(8,128)}), f32[16,8,128]{2,1,0:T(8,128)}, u32[]{:S(2)}, u32[]{:S(2)}) async-start(f32[16,8,128]{2,1,0:T(8,128)} %copy-done.28), calls=%async_computation.6 | async-start | bytes 131072 | tf_op jit(solution)/shard_map/softmax/all_to_all | solution.py:506
  200.1 21.7 %all-to-all-start.7 = ((bf16[8,64,1024]{2,1,0:T(8,128)(2,1)}), bf16[8,64,1024]{2,1,0:T(8,128)(2,1)}, u32[]{:S(2)}, u32[]{:S(2)}) async-start(bf16[8,64,1024]{2,1,0:T(8,128)(2,1)} %copy-done.12), calls=%async_computation.7 | async-start | bytes 2097152 | tf_op jit(solution)/shard_map/softmax/all_to_all | solution.py:506
  224.9 2.6 collective-permute-start.6
  244.2 1.5 collective-permute-start.7
  247.7 36.2 %copy-start.2 = (bf16[1024,1024]{1,0:T(8,128)(2,1)S(1)}, bf16[1024,1024]{1,0:T(8,128)(2,1)}, u32[]{:S(2)}) copy-start(bf16[1024,1024]{1,0:T(8,128)(2,1)} %head.7) | copy-start | bytes 6291460
  283.9 46.1 %copy-start.3 = (bf16[8,64,1664]{2,1,0:T(8,128)(2,1)}, bf16[8,64,1664]{2,1,0:T(8,128)(2,1)S(1)}, u32[]{:S(2)}) copy-start(bf16[8,64,1664]{2,1,0:T(8,128)(2,1)S(1)} %all_to_all.71.got.second.side) | copy-start | bytes 5111812
  284.9 4.5 %collective-permute-start.8 = (bf16[8,64,640]{2,1,0:T(8,128)(2,1)S(1)}, bf16[8,64,640]{2,1,0:T(8,128)(2,1)S(1)}, u32[]{:S(2)}, u32[]{:S(2)}) collective-permute-start(bf16[8,64,640]{2,1,0:T(8,128)(2,1)S(1)} %feed_away.1), channel_id=1, source_target_pairs={{0,8},{8,0},{1,9},{9,1},{2,10},{10,2},{3,11},{11,3},{4,12},{12,4},... | collective-permute-start | bytes 1966088 | tf_op jit(solution)/shard_map/back_first/ppermute | solution.py:503
  289.4 40.5 %copy-start.16 = (bf16[8,64,640]{2,1,0:T(8,128)(2,1)S(1)}, bf16[8,64,640]{2,1,0:T(8,128)(2,1)}, u32[]{:S(2)}) copy-start(bf16[8,64,640]{2,1,0:T(8,128)(2,1)} %copy-done.15) | copy-start | bytes 1966084
  290.4 39.5 %copy-start.5 = (bf16[3,512,512]{2,1,0:T(8,128)(2,1)S(1)}, bf16[3,512,512]{2,1,0:T(8,128)(2,1)}, u32[]{:S(2)}) copy-start(bf16[3,512,512]{2,1,0:T(8,128)(2,1)} %copy-done.4) | copy-start | bytes 4718596
  290.5 39.5 %copy-start.9 = (bf16[8,64,640]{2,1,0:T(8,128)(2,1)S(1)}, bf16[8,64,640]{2,1,0:T(8,128)(2,1)}, u32[]{:S(2)}) copy-start(bf16[8,64,640]{2,1,0:T(8,128)(2,1)} %copy-done.8) | copy-start | bytes 1966084
  290.5 39.5 %copy-start.11 = (bf16[3,512,512]{2,1,0:T(8,128)(2,1)S(1)}, bf16[3,512,512]{2,1,0:T(8,128)(2,1)}, u32[]{:S(2)}) copy-start(bf16[3,512,512]{2,1,0:T(8,128)(2,1)} %copy-done.10) | copy-start | bytes 4718596
  304.0 0.7 collective-permute-start.9
  338.8 16.5 %all-to-all-start.12 = ((f32[128,1,128]{2,1,0:T(1,128)}), f32[128,1,128]{2,1,0:T(1,128)S(1)}, u32[]{:S(2)}, u32[]{:S(2)}) async-start(f32[128,1,128]{2,1,0:T(1,128)} %broadcast_in_dim.11), calls=%async_computation.12 | async-start | bytes 131072 | tf_op jit(solution)/shard_map/gradients/all_to_all | solution.py:506
  (24 other events, 80.1 us)

commit v3 on v1

v3 whole, which is shorter than its diff:
```python
import jax
import jax.numpy as jnp
from jax import lax
from jax.experimental import pallas as pl
from jax.experimental.pallas import tpu as pltpu
from jax.sharding import Mesh, PartitionSpec as P

D = 8192
STEPS = 2
BLOCK = 256
LANES = 128
CHUNKS = 8

norm_eps = 1e-05
clip_norm = 1.0
learn_rate = 0.0003
weight_decay = 0.1
beta_first = 0.9
beta_second = 0.999
step_count = 10.0
adam_eps = 1e-08
scale_eps = 1e-12

bf16 = jnp.bfloat16
f32 = jnp.float32
AXES = ("p", "b", "m")
VMEM = pl.BlockSpec(memory_space=pltpu.VMEM)
SMEM = pl.BlockSpec(memory_space=pltpu.SMEM)


def dot(left, right):
    return jnp.dot(left, right, preferred_element_type=f32)


def contract_last(left, right):
    return lax.dot_general(
        left, right, (((1,), (1,)), ((), ())), preferred_element_type=f32
    )


def contract_first(left, right):
    return lax.dot_general(
        left, right, (((0,), (0,)), ((), ())), preferred_element_type=f32
    )


def put_lanes(rows, columns):
    lane = lax.broadcasted_iota(jnp.int32, (rows, LANES), 1)
    block = jnp.zeros((rows, LANES), f32)
    for place, column in enumerate(columns):
        block = jnp.where(lane == place, column, block)
    return block


def total_over(parts, picks, start, stop):
    total = parts[picks[0], :, start:stop].astype(f32)
    for pick in picks[1:]:
        total += parts[pick, :, start:stop].astype(f32)
    return total


def column_sum(parts, row, start, stop):
    return total_over(parts, [row * CHUNKS + m for m in range(CHUNKS)], start, stop)


def row_sum(parts, column, start, stop):
    return total_over(parts, [p * CHUNKS + column for p in range(CHUNKS)], start, stop)


def lane_total(values):
    total = values[0]
    for value in values[1:]:
        total = total + value
    return jnp.broadcast_to(jnp.sum(total, -1, keepdims=True), (8, LANES))


def to_blocks(value):
    return value.reshape(64, 8, value.shape[-1]).astype(bf16)


def half_rows(core):
    return pl.ds(pl.multiple_of(core * 512, 512), 512)


def call(kernel, name, outs, *operands, specs=None, flops=0):
    options = {}
    if specs is None:
        options["in_specs"] = [SMEM if space == "s" else VMEM for space, _ in operands]
        options["out_specs"] = [VMEM] * len(outs)
    else:
        options["grid_spec"] = pltpu.PrefetchScalarGridSpec(
            num_scalar_prefetch=1,
            grid=(1,),
            in_specs=specs,
            out_specs=[whole_block(shape) for shape, _ in outs],
        )
    result = pl.pallas_call(
        kernel,
        out_shape=[jax.ShapeDtypeStruct(shape, dtype) for shape, dtype in outs],
        compiler_params=pltpu.CompilerParams(vmem_limit_bytes=40 * 2**20),
        cost_estimate=pl.CostEstimate(
            flops=flops, bytes_accessed=4 * 2**20, transcendentals=0
        ),
        name=name,
        **options,
    )(*[operand for _, operand in operands])
    return result[0] if len(outs) == 1 else result


def whole_block(shape):
    return pl.BlockSpec(shape, lambda i, core: (0,) * len(shape))


def half_out_kernel(core, taps, out):
    sets, _, width = taps.shape
    chunks = width // 1024
    other = (1 - core[0]) * 512
    for s in range(sets):
        for chunk in range(chunks):
            start = pl.multiple_of(chunk * 1024 + other, 512)
            out[s, :, chunk * 512 : (chunk + 1) * 512] = taps[s, :, pl.ds(start, 512)]


def half_join_kernel(core, taps, received, out):
    sets, _, width = taps.shape
    chunks = width // 1024
    copies = out.shape[0] // chunks
    own = core[0] * 512
    first = core[0] == 0
    for chunk in range(chunks):
        rows = []
        for s in range(sets):
            start = pl.multiple_of(chunk * 1024 + own, 512)
            mine = taps[s, :, pl.ds(start, 512)].astype(f32)
            theirs = received[s, :, chunk * 512 : (chunk + 1) * 512].astype(f32)
            rows.append(jnp.where(first, mine, theirs))
            rows.append(jnp.where(first, theirs, mine))
        block = jnp.concatenate(rows, axis=0).astype(bf16)
        for copy in range(copies):
            out[copy * chunks + chunk] = block


def join_own_kernel(core, taps, weight, out):
    out[0] = dot(taps[0], weight[0]) + dot(taps[1], weight[1])
    out[1] = dot(taps[2], weight[2])


def join_other_kernel(core, taps, weight, begun, side, constant, out):
    fixed = begun[0] + dot(taps[0], weight[0]) + dot(taps[1], weight[1])
    constant[...] = fixed
    out[:, :, :512] = to_blocks(fixed + begun[1] + dot(taps[2], weight[2]))
    out[:, :, 512:] = jnp.broadcast_to(side[...], (64, 8, LANES)).astype(bf16)


def both_halves(core, mine, theirs, weight):
    return dot(mine[...], weight[half_rows(core[0])]) + dot(
        theirs[...], weight[half_rows(1 - core[0])]
    )


def join_second_kernel(core, mine, theirs, weight, head, constant, out):
    joined = constant[...] + both_halves(core, mine, theirs, weight.at[0])
    out[:, :, :512] = to_blocks(joined)
    out[:, :, 512:] = to_blocks(both_halves(core, mine, theirs, head))


def logits_kernel(core, mine, theirs, head, out):
    out[...] = to_blocks(both_halves(core, mine, theirs, head))


def head_back_kernel(core, grads, head, *rest):
    *added, out = rest
    value = contract_last(grads[...], head[half_rows(core[0])])
    if added:
        value += added[0][...].astype(f32).reshape(512, 512)
    out[...] = to_blocks(value)


def feed_back_kernel(core, got, weight, head, *rest):
    *added, out = rest
    rows = half_rows(core[0])
    value = contract_last(got[:, :512], weight[0, rows])
    value += contract_last(got[:, 512:], head[rows])
    if added:
        value += added[0][...].astype(f32).reshape(512, 512)
    out[...] = to_blocks(value)


def first_rows_kernel(got, joining, gain, counts, squares):
    terms = []
    for chunk in range(CHUNKS):
        value = column_sum(got, chunk, 0, 512)
        joining[chunk] = value
        terms.append(value * value)
        side = total_over(got, [chunk * CHUNKS, chunk * CHUNKS + 1], 512, 640)
        row = jnp.concatenate([side[i : i + 1] for i in range(4)], axis=1)
        gain[chunk] = jnp.broadcast_to(row, (8, 512))
    squares[...] = lane_total(terms)
    counts[...] = jnp.broadcast_to(column_sum(got, 0, 512, 640)[4:5], (8, LANES))


def second_rows_kernel(got, joining, logits, squares):
    terms = []
    for chunk in range(CHUNKS):
        value = column_sum(got, chunk, 0, 512)
        joining[chunk] = value
        terms.append(value * value)
        logits[chunk] = column_sum(got, chunk, 512, 1536)
    squares[...] = lane_total(terms)


def norm_kernel(joining, gain, squares, squares_other, inverse, out):
    factor = lax.rsqrt((squares[...] + squares_other[...]) / D + norm_eps)
    inverse[...] = factor
    for chunk in range(CHUNKS):
        hidden = (joining[chunk] * factor[:, 0:1] * gain[chunk]).astype(bf16)
        for copy in range(CHUNKS):
            out[copy * CHUNKS + chunk] = hidden


def norm_inner_kernel(got, joining, gain, scaled, inner):
    terms = []
    for chunk in range(CHUNKS):
        value = row_sum(got, chunk, 0, 512) * gain[chunk]
        scaled[chunk] = value
        terms.append(value * joining[chunk])
    inner[...] = lane_total(terms)


def norm_back_kernel(scaled, joining, inverse, inner, inner_other, *rest):
    *riders, out = rest
    factor = inverse[:, 0:1]
    pull = factor * factor * factor * (inner[:, 0:1] + inner_other[:, 0:1]) / D
    for chunk in range(CHUNKS):
        grad = (factor * scaled[chunk] - pull * joining[chunk]).astype(bf16)
        for copy in range(CHUNKS):
            out[chunk * CHUNKS + copy, :, :512] = grad
            if riders:
                out[chunk * CHUNKS + copy, :, 512:] = riders[0][chunk]


def vocab_of(core, chunk):
    return lax.broadcasted_iota(jnp.int32, (8, 1024), 1) + (2 * chunk + core) * 1024


def stats_kernel(core, got, logits_first, targets, logits_second, stats):
    for chunk in range(CHUNKS):
        logits_second[chunk] = column_sum(got, chunk, 0, 1024)
    columns = []
    for step, logits in enumerate((logits_first, logits_second)):
        top = logits[0]
        for chunk in range(1, CHUNKS):
            top = jnp.maximum(top, logits[chunk])
        top = jnp.max(top, -1, keepdims=True)
        weights = jnp.zeros((8, 1024), f32)
        picked = jnp.zeros((8, 1024), f32)
        for chunk in range(CHUNKS):
            weights += jnp.exp(logits[chunk] - top)
            hit = vocab_of(core[0], chunk) == targets[step]
            picked += jnp.where(hit, logits[chunk], 0.0)
        columns += [
            top,
            jnp.sum(weights, -1, keepdims=True),
            jnp.sum(picked, -1, keepdims=True),
        ]
    stats[...] = put_lanes(8, columns)


def logit_grad_kernel(
    core, stats, stats_other, logits_first, logits_second, targets, masks, counts,
    grads_first, grads_second, loss,
):
    lost = jnp.zeros((8, 1), f32)
    for step, logits in enumerate((logits_first, logits_second)):
        place = 3 * step
        top_mine, top_other = [x[:, place : place + 1] for x in (stats, stats_other)]
        sum_mine, sum_other = [
            x[:, place + 1 : place + 2] for x in (stats, stats_other)
        ]
        picked = stats[:, place + 2 : place + 3] + stats_other[:, place + 2 : place + 3]
        top = jnp.maximum(top_mine, top_other)
        total = sum_mine * jnp.exp(top_mine - top) + sum_other * jnp.exp(top_other - top)
        log_total = top + jnp.log(total)
        weight = masks[step] / counts[:, step : step + 1]
        lost += weight * (log_total - picked)
        for chunk in range(CHUNKS):
            probs = jnp.exp(logits[chunk] - log_total)
            hit = jnp.where(vocab_of(core[0], chunk) == targets[step], 1.0, 0.0)
            grad = (weight * (probs - hit)).astype(bf16)
            if step == 0:
                grads_first[chunk] = grad
            else:
                for copy in range(CHUNKS):
                    grads_second[chunk * CHUNKS + copy] = grad
    once = jnp.where(core[0] == 0, 1.0, 0.0)
    loss[...] = jnp.broadcast_to(jnp.sum(lost, 0, keepdims=True) * once, (8, LANES))


def grad_kernel(core, own, other, mine, theirs, first, second, loss, grad, totals):
    tap = pl.program_id(0)

    def both(lefts):
        for half, (left, left_later) in enumerate(lefts):
            value = contract_first(left, first[...]) + contract_first(
                left_later, second[...]
            )
            grad[0, half_rows(core[0] if half == 0 else 1 - core[0])] = value
            total = jnp.sum((value * value).reshape(-1, 8, 512), 0)
            total = total[:, :128] + total[:, 128:256] + total[:, 256:384] + total[:, 384:]
            totals[0] += total

    @pl.when(tap == 0)
    def _():
        totals[0] = jnp.zeros((8, LANES), f32)
        totals[1] = loss[...]

    @pl.when(tap < 2)
    def _():
        both([(own[0], own[0]), (other[0], other[0])])

    @pl.when(tap == 2)
    def _():
        both([(own[0], mine[...]), (other[0], theirs[...])])


def gradients(core, own, other, mine, theirs, first, got, loss):
    tap = lambda s, core: (s, 0, 0)
    still = pl.BlockSpec((512, 512), lambda s, core: (0, 0))
    return pl.pallas_call(
        grad_kernel,
        grid_spec=pltpu.PrefetchScalarGridSpec(
            num_scalar_prefetch=1,
            grid=(3,),
            in_specs=[
                pl.BlockSpec((1, 512, 512), tap),
                pl.BlockSpec((1, 512, 512), tap),
                still,
                still,
                still,
                still,
                pl.BlockSpec((8, LANES), lambda s, core: (0, 0)),
            ],
            out_specs=[
                pl.BlockSpec((1, 1024, 512), tap),
                pl.BlockSpec((2, 8, LANES), lambda s, core: (0, 0, 0)),
            ],
        ),
        out_shape=[
            jax.ShapeDtypeStruct((3, 1024, 512), f32),
            jax.ShapeDtypeStruct((2, 8, LANES), f32),
        ],
        compiler_params=pltpu.CompilerParams(vmem_limit_bytes=40 * 2**20),
        cost_estimate=pl.CostEstimate(
            flops=6 * 4 * 512 * 512 * 512, bytes_accessed=10 * 2**20, transcendentals=0
        ),
        name="gradients",
    )(core, own, other, mine, theirs, first, got, loss)


def adam_kernel(
    clip, weight, grad, first, second, first_scale, second_scale,
    new_weight, new_first, new_second, new_first_scale, new_second_scale,
):
    rows = weight.shape[1]
    clip_value = clip[0]
    old_scales = jnp.concatenate(
        [first_scale[0], second_scale[0], jnp.zeros((4, rows), f32)], axis=0
    ).T
    new_columns = []
    for block in range(2):
        span = slice(block * BLOCK, (block + 1) * BLOCK)
        clipped = grad[0, :, span] * clip_value
        first_new = (
            first[0, :, span].astype(f32) * (beta_first * old_scales[:, block : block + 1])
            + (1.0 - beta_first) * clipped
        )
        second_new = (
            second[0, :, span].astype(f32)
            * (beta_second * old_scales[:, 2 + block : 3 + block])
            + (1.0 - beta_second) * clipped * clipped
        )
        current = weight[0, :, span].astype(f32)
        spread_sq = second_new * (1.0 / (1.0 - beta_second**step_count))
        spread = spread_sq * lax.rsqrt(spread_sq) + adam_eps
        turned = pl.reciprocal(spread, approx=True)
        turned = turned * (2.0 - spread * turned)
        step = first_new * turned * (learn_rate / (1.0 - beta_first**step_count))
        new_weight[0, :, span] = (
            current * (1.0 - learn_rate * weight_decay) - step
        ).astype(bf16)
        first_top = jnp.max(jnp.abs(first_new), -1, keepdims=True) + scale_eps
        second_top = jnp.max(jnp.abs(second_new), -1, keepdims=True) + scale_eps
        new_first[0, :, span] = (first_new * (1.0 / first_top)).astype(bf16)
        new_second[0, :, span] = (second_new * (1.0 / second_top)).astype(bf16)
        new_columns.append((first_top, second_top))
    lane = lax.broadcasted_iota(jnp.int32, (rows, LANES), 1)
    table = jnp.zeros((rows, LANES), f32)
    for block, (first_top, second_top) in enumerate(new_columns):
        table = jnp.where(lane == block, first_top, table)
        table = jnp.where(lane == 2 + block, second_top, table)
    turned = table.T
    new_first_scale[0] = turned[0:2]
    new_second_scale[0] = turned[2:4]


def adam(clip, weight, grad, first, second, first_scale, second_scale):
    rows = 256
    wide = pl.BlockSpec((1, rows, 512), lambda s, i: (s, i, 0))
    thin = pl.BlockSpec((1, 2, rows), lambda s, i: (s, 0, i))
    return pl.pallas_call(
        adam_kernel,
        grid=(3, 1024 // rows),
        in_specs=[SMEM, wide, wide, wide, wide, thin, thin],
        out_specs=[wide, wide, wide, thin, thin],
        out_shape=[
            jax.ShapeDtypeStruct((3, 1024, 512), bf16),
            jax.ShapeDtypeStruct((3, 1024, 512), bf16),
            jax.ShapeDtypeStruct((3, 1024, 512), bf16),
            jax.ShapeDtypeStruct((3, 2, 1024), f32),
            jax.ShapeDtypeStruct((3, 2, 1024), f32),
        ],
        compiler_params=pltpu.CompilerParams(vmem_limit_bytes=60 * 2**20),
        name="update",
    )(clip, weight, grad, first, second, first_scale, second_scale)


def shards(
    taps, gain, join_weight, head_weight, targets, masks,
    first_codes, first_scales, second_codes, second_scales,
):
    core = lax.axis_index("b")
    row = lax.axis_index("p")
    column = lax.axis_index("m")
    own = core.reshape(1).astype(jnp.int32)
    other = 1 - own
    chips = ("p", "m")

    def swap(value):
        return lax.ppermute(value, "b", [(0, 1), (1, 0)])

    def exchange(value, axes=chips):
        return lax.all_to_all(value, axes, 0, 0, tiled=False)

    def own_tokens(values):
        mine = lax.dynamic_slice_in_dim(values, 2 * row, 2, 1)
        return mine.reshape(STEPS, 8, 1)

    target_ids = own_tokens(targets)
    mask_float = own_tokens(masks).astype(f32)
    gain_rows = gain.reshape(4, LANES)
    gain_high = lax.reduce_precision(gain_rows, 8, 7)
    live = jnp.sum(masks.astype(f32), axis=(1, 2)).reshape(1, STEPS)
    side = jnp.concatenate(
        [
            jnp.where(column % 2 == 0, gain_high, gain_rows - gain_high),
            jnp.pad(live, ((0, 3), (0, LANES - STEPS))),
        ]
    )
    rows_f32, table = ((CHUNKS, 8, 512), f32), ((8, LANES), f32)
    vocab_f32 = ((CHUNKS, 8, 1024), f32)
    blocks = ((64, 8, 512), bf16)
    half_flops = 2 * 512**3
    last_join = pl.BlockSpec((1, 1024, 512), lambda i, core: (2, 0, 0))
    tokens_half, tokens_wide = whole_block((512, 512)), whole_block((512, 1024))
    head_block, parts_block = whole_block((1024, 1024)), whole_block((64, 8, 512))

    with jax.named_scope("taps_in"):
        outgoing = call(
            half_out_kernel, "half_out", [((3, 4, D // 2), bf16)], ("s", own), ("v", taps)
        )
        packed = call(
            half_join_kernel, "half_join", [((64, 24, 512), bf16)],
            ("s", own), ("v", taps), ("v", swap(outgoing)),
        )
        landed = exchange(packed)
        taps_own = landed.reshape(64, 3, 8, 512).transpose(1, 0, 2, 3).reshape(3, 512, 512)
        taps_other = swap(taps_own)

    with jax.named_scope("join_first"):
        sets = whole_block((3, 512, 512))
        begun = call(
            join_own_kernel, "join_own", [((2, 512, 512), f32)],
            ("s", own), ("v", taps_own), ("v", join_weight),
            specs=[sets, pl.BlockSpec((3, 512, 512), lambda i, core: (0, core[0], 0))],
            flops=3 * half_flops,
        )
        constant, parts = call(
            join_other_kernel, "join_other",
            [((512, 512), f32), ((64, 8, 640), bf16)],
            ("s", other), ("v", taps_other), ("v", join_weight), ("v", begun), ("v", side),
            specs=[
                sets,
                pl.BlockSpec((3, 512, 512), lambda i, core: (0, core[0], 0)),
                whole_block((2, 512, 512)),
                whole_block((8, LANES)),
            ],
            flops=3 * half_flops,
        )
        joining_first, gains, counts, squares = call(
            first_rows_kernel, "first_rows", [rows_f32, rows_f32, table, table],
            ("v", exchange(parts)),
        )

    def to_hidden(joining, squares):
        inverse, copies = call(
            norm_kernel, "norm", [table, blocks],
            ("v", joining), ("v", gains), ("v", squares), ("v", swap(squares)),
        )
        mine = exchange(copies).reshape(512, 512)
        return inverse, mine, swap(mine)

    with jax.named_scope("hidden_first"):
        inverse_first, hidden_mine, hidden_theirs = to_hidden(joining_first, squares)

    with jax.named_scope("join_second"):
        parts = call(
            join_second_kernel, "join_second", [((64, 8, 1536), bf16)],
            ("s", own), ("v", hidden_mine), ("v", hidden_theirs), ("v", join_weight),
            ("v", head_weight), ("v", constant),
            specs=[tokens_half, tokens_half, last_join, head_block, tokens_half],
            flops=6 * half_flops,
        )
        joining_second, logits_first, squares = call(
            second_rows_kernel, "second_rows", [rows_f32, vocab_f32, table],
            ("v", exchange(parts)),
        )

    with jax.named_scope("hidden_second"):
        inverse_second, later_mine, later_theirs = to_hidden(joining_second, squares)

    with jax.named_scope("logits"):
        parts = call(
            logits_kernel, "logits", [((64, 8, 1024), bf16)],
            ("s", own), ("v", later_mine), ("v", later_theirs), ("v", head_weight),
            specs=[tokens_half, tokens_half, head_block],
            flops=4 * half_flops,
        )
        got = exchange(parts)

    with jax.named_scope("softmax"):
        logits_second, stats = call(
            stats_kernel, "stats", [vocab_f32, table],
            ("s", own), ("v", got), ("v", logits_first), ("v", target_ids),
        )
        grads_first, copies, loss = call(
            logit_grad_kernel, "logit_grad",
            [((CHUNKS, 8, 1024), bf16), ((64, 8, 1024), bf16), table],
            ("s", own), ("v", stats), ("v", swap(stats)), ("v", logits_first),
            ("v", logits_second), ("v", target_ids), ("v", mask_float), ("v", counts),
        )
        grads_second = exchange(copies).reshape(512, 1024)

    def row_gradients(parts, joining, inverse, *riders):
        scaled, inner = call(
            norm_inner_kernel, "norm_inner", [rows_f32, table],
            ("v", exchange(parts)), ("v", joining), ("v", gains),
        )
        width = 512 + sum(rider.shape[-1] for rider in riders)
        copies = call(
            norm_back_kernel, "norm_back", [((64, 8, width), bf16)],
            ("v", scaled), ("v", joining), ("v", inverse), ("v", inner),
            ("v", swap(inner)), *[("v", rider) for rider in riders],
        )
        return exchange(copies).reshape(512, width)

    with jax.named_scope("back_second"):
        specs, operands = [tokens_wide, head_block], (("v", grads_second), ("v", head_weight))
        away = call(
            head_back_kernel, "head_away", [blocks], ("s", other), *operands,
            specs=specs, flops=2 * half_flops,
        )
        parts = call(
            head_back_kernel, "head_keep", [blocks], ("s", own), *operands,
            ("v", swap(away)), specs=specs + [parts_block], flops=2 * half_flops,
        )
        got = row_gradients(parts, joining_second, inverse_second, grads_first)

    with jax.named_scope("back_first"):
        specs = [whole_block((512, 1536)), last_join, head_block]
        operands = (("v", got), ("v", join_weight), ("v", head_weight))
        away = call(
            feed_back_kernel, "feed_away", [blocks], ("s", other), *operands,
            specs=specs, flops=3 * half_flops,
        )
        parts = call(
            feed_back_kernel, "feed_keep", [blocks], ("s", own), *operands,
            ("v", swap(away)), specs=specs + [parts_block], flops=3 * half_flops,
        )
        first_all = row_gradients(parts, joining_first, inverse_first)

    with jax.named_scope("gradients"):
        grads, totals = gradients(
            own, taps_own, taps_other, hidden_mine, hidden_theirs, first_all, got, loss
        )
        square_sum = jnp.broadcast_to(jnp.sum(totals[0]), (1, LANES))
        lane = lax.broadcasted_iota(jnp.int32, (1, LANES), 1)
        shared = jnp.where(lane == 0, square_sum, totals[1, 0:1])
        shared = exchange(jnp.broadcast_to(shared, (128, 1, LANES)), AXES)
        shared = jnp.sum(shared[:, 0, 0:2], 0)
        clip = jnp.minimum(1.0, clip_norm / (jnp.sqrt(shared[0]) + 1e-06))
        loss = shared[1]

    with jax.named_scope("update"):
        new_join, new_first, new_second, first_scale, second_scale = adam(
            clip.reshape(1),
            join_weight,
            grads,
            first_codes,
            second_codes,
            jnp.swapaxes(first_scales, 1, 2),
            jnp.swapaxes(second_scales, 1, 2),
        )
    return (
        new_join,
        new_first,
        jnp.swapaxes(first_scale, 1, 2),
        new_second,
        jnp.swapaxes(second_scale, 1, 2),
        loss,
    )


def solution(mesh):
    rows = mesh.shape["dp"] // 2
    fine = Mesh(mesh.devices.reshape(rows, 2, mesh.shape["mp"]), AXES)
    dp, mp = ("p", "b"), "m"
    return jax.shard_map(
        shards,
        mesh=fine,
        in_specs=(
            P(None, ("p", "b", "m"), None),
            P(dp),
            P(None, mp, dp),
            P(mp, dp),
            P(None, None, mp),
            P(None, None, mp),
            P(None, mp, dp),
            P(None, mp, dp),
            P(None, mp, dp),
            P(None, mp, dp),
        ),
        out_specs=(
            P(None, mp, dp),
            P(None, mp, dp),
            P(None, mp, dp),
            P(None, mp, dp),
            P(None, mp, dp),
            P(),
        ),
        check_vma=False,
    )
```

time: 419 us -> 337 us (0.80)
  blocking collectives: 115 us -> 224 us
  waiting for transfers between devices: 118 us -> 28.2 us
  starting transfers between devices: 72.3 us -> 28.2 us
  other arithmetic: 34.9 us -> 1.59 us
  matrix products: 22.6 us -> 0 us
  Pallas kernels: 21.4 us -> 37 us
  local copies, waits for them, and re-layouts: 26.6 us -> 14.2 us
    all_to_all x4 -> x11, blocking collectives: 115 us -> 224 us  [exchange(): return lax.all_to_all(value, axes, 0, 0, tiled=False)]
    all_to_all x9 -> x1, waiting for transfers between devices: 115 us -> 17 us  [exchange(): return lax.all_to_all(value, axes, 0, 0, tiled=False)]
    all_to_all x9 -> x1, starting transfers between devices: 56.8 us -> 5.65 us  [exchange(): return lax.all_to_all(value, axes, 0, 0, tiled=False)]
    dot_general x18 -> x0, matrix products: 22.6 us -> none  [the longest x12 15.6 us: dot(): return jnp.dot(left, right, preferred_element_type=f32)]
    pallas_call x2 -> x20, Pallas kernels: 1.84 us -> 15.9 us  [call(): pl.pallas_call(kernel, out_shape=[jax.ShapeDtypeStruct(shape, dtype) for...]
    reduce_sum x25 -> x3, other arithmetic: 12.4 us -> 0.85 us  [the longest x1 0.6 us: shards(): square_sum = jnp.broadcast_to(jnp.sum(totals[0]), (1, LANES))]
    ppermute x6 -> x11, starting transfers between devices: 12.8 us -> 22.6 us  [swap(): return lax.ppermute(value, 'b', [(0, 1), (1, 0)])]
    another operation x5 -> x0, other arithmetic: 9.27 us -> none  [the longest x3 6.93 us: shards(): jnp.stack([jnp.concatenate([taps_own, hidden_own[None]], 0), jnp.concaten...]
  transfers between devices with their start and end apart: 19 -> 12, of which waited for: 13 -> 11; matrix products, arithmetic and copies ran while one was open for 5% -> 1% of each run, Pallas kernels for 0% -> 1%
where the time goes in v3:
time: 337 us; the launch traced here: 335 us
  blocking collectives  224 us (66%)
  Pallas kernels  37 us (11%)
  starting transfers between devices  28.2 us (8%)
  waiting for transfers between devices  28.2 us (8%)
  local copies, waits for them, and re-layouts  14.2 us (4%)
    all_to_all x11, blocking collectives, exchange(): return lax.all_to_all(value, axes, 0, 0, tiled=False)  224 us
    ppermute x11, starting transfers between devices, swap(): return lax.ppermute(value, 'b', [(0, 1), (1, 0)])  22.6 us
    all_to_all x1, waiting for transfers between devices, exchange(): return lax.all_to_all(value, axes, 0, 0, tiled=False)  17 us
    pallas_call x1, Pallas kernels, adam(): pl.pallas_call(adam_kernel, grid=(3, 1024 // rows), in_specs=[SMEM, wide,...  15.9 us
    pallas_call x20, Pallas kernels, call(): pl.pallas_call(kernel, out_shape=[jax.ShapeDtypeStruct(shape, dtype) for...  15.9 us
    ppermute x11, waiting for transfers between devices, swap(): return lax.ppermute(value, 'b', [(0, 1), (1, 0)])  11.2 us
    unnamed x50, local copies, waits for them, and re-layouts  10.7 us
  transfers between devices with their start and end apart: 12, of which 11 were waited for; matrix products, arithmetic and copies ran while one was open for 1% of the time, Pallas kernels for 1%

profile of v3, /device:TPU:1, one launch (start us, length us, event | category | flops | bytes accessed | tf_op | source)
XLA Modules:
  0.0 335.4 jit_solution(17657787613276538314)
XLA Ops:
  5.1 33.0 %all_to_all.60 = bf16[64,24,512]{2,1,0:T(8,128)(2,1)S(1)} all-to-all(bf16[64,24,512]{2,1,0:T(8,128)(2,1)S(1)} %half_join.1), channel_id=1, replica_groups=mesh['p'=8,'b'=2,'m'=8] {'p','m'}, dimensions={0} | all-to-all | bytes 3145728 | tf_op jit(solution)/shard_map/taps_in/all_to_all | solution.py:442
  39.4 2.5 collective-permute-start.1
  42.0 2.4 join_own.1.begun
  45.2 2.4 join_other.1
  47.7 18.3 %all_to_all.61.got = bf16[64,8,640]{2,1,0:T(8,128)(2,1)S(1)} all-to-all(bf16[64,8,640]{2,1,0:T(8,128)(2,1)S(1)} %get-tuple-element.35), channel_id=1, replica_groups=mesh['p'=8,'b'=2,'m'=8] {'p','m'}, dimensions={0} | all-to-all | bytes 1310720 | tf_op jit(solution)/shard_map/join_first/all_to_all | solution.py:442
  66.1 2.0 collective-permute-start.2
  69.0 16.4 %all_to_all.62 = bf16[64,8,512]{2,1,0:T(8,128)(2,1)S(1)} all-to-all(bf16[64,8,512]{2,1,0:T(8,128)(2,1)S(1)} %get-tuple-element.39), channel_id=1, replica_groups=mesh['p'=8,'b'=2,'m'=8] {'p','m'}, dimensions={0} | all-to-all | bytes 1048576 | tf_op jit(solution)/shard_map/hidden_first/all_to_all | solution.py:442
  91.6 26.4 %all_to_all.63.got = bf16[64,8,1536]{2,1,0:T(8,128)(2,1)S(1)} all-to-all(bf16[64,8,1536]{2,1,0:T(8,128)(2,1)S(1)} %join_second.1), channel_id=1, replica_groups=mesh['p'=8,'b'=2,'m'=8] {'p','m'}, dimensions={0} | all-to-all | bytes 3145728 | tf_op jit(solution)/shard_map/join_second/all_to_all | solution.py:442
  118.2 2.5 collective-permute-start.4
  121.7 16.8 %all_to_all.64 = bf16[64,8,512]{2,1,0:T(8,128)(2,1)S(1)} all-to-all(bf16[64,8,512]{2,1,0:T(8,128)(2,1)S(1)} %get-tuple-element.43), channel_id=1, replica_groups=mesh['p'=8,'b'=2,'m'=8] {'p','m'}, dimensions={0} | all-to-all | bytes 1048576 | tf_op jit(solution)/shard_map/hidden_second/all_to_all | solution.py:442
  144.3 5.7 %all-to-all-start.5 = ((bf16[64,8,1024]{2,1,0:T(8,128)(2,1)}), bf16[64,8,1024]{2,1,0:T(8,128)(2,1)}, u32[]{:S(2)}, u32[]{:S(2)}) async-start(bf16[64,8,1024]{2,1,0:T(8,128)(2,1)} %copy-done.4), calls=%async_computation.5 | async-start | bytes 2097152 | tf_op jit(solution)/shard_map/logits/all_to_all | solution.py:442
  150.2 17.0 %all-to-all-done.5.got = bf16[64,8,1024]{2,1,0:T(8,128)(2,1)} async-done(((bf16[64,8,1024]{2,1,0:T(8,128)(2,1)}), bf16[64,8,1024]{2,1,0:T(8,128)(2,1)}, u32[]{:S(2)}, u32[]{:S(2)}) %all-to-all-start.5) | async-done | bytes 1048608 | tf_op jit(solution)/shard_map/logits/all_to_all | solution.py:442
  168.2 2.2 stats.1
  178.1 22.0 %all_to_all.65 = bf16[64,8,1024]{2,1,0:T(8,128)(2,1)S(1)} all-to-all(bf16[64,8,1024]{2,1,0:T(8,128)(2,1)S(1)} %get-tuple-element.48), channel_id=1, replica_groups=mesh['p'=8,'b'=2,'m'=8] {'p','m'}, dimensions={0} | all-to-all | bytes 2097152 | tf_op jit(solution)/shard_map/softmax/all_to_all | solution.py:442
  205.0 16.6 %all_to_all.66.got = bf16[64,8,512]{2,1,0:T(8,128)(2,1)S(1)} all-to-all(bf16[64,8,512]{2,1,0:T(8,128)(2,1)S(1)} %head_keep.1), channel_id=1, replica_groups=mesh['p'=8,'b'=2,'m'=8] {'p','m'}, dimensions={0} | all-to-all | bytes 1048576 | tf_op jit(solution)/shard_map/back_second/all_to_all | solution.py:442
  221.8 2.0 collective-permute-start.8
  224.7 26.4 %all_to_all.67 = bf16[64,8,1536]{2,1,0:T(8,128)(2,1)S(1)} all-to-all(bf16[64,8,1536]{2,1,0:T(8,128)(2,1)S(1)} %norm_back.2), channel_id=1, replica_groups=mesh['p'=8,'b'=2,'m'=8] {'p','m'}, dimensions={0} | all-to-all | bytes 3145728 | tf_op jit(solution)/shard_map/back_second/all_to_all | solution.py:442
  252.1 2.6 collective-permute-start.9
  257.2 17.0 %all_to_all.68.got = bf16[64,8,512]{2,1,0:T(8,128)(2,1)S(1)} all-to-all(bf16[64,8,512]{2,1,0:T(8,128)(2,1)S(1)} %feed_keep.1), channel_id=1, replica_groups=mesh['p'=8,'b'=2,'m'=8] {'p','m'}, dimensions={0} | all-to-all | bytes 1048576 | tf_op jit(solution)/shard_map/back_first/all_to_all | solution.py:442
  277.3 16.4 %all_to_all.69 = bf16[64,8,512]{2,1,0:T(8,128)(2,1)S(1)} all-to-all(bf16[64,8,512]{2,1,0:T(8,128)(2,1)S(1)} %norm_back.3), channel_id=1, replica_groups=mesh['p'=8,'b'=2,'m'=8] {'p','m'}, dimensions={0} | all-to-all | bytes 1048576 | tf_op jit(solution)/shard_map/back_first/all_to_all | solution.py:442
  293.7 5.1 %gradients.1 = (f32[3,1024,512]{2,1,0:T(8,128)S(1)}, f32[2,8,128]{2,1,0:T(8,128)S(1)}) custom-call(s32[1]{0:T(128)} %bitcast.core, bf16[3,512,512]{2,1,0:T(8,128)(2,1)} %copy_bitcast_fusion.taps.own, bf16[3,512,512]{2,1,0:T(8,128)(2,1)} %collective-permute-done.1.taps.other, bf16[512,512]{1,0:T(8,128)(2,1)S(1)} %bitcast.30, bf16[512,512]{1,0:T(8,128)(2,1)S(1)} %copy-done.13, ...), custom_call_target="tpu_custom_call" | custom-call | flops 3221225472 | bytes 10485760 | tf_op jit(solution)/shard_map/gradients/gradients/pallas_call | solution.py:329
  298.9 2.6 copy-done.3
  302.8 15.0 %all_to_all.70 = f32[128,1,128]{2,1,0:T(1,128)S(1)} all-to-all(f32[128,1,128]{2,1,0:T(1,128)S(1)} %broadcast_in_dim.7), channel_id=1, replica_groups=mesh['p'=8,'b'=2,'m'=8] {'p','b','m'}, dimensions={0} | all-to-all | bytes 131072 | tf_op jit(solution)/shard_map/gradients/all_to_all | solution.py:442
  319.3 15.9 %update.1 = (bf16[3,1024,512]{2,1,0:T(8,128)(2,1)}, bf16[3,1024,512]{2,1,0:T(8,128)(2,1)}, bf16[3,1024,512]{2,1,0:T(8,128)(2,1)}, f32[3,2,1024]{2,1,0:T(2,128)}, f32[3,2,1024]{2,1,0:T(2,128)}) custom-call(f32[1]{0:T(128)S(6)} %min.4.clip, bf16[3,1024,512]{2,1,0:T(8,128)(2,1)} %weight.11, f32[3,1024,512]{2,1,0:T(8,128)} %copy-done.3, ...), custom_call_target="tpu_custom_call" | custom-call | tf_op jit(solution)/shard_map/update/update/pallas_call | solution.py:410
  (97 shorter events, 44.4 us)
Async XLA Ops:
  1.6 2.4 collective-permute-start
  39.4 5.9 %collective-permute-start.1 = (bf16[3,512,512]{2,1,0:T(8,128)(2,1)}, bf16[3,512,512]{2,1,0:T(8,128)(2,1)}, u32[]{:S(2)}, u32[]{:S(2)}) collective-permute-start(bf16[3,512,512]{2,1,0:T(8,128)(2,1)} %copy_bitcast_fusion.taps.own), channel_id=1, source_target_pairs={{0,8},{8,0},{1,9},{9,1},{2,10},{10,2},{3,11},{11,3},{4,12},{12,4},... | collective-permute-start | bytes 4718600 | tf_op jit(solution)/shard_map/taps_in/ppermute | solution.py:439
  47.7 41.3 %copy-start.1 = (bf16[1024,1024]{1,0:T(8,128)(2,1)S(1)}, bf16[1024,1024]{1,0:T(8,128)(2,1)}, u32[]{:S(2)}) copy-start(bf16[1024,1024]{1,0:T(8,128)(2,1)} %head.11) | copy-start | bytes 6291460
  66.1 22.8 %copy-start.18 = (f32[8,128]{1,0:T(8,128)}, f32[8,128]{1,0:T(8,128)S(1)}, u32[]{:S(2)}) copy-start(f32[8,128]{1,0:T(8,128)S(1)} %get-tuple-element.47.counts) | copy-start | bytes 12292
  66.1 2.8 collective-permute-start.2
  69.0 19.9 %copy-start.16 = (f32[8,128]{1,0:T(8,128)}, f32[8,128]{1,0:T(8,128)S(1)}, u32[]{:S(2)}) copy-start(f32[8,128]{1,0:T(8,128)S(1)} %get-tuple-element.54.inverse) | copy-start | bytes 12292
  85.4 5.3 %copy-start.5 = (bf16[64,8,512]{2,1,0:T(8,128)(2,1)}, bf16[64,8,512]{2,1,0:T(8,128)(2,1)S(1)}, u32[]{:S(2)}) copy-start(bf16[64,8,512]{2,1,0:T(8,128)(2,1)S(1)} %all_to_all.62) | copy-start | bytes 1572868
  85.4 3.5 %collective-permute-start.3 = (bf16[512,512]{1,0:T(8,128)(2,1)S(1)}, bf16[512,512]{1,0:T(8,128)(2,1)S(1)}, u32[]{:S(2)}, u32[]{:S(2)}) collective-permute-start(bf16[512,512]{1,0:T(8,128)(2,1)S(1)} %bitcast.28), channel_id=1, source_target_pairs={{0,8},{8,0},{1,9},{9,1},{2,10},{10,2},{3,11},{11,3},{4,12},{12,4},... | collective-permute-start | bytes 1572872 | tf_op jit(solution)/shard_map/hidden_first/ppermute | solution.py:439
  118.2 22.3 %copy-start.7 = (f32[8,8,1024]{2,1,0:T(8,128)}, f32[8,8,1024]{2,1,0:T(8,128)S(1)}, u32[]{:S(2)}) copy-start(f32[8,8,1024]{2,1,0:T(8,128)S(1)} %get-tuple-element.44.logits_first) | copy-start | bytes 786436
  118.2 3.4 %collective-permute-start.4 = (f32[8,128]{1,0:T(8,128)S(1)}, f32[8,128]{1,0:T(8,128)S(1)}, u32[]{:S(2)}, u32[]{:S(2)}) collective-permute-start(f32[8,128]{1,0:T(8,128)S(1)} %get-tuple-element.42.squares), channel_id=1, source_target_pairs={{0,8},{8,0},{1,9},{9,1},{2,10},{10,2},{3,11},{11,3},{4,12},{12,4},... | collective-permute-start | bytes 12296 | tf_op jit(solution)/shard_map/hidden_second/ppermute | solution.py:439
  121.7 18.8 %copy-start.20 = (f32[8,128]{1,0:T(8,128)}, f32[8,128]{1,0:T(8,128)S(1)}, u32[]{:S(2)}) copy-start(f32[8,128]{1,0:T(8,128)S(1)} %get-tuple-element.50.inverse) | copy-start | bytes 12292
  138.5 3.5 %collective-permute-start.5 = (bf16[512,512]{1,0:T(8,128)(2,1)S(1)}, bf16[512,512]{1,0:T(8,128)(2,1)S(1)}, u32[]{:S(2)}, u32[]{:S(2)}) collective-permute-start(bf16[512,512]{1,0:T(8,128)(2,1)S(1)} %bitcast.31), channel_id=1, source_target_pairs={{0,8},{8,0},{1,9},{9,1},{2,10},{10,2},{3,11},{11,3},{4,12},{12,4},... | collective-permute-start | bytes 1572872 | tf_op jit(solution)/shard_map/hidden_second/ppermute | solution.py:439
  144.3 5.7 %copy-start.23 = (s32[2,16,4]{1,2,0:T(4,128)S(1)}, s32[2,16,4]{1,2,0:T(4,128)}, u32[]{:S(2)}) copy-start(s32[2,16,4]{1,2,0:T(4,128)} %param.14) | copy-start | bytes 1540
  144.3 22.9 %all-to-all-start.5 = ((bf16[64,8,1024]{2,1,0:T(8,128)(2,1)}), bf16[64,8,1024]{2,1,0:T(8,128)(2,1)}, u32[]{:S(2)}, u32[]{:S(2)}) async-start(bf16[64,8,1024]{2,1,0:T(8,128)(2,1)} %copy-done.4), calls=%async_computation.5 | async-start | bytes 2097152 | tf_op jit(solution)/shard_map/logits/all_to_all | solution.py:442
  171.0 3.2 collective-permute-start.6
  174.3 25.9 %copy-start.2 = (bf16[1024,1024]{1,0:T(8,128)(2,1)S(1)}, bf16[1024,1024]{1,0:T(8,128)(2,1)}, u32[]{:S(2)}) copy-start(bf16[1024,1024]{1,0:T(8,128)(2,1)} %head.11) | copy-start | bytes 6291460
  200.9 3.4 %collective-permute-start.7 = (bf16[64,8,512]{2,1,0:T(8,128)(2,1)S(1)}, bf16[64,8,512]{2,1,0:T(8,128)(2,1)S(1)}, u32[]{:S(2)}, u32[]{:S(2)}) collective-permute-start(bf16[64,8,512]{2,1,0:T(8,128)(2,1)S(1)} %head_away.1), channel_id=1, source_target_pairs={{0,8},{8,0},{1,9},{9,1},{2,10},{10,2},{3,11},{11,3},{4,12},{12,4},... | collective-permute-start | bytes 1572872 | tf_op jit(solution)/shard_map/back_second/ppermute | solution.py:439
  205.0 19.5 %copy-start.21 = (f32[8,128]{1,0:T(8,128)S(1)}, f32[8,128]{1,0:T(8,128)}, u32[]{:S(2)}) copy-start(f32[8,128]{1,0:T(8,128)} %copy-done.20) | copy-start | bytes 12292
  221.8 2.8 collective-permute-start.8
  252.1 4.1 %collective-permute-start.9 = (bf16[64,8,512]{2,1,0:T(8,128)(2,1)S(1)}, bf16[64,8,512]{2,1,0:T(8,128)(2,1)S(1)}, u32[]{:S(2)}, u32[]{:S(2)}) collective-permute-start(bf16[64,8,512]{2,1,0:T(8,128)(2,1)S(1)} %feed_away.1), channel_id=1, source_target_pairs={{0,8},{8,0},{1,9},{9,1},{2,10},{10,2},{3,11},{11,3},{4,12},{12,4},... | collective-permute-start | bytes 1572872 | tf_op jit(solution)/shard_map/back_first/ppermute | solution.py:439
  257.2 20.0 %copy-start.17 = (f32[8,128]{1,0:T(8,128)S(1)}, f32[8,128]{1,0:T(8,128)}, u32[]{:S(2)}) copy-start(f32[8,128]{1,0:T(8,128)} %copy-done.16) | copy-start | bytes 12292
  274.2 19.5 %copy-start.6 = (bf16[64,8,512]{2,1,0:T(8,128)(2,1)S(1)}, bf16[64,8,512]{2,1,0:T(8,128)(2,1)}, u32[]{:S(2)}) copy-start(bf16[64,8,512]{2,1,0:T(8,128)(2,1)} %copy-done.5) | copy-start | bytes 1572868
  274.2 19.5 %copy-start.13 = (bf16[512,512]{1,0:T(8,128)(2,1)S(1)}, bf16[512,512]{1,0:T(8,128)(2,1)}, u32[]{:S(2)}) copy-start(bf16[512,512]{1,0:T(8,128)(2,1)} %copy-done.12) | copy-start | bytes 1572868
  274.4 2.8 collective-permute-start.10
  (13 other events, 22.2 us)

commit v4 on v3

--- a/solution.py
+++ b/solution.py
@@ -97,7 +97,7 @@
     result = pl.pallas_call(
         kernel,
         out_shape=[jax.ShapeDtypeStruct(shape, dtype) for shape, dtype in outs],
-        compiler_params=pltpu.CompilerParams(vmem_limit_bytes=40 * 2**20),
+        compiler_params=pltpu.CompilerParams(vmem_limit_bytes=24 * 2**20),
         cost_estimate=pl.CostEstimate(
             flops=flops, bytes_accessed=4 * 2**20, transcendentals=0
         ),
@@ -243,7 +243,19 @@
     return lax.broadcasted_iota(jnp.int32, (8, 1024), 1) + (2 * chunk + core) * 1024
 
 
-def stats_kernel(core, got, logits_first, targets, logits_second, stats):
+def own_tokens(places, values):
+    wide = values.astype(f32)
+    lane = lax.broadcasted_iota(jnp.int32, wide.shape, 1)
+    return jnp.concatenate(
+        [
+            jnp.sum(jnp.where(lane == places[1] + i, wide, 0.0), -1, keepdims=True)
+            for i in range(2)
+        ],
+        axis=0,
+    )
+
+
+def stats_kernel(places, got, logits_first, targets, logits_second, stats):
     for chunk in range(CHUNKS):
         logits_second[chunk] = column_sum(got, chunk, 0, 1024)
     columns = []
@@ -253,10 +265,11 @@
             top = jnp.maximum(top, logits[chunk])
         top = jnp.max(top, -1, keepdims=True)
         weights = jnp.zeros((8, 1024), f32)
+        target = own_tokens(places, targets[step]).astype(jnp.int32)
         picked = jnp.zeros((8, 1024), f32)
         for chunk in range(CHUNKS):
             weights += jnp.exp(logits[chunk] - top)
-            hit = vocab_of(core[0], chunk) == targets[step]
+            hit = vocab_of(places[0], chunk) == target
             picked += jnp.where(hit, logits[chunk], 0.0)
         columns += [
             top,
@@ -267,7 +280,7 @@
 
 
 def logit_grad_kernel(
-    core, stats, stats_other, logits_first, logits_second, targets, masks, counts,
+    places, stats, stats_other, logits_first, logits_second, targets, masks, counts,
     grads_first, grads_second, loss,
 ):
     lost = jnp.zeros((8, 1), f32)
@@ -281,22 +294,25 @@
         top = jnp.maximum(top_mine, top_other)
         total = sum_mine * jnp.exp(top_mine - top) + sum_other * jnp.exp(top_other - top)
         log_total = top + jnp.log(total)
-        weight = masks[step] / counts[:, step : step + 1]
+        weight = own_tokens(places, masks[step]) / counts[:, step : step + 1]
+        target = own_tokens(places, targets[step]).astype(jnp.int32)
         lost += weight * (log_total - picked)
         for chunk in range(CHUNKS):
             probs = jnp.exp(logits[chunk] - log_total)
-            hit = jnp.where(vocab_of(core[0], chunk) == targets[step], 1.0, 0.0)
+            hit = jnp.where(vocab_of(places[0], chunk) == target, 1.0, 0.0)
             grad = (weight * (probs - hit)).astype(bf16)
             if step == 0:
                 grads_first[chunk] = grad
             else:
                 for copy in range(CHUNKS):
                     grads_second[chunk * CHUNKS + copy] = grad
-    once = jnp.where(core[0] == 0, 1.0, 0.0)
+    once = jnp.where(places[0] == 0, 1.0, 0.0)
     loss[...] = jnp.broadcast_to(jnp.sum(lost, 0, keepdims=True) * once, (8, LANES))
 
 
-def grad_kernel(core, own, other, mine, theirs, first, second, loss, grad, totals):
+def grad_kernel(
+    core, own, other, mine, theirs, first, second, loss, grad, payload, squares
+):
     tap = pl.program_id(0)
 
     def both(lefts):
@@ -307,12 +323,11 @@
             grad[0, half_rows(core[0] if half == 0 else 1 - core[0])] = value
             total = jnp.sum((value * value).reshape(-1, 8, 512), 0)
             total = total[:, :128] + total[:, 128:256] + total[:, 256:384] + total[:, 384:]
-            totals[0] += total
+            squares[...] += total
 
     @pl.when(tap == 0)
     def _():
-        totals[0] = jnp.zeros((8, LANES), f32)
-        totals[1] = loss[...]
+        squares[...] = jnp.zeros((8, LANES), f32)
 
     @pl.when(tap < 2)
     def _():
@@ -321,6 +336,11 @@
     @pl.when(tap == 2)
     def _():
         both([(own[0], mine[...]), (other[0], theirs[...])])
+        row = jnp.sum(squares[...], 0, keepdims=True)
+        total = jnp.sum(row, -1, keepdims=True)
+        lane = lax.broadcasted_iota(jnp.int32, (1, LANES), 1)
+        value = jnp.where(lane == 0, total, loss[0:1])
+        payload[...] = jnp.broadcast_to(value[None], payload.shape)
 
 
 def gradients(core, own, other, mine, theirs, first, got, loss):
@@ -342,14 +362,15 @@
             ],
             out_specs=[
                 pl.BlockSpec((1, 1024, 512), tap),
-                pl.BlockSpec((2, 8, LANES), lambda s, core: (0, 0, 0)),
+                pl.BlockSpec((128, 1, LANES), lambda s, core: (0, 0, 0)),
             ],
+            scratch_shapes=[pltpu.VMEM((8, LANES), f32)],
         ),
         out_shape=[
             jax.ShapeDtypeStruct((3, 1024, 512), f32),
-            jax.ShapeDtypeStruct((2, 8, LANES), f32),
+            jax.ShapeDtypeStruct((128, 1, LANES), f32),
         ],
-        compiler_params=pltpu.CompilerParams(vmem_limit_bytes=40 * 2**20),
+        compiler_params=pltpu.CompilerParams(vmem_limit_bytes=24 * 2**20),
         cost_estimate=pl.CostEstimate(
             flops=6 * 4 * 512 * 512 * 512, bytes_accessed=10 * 2**20, transcendentals=0
         ),
@@ -357,26 +378,40 @@
     )(core, own, other, mine, theirs, first, got, loss)
 
 
+def spread_scales(scales):
+    terms = []
+    for _ in range(3):
+        term = scales.astype(bf16)
+        terms.append(term.astype(f32))
+        scales = scales - terms[-1]
+    left = jnp.concatenate(terms + [jnp.zeros((2, scales.shape[1]), f32)], 0).astype(bf16)
+    place = lax.broadcasted_iota(jnp.int32, (8, 512), 0) % 2
+    block = lax.broadcasted_iota(jnp.int32, (8, 512), 1) // BLOCK
+    return contract_first(left, jnp.where(place == block, 1.0, 0.0).astype(bf16))
+
+
 def adam_kernel(
-    clip, weight, grad, first, second, first_scale, second_scale,
-    new_weight, new_first, new_second, new_first_scale, new_second_scale,
+    shared, weight, grad, first, second, first_scale, second_scale,
+    new_weight, new_first, new_second, new_first_scale, new_second_scale, loss,
 ):
     rows = weight.shape[1]
-    clip_value = clip[0]
-    old_scales = jnp.concatenate(
-        [first_scale[0], second_scale[0], jnp.zeros((4, rows), f32)], axis=0
-    ).T
+    total = jnp.sum(shared[:, 0, :], 0, keepdims=True)
+    loss[...] = total[:, 1:2]
+    clip = jnp.minimum(1.0, clip_norm / (jnp.sqrt(total[:, 0:1]) + 1e-06))
+    tap = pl.program_id(0)
+    here = pl.ds(pl.multiple_of(pl.program_id(1) * rows, rows), rows)
+    old_first = spread_scales(first_scale[tap, :, here] * beta_first)
+    old_second = spread_scales(second_scale[tap, :, here] * beta_second)
     new_columns = []
     for block in range(2):
         span = slice(block * BLOCK, (block + 1) * BLOCK)
-        clipped = grad[0, :, span] * clip_value
+        clipped = grad[0, :, span] * clip
         first_new = (
-            first[0, :, span].astype(f32) * (beta_first * old_scales[:, block : block + 1])
+            first[0, :, span].astype(f32) * old_first[:, span]
             + (1.0 - beta_first) * clipped
         )
         second_new = (
-            second[0, :, span].astype(f32)
-            * (beta_second * old_scales[:, 2 + block : 3 + block])
+            second[0, :, span].astype(f32) * old_second[:, span]
             + (1.0 - beta_second) * clipped * clipped
         )
         current = weight[0, :, span].astype(f32)
@@ -399,29 +434,35 @@
         table = jnp.where(lane == block, first_top, table)
         table = jnp.where(lane == 2 + block, second_top, table)
     turned = table.T
-    new_first_scale[0] = turned[0:2]
-    new_second_scale[0] = turned[2:4]
-
-
-def adam(clip, weight, grad, first, second, first_scale, second_scale):
-    rows = 256
+    new_first_scale[tap, :, here] = turned[0:2]
+    new_second_scale[tap, :, here] = turned[2:4]
+
+
+def adam(shared, weight, grad, first, second, first_scale, second_scale):
+    rows = 512
     wide = pl.BlockSpec((1, rows, 512), lambda s, i: (s, i, 0))
-    thin = pl.BlockSpec((1, 2, rows), lambda s, i: (s, 0, i))
+    thin = pl.BlockSpec((3, 2, 1024), lambda s, i: (0, 0, 0))
     return pl.pallas_call(
         adam_kernel,
         grid=(3, 1024 // rows),
-        in_specs=[SMEM, wide, wide, wide, wide, thin, thin],
-        out_specs=[wide, wide, wide, thin, thin],
+        in_specs=[
+            pl.BlockSpec((128, 1, LANES), lambda s, i: (0, 0, 0)),
+            wide, wide, wide, wide, thin, thin,
+        ],
+        out_specs=[
+            wide, wide, wide, thin, thin, pl.BlockSpec((1, 1), lambda s, i: (0, 0))
+        ],
         out_shape=[
             jax.ShapeDtypeStruct((3, 1024, 512), bf16),
             jax.ShapeDtypeStruct((3, 1024, 512), bf16),
             jax.ShapeDtypeStruct((3, 1024, 512), bf16),
             jax.ShapeDtypeStruct((3, 2, 1024), f32),
             jax.ShapeDtypeStruct((3, 2, 1024), f32),
+            jax.ShapeDtypeStruct((1, 1), f32),
         ],
-        compiler_params=pltpu.CompilerParams(vmem_limit_bytes=60 * 2**20),
+        compiler_params=pltpu.CompilerParams(vmem_limit_bytes=34 * 2**20),
         name="update",
-    )(clip, weight, grad, first, second, first_scale, second_scale)
+    )(shared, weight, grad, first, second, first_scale, second_scale)
 
 
 def shards(
@@ -431,8 +472,8 @@
     core = lax.axis_index("b")
     row = lax.axis_index("p")
     column = lax.axis_index("m")
-    own = core.reshape(1).astype(jnp.int32)
-    other = 1 - own
+    own = jnp.stack([core, 2 * row]).astype(jnp.int32)
+    other = jnp.stack([1 - core, 2 * row]).astype(jnp.int32)
     chips = ("p", "m")
 
     def swap(value):
@@ -441,12 +482,8 @@
     def exchange(value, axes=chips):
         return lax.all_to_all(value, axes, 0, 0, tiled=False)
 
-    def own_tokens(values):
-        mine = lax.dynamic_slice_in_dim(values, 2 * row, 2, 1)
-        return mine.reshape(STEPS, 8, 1)
-
-    target_ids = own_tokens(targets)
-    mask_float = own_tokens(masks).astype(f32)
+    target_ids = jnp.swapaxes(targets, 1, 2)
+    mask_ids = jnp.swapaxes(masks, 1, 2)
     gain_rows = gain.reshape(4, LANES)
     gain_high = lax.reduce_precision(gain_rows, 8, 7)
     live = jnp.sum(masks.astype(f32), axis=(1, 2)).reshape(1, STEPS)
@@ -546,7 +583,13 @@
             logit_grad_kernel, "logit_grad",
             [((CHUNKS, 8, 1024), bf16), ((64, 8, 1024), bf16), table],
             ("s", own), ("v", stats), ("v", swap(stats)), ("v", logits_first),
-            ("v", logits_second), ("v", target_ids), ("v", mask_float), ("v", counts),
+            ("v", logits_second), ("v", target_ids), ("v", mask_ids), ("v", counts),
+            specs=[
+                whole_block((8, LANES)), whole_block((8, LANES)),
+                whole_block((CHUNKS, 8, 1024)), whole_block((CHUNKS, 8, 1024)),
+                whole_block((STEPS, 4, 16)), whole_block((STEPS, 4, 16)),
+                whole_block((8, LANES)),
+            ],
         )
         grads_second = exchange(copies).reshape(512, 1024)
 
@@ -589,20 +632,14 @@
         first_all = row_gradients(parts, joining_first, inverse_first)
 
     with jax.named_scope("gradients"):
-        grads, totals = gradients(
+        grads, payload = gradients(
             own, taps_own, taps_other, hidden_mine, hidden_theirs, first_all, got, loss
         )
-        square_sum = jnp.broadcast_to(jnp.sum(totals[0]), (1, LANES))
-        lane = lax.broadcasted_iota(jnp.int32, (1, LANES), 1)
-        shared = jnp.where(lane == 0, square_sum, totals[1, 0:1])
-        shared = exchange(jnp.broadcast_to(shared, (128, 1, LANES)), AXES)
-        shared = jnp.sum(shared[:, 0, 0:2], 0)
-        clip = jnp.minimum(1.0, clip_norm / (jnp.sqrt(shared[0]) + 1e-06))
-        loss = shared[1]
+        shared = exchange(payload, AXES)
 
     with jax.named_scope("update"):
-        new_join, new_first, new_second, first_scale, second_scale = adam(
-            clip.reshape(1),
+        new_join, new_first, new_second, first_scale, second_scale, loss = adam(
+            shared,
             join_weight,
             grads,
             first_codes,
@@ -616,7 +653,7 @@
         jnp.swapaxes(first_scale, 1, 2),
         new_second,
         jnp.swapaxes(second_scale, 1, 2),
-        loss,
+        loss.reshape(()),
     )
 
 

time: 337 us -> 321 us (0.953)
  blocking collectives: 224 us -> 245 us
  waiting for transfers between devices: 28.2 us -> 11.4 us
  local copies, waits for them, and re-layouts: 14.2 us -> 2.23 us
  starting transfers between devices: 28.2 us -> 23.8 us
    all_to_all x11 -> x12, blocking collectives: 224 us -> 245 us  [exchange(): return lax.all_to_all(value, axes, 0, 0, tiled=False)]
    all_to_all x1 -> x0, waiting for transfers between devices: 17 us -> none  [exchange(): return lax.all_to_all(value, axes, 0, 0, tiled=False)]
    unnamed x50 -> x20, local copies, waits for them, and re-layouts: 10.7 us -> 0.97 us
    pallas_call x1, Pallas kernels: 15.9 us -> 9.98 us  [adam(): pl.pallas_call(adam_kernel, grid=(3, 1024 // rows), in_specs=[pl.BlockSpe...]
    all_to_all x1 -> x0, starting transfers between devices: 5.65 us -> none  [exchange(): return lax.all_to_all(value, axes, 0, 0, tiled=False)]
    pallas_call x20, Pallas kernels: 15.9 us -> 20 us  [call(): pl.pallas_call(kernel, out_shape=[jax.ShapeDtypeStruct(shape, dtype) for...]
  transfers between devices with their start and end apart: 12 -> 11, of which waited for: 11 -> 11; matrix products, arithmetic and copies ran while one was open for 1% -> 0% of each run, Pallas kernels for 1% -> 1%
where the time goes in v4:
time: 321 us; the launch traced here: 320 us
  blocking collectives  245 us (76%)
  Pallas kernels  36.1 us (11%)
  starting transfers between devices  23.8 us (7%)
  waiting for transfers between devices  11.4 us (4%)
    all_to_all x12, blocking collectives, exchange(): return lax.all_to_all(value, axes, 0, 0, tiled=False)  245 us
    ppermute x11, starting transfers between devices, swap(): return lax.ppermute(value, 'b', [(0, 1), (1, 0)])  23.8 us
    pallas_call x20, Pallas kernels, call(): pl.pallas_call(kernel, out_shape=[jax.ShapeDtypeStruct(shape, dtype) for...  20 us
    ppermute x11, waiting for transfers between devices, swap(): return lax.ppermute(value, 'b', [(0, 1), (1, 0)])  11.4 us
    pallas_call x1, Pallas kernels, adam(): pl.pallas_call(adam_kernel, grid=(3, 1024 // rows), in_specs=[pl.BlockSpe...  9.98 us
  transfers between devices with their start and end apart: 11, of which 11 were waited for; matrix products, arithmetic and copies ran while one was open for 0% of the time, Pallas kernels for 1%

profile of v4, /device:TPU:1, one launch (start us, length us, event | category | flops | bytes accessed | tf_op | source)
XLA Modules:
  0.0 320.0 jit_solution(7360113412903336318)
XLA Ops:
  5.3 33.0 %all_to_all.60 = bf16[64,24,512]{2,1,0:T(8,128)(2,1)S(1)} all-to-all(bf16[64,24,512]{2,1,0:T(8,128)(2,1)S(1)} %half_join.1), channel_id=1, replica_groups=mesh['p'=8,'b'=2,'m'=8] {'p','m'}, dimensions={0} | all-to-all | bytes 3145728 | tf_op jit(solution)/shard_map/taps_in/all_to_all | solution.py:483
  39.6 2.5 collective-permute-start.1
  42.3 2.9 join_own.1.begun
  45.5 2.9 join_other.1
  48.5 17.7 %all_to_all.61.got = bf16[64,8,640]{2,1,0:T(8,128)(2,1)S(1)} all-to-all(bf16[64,8,640]{2,1,0:T(8,128)(2,1)S(1)} %get-tuple-element.36), channel_id=1, replica_groups=mesh['p'=8,'b'=2,'m'=8] {'p','m'}, dimensions={0} | all-to-all | bytes 1310720 | tf_op jit(solution)/shard_map/join_first/all_to_all | solution.py:483
  66.3 2.6 collective-permute-start.2
  69.8 16.4 %all_to_all.62 = bf16[64,8,512]{2,1,0:T(8,128)(2,1)S(1)} all-to-all(bf16[64,8,512]{2,1,0:T(8,128)(2,1)S(1)} %get-tuple-element.40), channel_id=1, replica_groups=mesh['p'=8,'b'=2,'m'=8] {'p','m'}, dimensions={0} | all-to-all | bytes 1048576 | tf_op jit(solution)/shard_map/hidden_first/all_to_all | solution.py:483
  89.7 2.3 join_second.1
  92.0 26.4 %all_to_all.63.got = bf16[64,8,1536]{2,1,0:T(8,128)(2,1)S(1)} all-to-all(bf16[64,8,1536]{2,1,0:T(8,128)(2,1)S(1)} %join_second.1), channel_id=1, replica_groups=mesh['p'=8,'b'=2,'m'=8] {'p','m'}, dimensions={0} | all-to-all | bytes 3145728 | tf_op jit(solution)/shard_map/join_second/all_to_all | solution.py:483
  118.7 2.5 collective-permute-start.4
  122.2 16.8 %all_to_all.64 = bf16[64,8,512]{2,1,0:T(8,128)(2,1)S(1)} all-to-all(bf16[64,8,512]{2,1,0:T(8,128)(2,1)S(1)} %get-tuple-element.44), channel_id=1, replica_groups=mesh['p'=8,'b'=2,'m'=8] {'p','m'}, dimensions={0} | all-to-all | bytes 1048576 | tf_op jit(solution)/shard_map/hidden_second/all_to_all | solution.py:483
  144.3 21.6 %all_to_all.65.got = bf16[64,8,1024]{2,1,0:T(8,128)(2,1)S(1)} all-to-all(bf16[64,8,1024]{2,1,0:T(8,128)(2,1)S(1)} %logits.1), channel_id=1, replica_groups=mesh['p'=8,'b'=2,'m'=8] {'p','m'}, dimensions={0} | all-to-all | bytes 2097152 | tf_op jit(solution)/shard_map/logits/all_to_all | solution.py:483
  166.9 2.2 collective-permute-start.6
  170.9 21.8 %all_to_all.66 = bf16[64,8,1024]{2,1,0:T(8,128)(2,1)S(1)} all-to-all(bf16[64,8,1024]{2,1,0:T(8,128)(2,1)S(1)} %get-tuple-element.49), channel_id=1, replica_groups=mesh['p'=8,'b'=2,'m'=8] {'p','m'}, dimensions={0} | all-to-all | bytes 2097152 | tf_op jit(solution)/shard_map/softmax/all_to_all | solution.py:483
  193.9 2.1 collective-permute-start.7
  198.9 16.6 %all_to_all.67.got = bf16[64,8,512]{2,1,0:T(8,128)(2,1)S(1)} all-to-all(bf16[64,8,512]{2,1,0:T(8,128)(2,1)S(1)} %head_keep.1), channel_id=1, replica_groups=mesh['p'=8,'b'=2,'m'=8] {'p','m'}, dimensions={0} | all-to-all | bytes 1048576 | tf_op jit(solution)/shard_map/back_second/all_to_all | solution.py:483
  218.5 26.4 %all_to_all.68 = bf16[64,8,1536]{2,1,0:T(8,128)(2,1)S(1)} all-to-all(bf16[64,8,1536]{2,1,0:T(8,128)(2,1)S(1)} %norm_back.2), channel_id=1, replica_groups=mesh['p'=8,'b'=2,'m'=8] {'p','m'}, dimensions={0} | all-to-all | bytes 3145728 | tf_op jit(solution)/shard_map/back_second/all_to_all | solution.py:483
  246.5 2.6 collective-permute-start.9
  252.2 17.0 %all_to_all.69.got = bf16[64,8,512]{2,1,0:T(8,128)(2,1)S(1)} all-to-all(bf16[64,8,512]{2,1,0:T(8,128)(2,1)S(1)} %feed_keep.1), channel_id=1, replica_groups=mesh['p'=8,'b'=2,'m'=8] {'p','m'}, dimensions={0} | all-to-all | bytes 1048576 | tf_op jit(solution)/shard_map/back_first/all_to_all | solution.py:483
  269.3 2.0 collective-permute-start.10
  272.2 16.4 %all_to_all.70 = bf16[64,8,512]{2,1,0:T(8,128)(2,1)S(1)} all-to-all(bf16[64,8,512]{2,1,0:T(8,128)(2,1)S(1)} %norm_back.3), channel_id=1, replica_groups=mesh['p'=8,'b'=2,'m'=8] {'p','m'}, dimensions={0} | all-to-all | bytes 1048576 | tf_op jit(solution)/shard_map/back_first/all_to_all | solution.py:483
  288.7 6.1 %gradients.1 = (f32[3,1024,512]{2,1,0:T(8,128)S(1)}, f32[128,1,128]{2,1,0:T(1,128)S(1)}) custom-call(s32[2]{0:T(128)S(1)} %pad_add_fusion.core.places, bf16[3,512,512]{2,1,0:T(8,128)(2,1)} %copy_bitcast_fusion.taps.own, bf16[3,512,512]{2,1,0:T(8,128)(2,1)} %collective-permute-done.1.taps.other, bf16[512,512]{1,0:T(8,128)(2,1)S(1)} %bitcast.32, ...), custom_call_target="tpu_custom_call" | custom-call | flops 3221225472 | bytes 10485760 | tf_op jit(solution)/shard_map/gradients/gradients/pallas_call | solution.py:349
  294.8 15.0 %all_to_all.71.shared = f32[128,1,128]{2,1,0:T(1,128)S(1)} all-to-all(f32[128,1,128]{2,1,0:T(1,128)S(1)} %get-tuple-element.58), channel_id=1, replica_groups=mesh['p'=8,'b'=2,'m'=8] {'p','b','m'}, dimensions={0} | all-to-all | bytes 131072 | tf_op jit(solution)/shard_map/gradients/all_to_all | solution.py:483
  309.8 10.0 %update.1 = (bf16[3,1024,512]{2,1,0:T(8,128)(2,1)}, bf16[3,1024,512]{2,1,0:T(8,128)(2,1)}, bf16[3,1024,512]{2,1,0:T(8,128)(2,1)}, f32[3,2,1024]{2,1,0:T(2,128)}, f32[3,2,1024]{2,1,0:T(2,128)}, /*index=5*/f32[1,1]{1,0:T(1,128)}) custom-call(f32[128,1,128]{2,1,0:T(1,128)S(1)} %all_to_all.71.shared, bf16[3,1024,512]{2,1,0:T(8,128)(2,1)S(1)} %copy-done, ...), custom_call_target="tpu_custom_call" | custom-call | tf_op jit(solution)/shard_map/update/update/pallas_call | solution.py:445
  (58 shorter events, 33.1 us)
Async XLA Ops:
  0.7 0.9 copy-start.4
  2.2 2.4 collective-permute-start
  38.3 3.8 %copy-start.8 = (s32[2,16,4]{1,2,0:T(4,128)S(1)}, s32[2,16,4]{1,2,0:T(4,128)}, u32[]{:S(2)}) copy-start(s32[2,16,4]{1,2,0:T(4,128)} %param.15) | copy-start | bytes 1540
  38.3 3.9 %copy-start.9 = (f32[512]{0:T(512)S(1)}, f32[512]{0:T(512)}, u32[]{:S(2)}) copy-start(f32[512]{0:T(512)} %param.11) | copy-start | bytes 6148
  38.3 4.0 %copy-start = (bf16[3,1024,512]{2,1,0:T(8,128)(2,1)S(1)}, bf16[3,1024,512]{2,1,0:T(8,128)(2,1)}, u32[]{:S(2)}) copy-start(bf16[3,1024,512]{2,1,0:T(8,128)(2,1)} %weight.11) | copy-start | bytes 9437188
  39.6 5.9 %collective-permute-start.1 = (bf16[3,512,512]{2,1,0:T(8,128)(2,1)}, bf16[3,512,512]{2,1,0:T(8,128)(2,1)}, u32[]{:S(2)}, u32[]{:S(2)}) collective-permute-start(bf16[3,512,512]{2,1,0:T(8,128)(2,1)} %copy_bitcast_fusion.taps.own), channel_id=1, source_target_pairs={{0,8},{8,0},{1,9},{9,1},{2,10},{10,2},{3,11},{11,3},{4,12},{12,4},... | collective-permute-start | bytes 4718600 | tf_op jit(solution)/shard_map/taps_in/ppermute | solution.py:480
  48.4 41.2 %copy-start.1 = (bf16[1024,1024]{1,0:T(8,128)(2,1)S(1)}, bf16[1024,1024]{1,0:T(8,128)(2,1)}, u32[]{:S(2)}) copy-start(bf16[1024,1024]{1,0:T(8,128)(2,1)} %head.11) | copy-start | bytes 6291460
  66.3 3.4 %collective-permute-start.2 = (f32[8,128]{1,0:T(8,128)S(1)}, f32[8,128]{1,0:T(8,128)S(1)}, u32[]{:S(2)}, u32[]{:S(2)}) collective-permute-start(f32[8,128]{1,0:T(8,128)S(1)} %get-tuple-element.39.squares), channel_id=1, source_target_pairs={{0,8},{8,0},{1,9},{9,1},{2,10},{10,2},{3,11},{11,3},{4,12},{12,4},... | collective-permute-start | bytes 12296 | tf_op jit(solution)/shard_map/hidden_first/ppermute | solution.py:480
  86.2 3.5 %collective-permute-start.3 = (bf16[512,512]{1,0:T(8,128)(2,1)S(1)}, bf16[512,512]{1,0:T(8,128)(2,1)S(1)}, u32[]{:S(2)}, u32[]{:S(2)}) collective-permute-start(bf16[512,512]{1,0:T(8,128)(2,1)S(1)} %bitcast.30), channel_id=1, source_target_pairs={{0,8},{8,0},{1,9},{9,1},{2,10},{10,2},{3,11},{11,3},{4,12},{12,4},... | collective-permute-start | bytes 1572872 | tf_op jit(solution)/shard_map/hidden_first/ppermute | solution.py:480
  118.7 3.3 %collective-permute-start.4 = (f32[8,128]{1,0:T(8,128)S(1)}, f32[8,128]{1,0:T(8,128)S(1)}, u32[]{:S(2)}, u32[]{:S(2)}) collective-permute-start(f32[8,128]{1,0:T(8,128)S(1)} %get-tuple-element.43.squares), channel_id=1, source_target_pairs={{0,8},{8,0},{1,9},{9,1},{2,10},{10,2},{3,11},{11,3},{4,12},{12,4},... | collective-permute-start | bytes 12296 | tf_op jit(solution)/shard_map/hidden_second/ppermute | solution.py:480
  139.0 3.5 %collective-permute-start.5 = (bf16[512,512]{1,0:T(8,128)(2,1)S(1)}, bf16[512,512]{1,0:T(8,128)(2,1)S(1)}, u32[]{:S(2)}, u32[]{:S(2)}) collective-permute-start(bf16[512,512]{1,0:T(8,128)(2,1)S(1)} %bitcast.33), channel_id=1, source_target_pairs={{0,8},{8,0},{1,9},{9,1},{2,10},{10,2},{3,11},{11,3},{4,12},{12,4},... | collective-permute-start | bytes 1572872 | tf_op jit(solution)/shard_map/hidden_second/ppermute | solution.py:480
  144.3 21.6 %copy-start.7 = (s32[2,16,4]{1,2,0:T(4,128)S(1)}, s32[2,16,4]{1,2,0:T(4,128)}, u32[]{:S(2)}) copy-start(s32[2,16,4]{1,2,0:T(4,128)} %param.14) | copy-start | bytes 1540
  166.9 3.1 collective-permute-start.6
  193.9 3.6 %collective-permute-start.7 = (bf16[64,8,512]{2,1,0:T(8,128)(2,1)S(1)}, bf16[64,8,512]{2,1,0:T(8,128)(2,1)S(1)}, u32[]{:S(2)}, u32[]{:S(2)}) collective-permute-start(bf16[64,8,512]{2,1,0:T(8,128)(2,1)S(1)} %head_away.1), channel_id=1, source_target_pairs={{0,8},{8,0},{1,9},{9,1},{2,10},{10,2},{3,11},{11,3},{4,12},{12,4},... | collective-permute-start | bytes 1572872 | tf_op jit(solution)/shard_map/back_second/ppermute | solution.py:480
  215.6 2.8 collective-permute-start.8
  246.5 4.1 %collective-permute-start.9 = (bf16[64,8,512]{2,1,0:T(8,128)(2,1)S(1)}, bf16[64,8,512]{2,1,0:T(8,128)(2,1)S(1)}, u32[]{:S(2)}, u32[]{:S(2)}) collective-permute-start(bf16[64,8,512]{2,1,0:T(8,128)(2,1)S(1)} %feed_away.1), channel_id=1, source_target_pairs={{0,8},{8,0},{1,9},{9,1},{2,10},{10,2},{3,11},{11,3},{4,12},{12,4},... | collective-permute-start | bytes 1572872 | tf_op jit(solution)/shard_map/back_first/ppermute | solution.py:480
  269.3 2.8 collective-permute-start.10
  288.6 21.2 %copy-start.2 = (bf16[3,1024,512]{2,1,0:T(8,128)(2,1)S(1)}, bf16[3,1024,512]{2,1,0:T(8,128)(2,1)}, u32[]{:S(2)}) copy-start(bf16[3,1024,512]{2,1,0:T(8,128)(2,1)} %first.1) | copy-start | bytes 9437188
  288.6 21.2 %copy-start.3 = (bf16[3,1024,512]{2,1,0:T(8,128)(2,1)S(1)}, bf16[3,1024,512]{2,1,0:T(8,128)(2,1)}, u32[]{:S(2)}) copy-start(bf16[3,1024,512]{2,1,0:T(8,128)(2,1)} %second.1) | copy-start | bytes 9437188
  288.6 21.2 %copy-start.5 = (f32[3,1024,2]{1,2,0:T(2,128)S(1)}, f32[3,1024,2]{1,2,0:T(2,128)}, u32[]{:S(2)}) copy-start(f32[3,1024,2]{1,2,0:T(2,128)} %param.17) | copy-start | bytes 73732
  288.6 21.2 %copy-start.6 = (f32[3,1024,2]{1,2,0:T(2,128)S(1)}, f32[3,1024,2]{1,2,0:T(2,128)}, u32[]{:S(2)}) copy-start(f32[3,1024,2]{1,2,0:T(2,128)} %param.19) | copy-start | bytes 73732

commit v5 on v4

--- a/solution.py
+++ b/solution.py
@@ -111,10 +111,10 @@
     return pl.BlockSpec(shape, lambda i, core: (0,) * len(shape))
 
 
-def half_out_kernel(core, taps, out):
+def half_out_kernel(group, taps, out):
     sets, _, width = taps.shape
     chunks = width // 1024
-    other = (1 - core[0]) * 512
+    other = (1 - group[0] % 2) * 512
     for s in range(sets):
         for chunk in range(chunks):
             start = pl.multiple_of(chunk * 1024 + other, 512)
@@ -141,14 +141,16 @@
 
 
 def join_own_kernel(core, taps, weight, out):
-    out[0] = dot(taps[0], weight[0]) + dot(taps[1], weight[1])
-    out[1] = dot(taps[2], weight[2])
+    rows = half_rows(core[0])
+    out[0] = dot(taps[0], weight[0, rows]) + dot(taps[1], weight[1, rows])
+    out[1] = dot(taps[2], weight[2, rows])
 
 
 def join_other_kernel(core, taps, weight, begun, side, constant, out):
-    fixed = begun[0] + dot(taps[0], weight[0]) + dot(taps[1], weight[1])
+    rows = half_rows(core[0])
+    fixed = begun[0] + dot(taps[0], weight[0, rows]) + dot(taps[1], weight[1, rows])
     constant[...] = fixed
-    out[:, :, :512] = to_blocks(fixed + begun[1] + dot(taps[2], weight[2]))
+    out[:, :, :512] = to_blocks(fixed + begun[1] + dot(taps[2], weight[2, rows]))
     out[:, :, 512:] = jnp.broadcast_to(side[...], (64, 8, LANES)).astype(bf16)
 
 
@@ -159,7 +161,7 @@
 
 
 def join_second_kernel(core, mine, theirs, weight, head, constant, out):
-    joined = constant[...] + both_halves(core, mine, theirs, weight.at[0])
+    joined = constant[...] + both_halves(core, mine, theirs, weight.at[2])
     out[:, :, :512] = to_blocks(joined)
     out[:, :, 512:] = to_blocks(both_halves(core, mine, theirs, head))
 
@@ -179,7 +181,7 @@
 def feed_back_kernel(core, got, weight, head, *rest):
     *added, out = rest
     rows = half_rows(core[0])
-    value = contract_last(got[:, :512], weight[0, rows])
+    value = contract_last(got[:, :512], weight[2, rows])
     value += contract_last(got[:, 512:], head[rows])
     if added:
         value += added[0][...].astype(f32).reshape(512, 512)
@@ -243,19 +245,19 @@
     return lax.broadcasted_iota(jnp.int32, (8, 1024), 1) + (2 * chunk + core) * 1024
 
 
-def own_tokens(places, values):
+def own_tokens(group, values):
     wide = values.astype(f32)
     lane = lax.broadcasted_iota(jnp.int32, wide.shape, 1)
     return jnp.concatenate(
         [
-            jnp.sum(jnp.where(lane == places[1] + i, wide, 0.0), -1, keepdims=True)
+            jnp.sum(jnp.where(lane == group[0] - group[0] % 2 + i, wide, 0.0), -1, keepdims=True)
             for i in range(2)
         ],
         axis=0,
     )
 
 
-def stats_kernel(places, got, logits_first, targets, logits_second, stats):
+def stats_kernel(group, got, logits_first, targets, logits_second, stats):
     for chunk in range(CHUNKS):
         logits_second[chunk] = column_sum(got, chunk, 0, 1024)
     columns = []
@@ -265,11 +267,11 @@
             top = jnp.maximum(top, logits[chunk])
         top = jnp.max(top, -1, keepdims=True)
         weights = jnp.zeros((8, 1024), f32)
-        target = own_tokens(places, targets[step]).astype(jnp.int32)
+        target = own_tokens(group, targets[step]).astype(jnp.int32)
         picked = jnp.zeros((8, 1024), f32)
         for chunk in range(CHUNKS):
             weights += jnp.exp(logits[chunk] - top)
-            hit = vocab_of(places[0], chunk) == target
+            hit = vocab_of(group[0] % 2, chunk) == target
             picked += jnp.where(hit, logits[chunk], 0.0)
         columns += [
             top,
@@ -280,7 +282,7 @@
 
 
 def logit_grad_kernel(
-    places, stats, stats_other, logits_first, logits_second, targets, masks, counts,
+    group, stats, stats_other, logits_first, logits_second, targets, masks, counts,
     grads_first, grads_second, loss,
 ):
     lost = jnp.zeros((8, 1), f32)
@@ -294,19 +296,19 @@
         top = jnp.maximum(top_mine, top_other)
         total = sum_mine * jnp.exp(top_mine - top) + sum_other * jnp.exp(top_other - top)
         log_total = top + jnp.log(total)
-        weight = own_tokens(places, masks[step]) / counts[:, step : step + 1]
-        target = own_tokens(places, targets[step]).astype(jnp.int32)
+        weight = own_tokens(group, masks[step]) / counts[:, step : step + 1]
+        target = own_tokens(group, targets[step]).astype(jnp.int32)
         lost += weight * (log_total - picked)
         for chunk in range(CHUNKS):
             probs = jnp.exp(logits[chunk] - log_total)
-            hit = jnp.where(vocab_of(places[0], chunk) == target, 1.0, 0.0)
+            hit = jnp.where(vocab_of(group[0] % 2, chunk) == target, 1.0, 0.0)
             grad = (weight * (probs - hit)).astype(bf16)
             if step == 0:
                 grads_first[chunk] = grad
             else:
                 for copy in range(CHUNKS):
                     grads_second[chunk * CHUNKS + copy] = grad
-    once = jnp.where(places[0] == 0, 1.0, 0.0)
+    once = jnp.where(group[0] % 2 == 0, 1.0, 0.0)
     loss[...] = jnp.broadcast_to(jnp.sum(lost, 0, keepdims=True) * once, (8, LANES))
 
 
@@ -472,8 +474,9 @@
     core = lax.axis_index("b")
     row = lax.axis_index("p")
     column = lax.axis_index("m")
-    own = jnp.stack([core, 2 * row]).astype(jnp.int32)
-    other = jnp.stack([1 - core, 2 * row]).astype(jnp.int32)
+    own = core.reshape(1).astype(jnp.int32)
+    other = 1 - own
+    group = (2 * row + core).reshape(1).astype(jnp.int32)
     chips = ("p", "m")
 
     def swap(value):
@@ -497,13 +500,10 @@
     vocab_f32 = ((CHUNKS, 8, 1024), f32)
     blocks = ((64, 8, 512), bf16)
     half_flops = 2 * 512**3
-    last_join = pl.BlockSpec((1, 1024, 512), lambda i, core: (2, 0, 0))
-    tokens_half, tokens_wide = whole_block((512, 512)), whole_block((512, 1024))
-    head_block, parts_block = whole_block((1024, 1024)), whole_block((64, 8, 512))
 
     with jax.named_scope("taps_in"):
         outgoing = call(
-            half_out_kernel, "half_out", [((3, 4, D // 2), bf16)], ("s", own), ("v", taps)
+            half_out_kernel, "half_out", [((3, 4, D // 2), bf16)], ("s", group), ("v", taps)
         )
         packed = call(
             half_join_kernel, "half_join", [((64, 24, 512), bf16)],
@@ -514,23 +514,15 @@
         taps_other = swap(taps_own)
 
     with jax.named_scope("join_first"):
-        sets = whole_block((3, 512, 512))
         begun = call(
             join_own_kernel, "join_own", [((2, 512, 512), f32)],
             ("s", own), ("v", taps_own), ("v", join_weight),
-            specs=[sets, pl.BlockSpec((3, 512, 512), lambda i, core: (0, core[0], 0))],
             flops=3 * half_flops,
         )
         constant, parts = call(
             join_other_kernel, "join_other",
             [((512, 512), f32), ((64, 8, 640), bf16)],
             ("s", other), ("v", taps_other), ("v", join_weight), ("v", begun), ("v", side),
-            specs=[
-                sets,
-                pl.BlockSpec((3, 512, 512), lambda i, core: (0, core[0], 0)),
-                whole_block((2, 512, 512)),
-                whole_block((8, LANES)),
-            ],
             flops=3 * half_flops,
         )
         joining_first, gains, counts, squares = call(
@@ -554,7 +546,6 @@
             join_second_kernel, "join_second", [((64, 8, 1536), bf16)],
             ("s", own), ("v", hidden_mine), ("v", hidden_theirs), ("v", join_weight),
             ("v", head_weight), ("v", constant),
-            specs=[tokens_half, tokens_half, last_join, head_block, tokens_half],
             flops=6 * half_flops,
         )
         joining_second, logits_first, squares = call(
@@ -569,7 +560,6 @@
         parts = call(
             logits_kernel, "logits", [((64, 8, 1024), bf16)],
             ("s", own), ("v", later_mine), ("v", later_theirs), ("v", head_weight),
-            specs=[tokens_half, tokens_half, head_block],
             flops=4 * half_flops,
         )
         got = exchange(parts)
@@ -577,12 +567,12 @@
     with jax.named_scope("softmax"):
         logits_second, stats = call(
             stats_kernel, "stats", [vocab_f32, table],
-            ("s", own), ("v", got), ("v", logits_first), ("v", target_ids),
+            ("s", group), ("v", got), ("v", logits_first), ("v", target_ids),
         )
         grads_first, copies, loss = call(
             logit_grad_kernel, "logit_grad",
             [((CHUNKS, 8, 1024), bf16), ((64, 8, 1024), bf16), table],
-            ("s", own), ("v", stats), ("v", swap(stats)), ("v", logits_first),
+            ("s", group), ("v", stats), ("v", swap(stats)), ("v", logits_first),
             ("v", logits_second), ("v", target_ids), ("v", mask_ids), ("v", counts),
             specs=[
                 whole_block((8, LANES)), whole_block((8, LANES)),
@@ -607,27 +597,26 @@
         return exchange(copies).reshape(512, width)
 
     with jax.named_scope("back_second"):
-        specs, operands = [tokens_wide, head_block], (("v", grads_second), ("v", head_weight))
+        operands = (("v", grads_second), ("v", head_weight))
         away = call(
             head_back_kernel, "head_away", [blocks], ("s", other), *operands,
-            specs=specs, flops=2 * half_flops,
+            flops=2 * half_flops,
         )
         parts = call(
             head_back_kernel, "head_keep", [blocks], ("s", own), *operands,
-            ("v", swap(away)), specs=specs + [parts_block], flops=2 * half_flops,
+            ("v", swap(away)), flops=2 * half_flops,
         )
         got = row_gradients(parts, joining_second, inverse_second, grads_first)
 
     with jax.named_scope("back_first"):
-        specs = [whole_block((512, 1536)), last_join, head_block]
         operands = (("v", got), ("v", join_weight), ("v", head_weight))
         away = call(
             feed_back_kernel, "feed_away", [blocks], ("s", other), *operands,
-            specs=specs, flops=3 * half_flops,
+            flops=3 * half_flops,
         )
         parts = call(
             feed_back_kernel, "feed_keep", [blocks], ("s", own), *operands,
-            ("v", swap(away)), specs=specs + [parts_block], flops=3 * half_flops,
+            ("v", swap(away)), flops=3 * half_flops,
         )
         first_all = row_gradients(parts, joining_first, inverse_first)
 

time: 321 us -> 315 us (0.981)
  Pallas kernels: 36.1 us -> 28.9 us
    pallas_call x20, Pallas kernels: 20 us -> 13.5 us  [call(): pl.pallas_call(kernel, out_shape=[jax.ShapeDtypeStruct(shape, dtype) for...]
where the time goes in v5:
time: 315 us; the launch traced here: 314 us
  blocking collectives  246 us (78%)
  Pallas kernels  28.9 us (9%)
  starting transfers between devices  23.3 us (7%)
  waiting for transfers between devices  12.1 us (4%)
  local copies, waits for them, and re-layouts  3.15 us (1%)
    all_to_all x12, blocking collectives, exchange(): return lax.all_to_all(value, axes, 0, 0, tiled=False)  246 us
    ppermute x11, starting transfers between devices, swap(): return lax.ppermute(value, 'b', [(0, 1), (1, 0)])  23.3 us
    pallas_call x20, Pallas kernels, call(): pl.pallas_call(kernel, out_shape=[jax.ShapeDtypeStruct(shape, dtype) for...  13.5 us
    ppermute x11, waiting for transfers between devices, swap(): return lax.ppermute(value, 'b', [(0, 1), (1, 0)])  12.1 us
    pallas_call x1, Pallas kernels, adam(): pl.pallas_call(adam_kernel, grid=(3, 1024 // rows), in_specs=[pl.BlockSpe...  9.98 us
  transfers between devices with their start and end apart: 11, of which 11 were waited for; matrix products, arithmetic and copies ran while one was open for 0% of the time, Pallas kernels for 1%

profile of v5, /device:TPU:1, one launch (start us, length us, event | category | flops | bytes accessed | tf_op | source)
XLA Modules:
  0.0 314.2 jit_solution(961491130338229750)
XLA Ops:
  5.1 33.0 %all_to_all.60 = bf16[64,24,512]{2,1,0:T(8,128)(2,1)S(1)} all-to-all(bf16[64,24,512]{2,1,0:T(8,128)(2,1)S(1)} %half_join.1), channel_id=1, replica_groups=mesh['p'=8,'b'=2,'m'=8] {'p','m'}, dimensions={0} | all-to-all | bytes 3145728 | tf_op jit(solution)/shard_map/taps_in/all_to_all | solution.py:486
  39.4 2.5 collective-permute-start.1
  42.0 2.4 join_own.1.begun
  45.2 2.4 join_other.1
  47.7 18.3 %all_to_all.61.got = bf16[64,8,640]{2,1,0:T(8,128)(2,1)S(1)} all-to-all(bf16[64,8,640]{2,1,0:T(8,128)(2,1)S(1)} %get-tuple-element.36), channel_id=1, replica_groups=mesh['p'=8,'b'=2,'m'=8] {'p','m'}, dimensions={0} | all-to-all | bytes 1310720 | tf_op jit(solution)/shard_map/join_first/all_to_all | solution.py:486
  66.1 2.0 collective-permute-start.2
  69.0 16.4 %all_to_all.62 = bf16[64,8,512]{2,1,0:T(8,128)(2,1)S(1)} all-to-all(bf16[64,8,512]{2,1,0:T(8,128)(2,1)S(1)} %get-tuple-element.40), channel_id=1, replica_groups=mesh['p'=8,'b'=2,'m'=8] {'p','m'}, dimensions={0} | all-to-all | bytes 1048576 | tf_op jit(solution)/shard_map/hidden_first/all_to_all | solution.py:486
  90.7 26.4 %all_to_all.63.got = bf16[64,8,1536]{2,1,0:T(8,128)(2,1)S(1)} all-to-all(bf16[64,8,1536]{2,1,0:T(8,128)(2,1)S(1)} %join_second.1), channel_id=1, replica_groups=mesh['p'=8,'b'=2,'m'=8] {'p','m'}, dimensions={0} | all-to-all | bytes 3145728 | tf_op jit(solution)/shard_map/join_second/all_to_all | solution.py:486
  117.4 2.5 collective-permute-start.4
  120.9 16.8 %all_to_all.64 = bf16[64,8,512]{2,1,0:T(8,128)(2,1)S(1)} all-to-all(bf16[64,8,512]{2,1,0:T(8,128)(2,1)S(1)} %get-tuple-element.44), channel_id=1, replica_groups=mesh['p'=8,'b'=2,'m'=8] {'p','m'}, dimensions={0} | all-to-all | bytes 1048576 | tf_op jit(solution)/shard_map/hidden_second/all_to_all | solution.py:486
  142.5 21.6 %all_to_all.65.got = bf16[64,8,1024]{2,1,0:T(8,128)(2,1)S(1)} all-to-all(bf16[64,8,1024]{2,1,0:T(8,128)(2,1)S(1)} %logits.1), channel_id=1, replica_groups=mesh['p'=8,'b'=2,'m'=8] {'p','m'}, dimensions={0} | all-to-all | bytes 2097152 | tf_op jit(solution)/shard_map/logits/all_to_all | solution.py:486
  164.4 2.3 collective-permute-start.6
  167.9 21.8 %all_to_all.66 = bf16[64,8,1024]{2,1,0:T(8,128)(2,1)S(1)} all-to-all(bf16[64,8,1024]{2,1,0:T(8,128)(2,1)S(1)} %get-tuple-element.49), channel_id=1, replica_groups=mesh['p'=8,'b'=2,'m'=8] {'p','m'}, dimensions={0} | all-to-all | bytes 2097152 | tf_op jit(solution)/shard_map/softmax/all_to_all | solution.py:486
  190.5 2.1 collective-permute-start.7
  194.8 16.6 %all_to_all.67.got = bf16[64,8,512]{2,1,0:T(8,128)(2,1)S(1)} all-to-all(bf16[64,8,512]{2,1,0:T(8,128)(2,1)S(1)} %head_keep.1), channel_id=1, replica_groups=mesh['p'=8,'b'=2,'m'=8] {'p','m'}, dimensions={0} | all-to-all | bytes 1048576 | tf_op jit(solution)/shard_map/back_second/all_to_all | solution.py:486
  211.6 2.0 collective-permute-start.8
  214.5 26.4 %all_to_all.68 = bf16[64,8,1536]{2,1,0:T(8,128)(2,1)S(1)} all-to-all(bf16[64,8,1536]{2,1,0:T(8,128)(2,1)S(1)} %norm_back.2), channel_id=1, replica_groups=mesh['p'=8,'b'=2,'m'=8] {'p','m'}, dimensions={0} | all-to-all | bytes 3145728 | tf_op jit(solution)/shard_map/back_second/all_to_all | solution.py:486
  241.9 2.6 collective-permute-start.9
  247.1 17.0 %all_to_all.69.got = bf16[64,8,512]{2,1,0:T(8,128)(2,1)S(1)} all-to-all(bf16[64,8,512]{2,1,0:T(8,128)(2,1)S(1)} %feed_keep.1), channel_id=1, replica_groups=mesh['p'=8,'b'=2,'m'=8] {'p','m'}, dimensions={0} | all-to-all | bytes 1048576 | tf_op jit(solution)/shard_map/back_first/all_to_all | solution.py:486
  264.2 2.0 collective-permute-start.10
  267.1 16.4 %all_to_all.70 = bf16[64,8,512]{2,1,0:T(8,128)(2,1)S(1)} all-to-all(bf16[64,8,512]{2,1,0:T(8,128)(2,1)S(1)} %norm_back.3), channel_id=1, replica_groups=mesh['p'=8,'b'=2,'m'=8] {'p','m'}, dimensions={0} | all-to-all | bytes 1048576 | tf_op jit(solution)/shard_map/back_first/all_to_all | solution.py:486
  283.5 5.4 %gradients.1 = (f32[3,1024,512]{2,1,0:T(8,128)S(1)}, f32[128,1,128]{2,1,0:T(1,128)S(1)}) custom-call(s32[1]{0:T(128)} %bitcast.core, bf16[3,512,512]{2,1,0:T(8,128)(2,1)} %copy_bitcast_fusion.taps.own, bf16[3,512,512]{2,1,0:T(8,128)(2,1)} %collective-permute-done.1.taps.other, bf16[512,512]{1,0:T(8,128)(2,1)S(1)} %bitcast.31, ...), custom_call_target="tpu_custom_call" | custom-call | flops 3221225472 | bytes 10485760 | tf_op jit(solution)/shard_map/gradients/gradients/pallas_call | solution.py:351
  289.0 15.0 %all_to_all.71.shared = f32[128,1,128]{2,1,0:T(1,128)S(1)} all-to-all(f32[128,1,128]{2,1,0:T(1,128)S(1)} %get-tuple-element.58), channel_id=1, replica_groups=mesh['p'=8,'b'=2,'m'=8] {'p','b','m'}, dimensions={0} | all-to-all | bytes 131072 | tf_op jit(solution)/shard_map/gradients/all_to_all | solution.py:486
  304.1 10.0 %update.1 = (bf16[3,1024,512]{2,1,0:T(8,128)(2,1)}, bf16[3,1024,512]{2,1,0:T(8,128)(2,1)}, bf16[3,1024,512]{2,1,0:T(8,128)(2,1)}, f32[3,2,1024]{2,1,0:T(2,128)}, f32[3,2,1024]{2,1,0:T(2,128)}, /*index=5*/f32[1,1]{1,0:T(1,128)}) custom-call(f32[128,1,128]{2,1,0:T(1,128)S(1)} %all_to_all.71.shared, bf16[3,1024,512]{2,1,0:T(8,128)(2,1)S(1)} %copy-done, ...), custom_call_target="tpu_custom_call" | custom-call | tf_op jit(solution)/shard_map/update/update/pallas_call | solution.py:447
  (58 shorter events, 29.4 us)
Async XLA Ops:
  0.6 0.9 copy-start.4
  1.6 2.4 collective-permute-start
  4.0 0.9 copy-start.5
  38.1 3.8 %copy-start.9 = (s32[2,16,4]{1,2,0:T(4,128)S(1)}, s32[2,16,4]{1,2,0:T(4,128)}, u32[]{:S(2)}) copy-start(s32[2,16,4]{1,2,0:T(4,128)} %param.15) | copy-start | bytes 1540
  38.1 3.9 %copy-start.10 = (f32[512]{0:T(512)S(1)}, f32[512]{0:T(512)}, u32[]{:S(2)}) copy-start(f32[512]{0:T(512)} %param.11) | copy-start | bytes 6148
  38.1 3.9 %copy-start = (bf16[3,1024,512]{2,1,0:T(8,128)(2,1)S(1)}, bf16[3,1024,512]{2,1,0:T(8,128)(2,1)}, u32[]{:S(2)}) copy-start(bf16[3,1024,512]{2,1,0:T(8,128)(2,1)} %weight.11) | copy-start | bytes 9437188
  39.4 5.9 %collective-permute-start.1 = (bf16[3,512,512]{2,1,0:T(8,128)(2,1)}, bf16[3,512,512]{2,1,0:T(8,128)(2,1)}, u32[]{:S(2)}, u32[]{:S(2)}) collective-permute-start(bf16[3,512,512]{2,1,0:T(8,128)(2,1)} %copy_bitcast_fusion.taps.own), channel_id=1, source_target_pairs={{0,8},{8,0},{1,9},{9,1},{2,10},{10,2},{3,11},{11,3},{4,12},{12,4},... | collective-permute-start | bytes 4718600 | tf_op jit(solution)/shard_map/taps_in/ppermute | solution.py:483
  47.7 41.2 %copy-start.1 = (bf16[1024,1024]{1,0:T(8,128)(2,1)S(1)}, bf16[1024,1024]{1,0:T(8,128)(2,1)}, u32[]{:S(2)}) copy-start(bf16[1024,1024]{1,0:T(8,128)(2,1)} %head.11) | copy-start | bytes 6291460
  66.1 2.8 collective-permute-start.2
  85.4 3.5 %collective-permute-start.3 = (bf16[512,512]{1,0:T(8,128)(2,1)S(1)}, bf16[512,512]{1,0:T(8,128)(2,1)S(1)}, u32[]{:S(2)}, u32[]{:S(2)}) collective-permute-start(bf16[512,512]{1,0:T(8,128)(2,1)S(1)} %bitcast.29), channel_id=1, source_target_pairs={{0,8},{8,0},{1,9},{9,1},{2,10},{10,2},{3,11},{11,3},{4,12},{12,4},... | collective-permute-start | bytes 1572872 | tf_op jit(solution)/shard_map/hidden_first/ppermute | solution.py:483
  117.4 3.3 %collective-permute-start.4 = (f32[8,128]{1,0:T(8,128)S(1)}, f32[8,128]{1,0:T(8,128)S(1)}, u32[]{:S(2)}, u32[]{:S(2)}) collective-permute-start(f32[8,128]{1,0:T(8,128)S(1)} %get-tuple-element.43.squares), channel_id=1, source_target_pairs={{0,8},{8,0},{1,9},{9,1},{2,10},{10,2},{3,11},{11,3},{4,12},{12,4},... | collective-permute-start | bytes 12296 | tf_op jit(solution)/shard_map/hidden_second/ppermute | solution.py:483
  137.7 3.5 %collective-permute-start.5 = (bf16[512,512]{1,0:T(8,128)(2,1)S(1)}, bf16[512,512]{1,0:T(8,128)(2,1)S(1)}, u32[]{:S(2)}, u32[]{:S(2)}) collective-permute-start(bf16[512,512]{1,0:T(8,128)(2,1)S(1)} %bitcast.32), channel_id=1, source_target_pairs={{0,8},{8,0},{1,9},{9,1},{2,10},{10,2},{3,11},{11,3},{4,12},{12,4},... | collective-permute-start | bytes 1572872 | tf_op jit(solution)/shard_map/hidden_second/ppermute | solution.py:483
  142.5 21.6 %copy-start.8 = (s32[2,16,4]{1,2,0:T(4,128)S(1)}, s32[2,16,4]{1,2,0:T(4,128)}, u32[]{:S(2)}) copy-start(s32[2,16,4]{1,2,0:T(4,128)} %param.14) | copy-start | bytes 1540
  164.4 3.1 collective-permute-start.6
  190.5 3.6 %collective-permute-start.7 = (bf16[64,8,512]{2,1,0:T(8,128)(2,1)S(1)}, bf16[64,8,512]{2,1,0:T(8,128)(2,1)S(1)}, u32[]{:S(2)}, u32[]{:S(2)}) collective-permute-start(bf16[64,8,512]{2,1,0:T(8,128)(2,1)S(1)} %head_away.1), channel_id=1, source_target_pairs={{0,8},{8,0},{1,9},{9,1},{2,10},{10,2},{3,11},{11,3},{4,12},{12,4},... | collective-permute-start | bytes 1572872 | tf_op jit(solution)/shard_map/back_second/ppermute | solution.py:483
  211.6 2.8 collective-permute-start.8
  241.9 4.1 %collective-permute-start.9 = (bf16[64,8,512]{2,1,0:T(8,128)(2,1)S(1)}, bf16[64,8,512]{2,1,0:T(8,128)(2,1)S(1)}, u32[]{:S(2)}, u32[]{:S(2)}) collective-permute-start(bf16[64,8,512]{2,1,0:T(8,128)(2,1)S(1)} %feed_away.1), channel_id=1, source_target_pairs={{0,8},{8,0},{1,9},{9,1},{2,10},{10,2},{3,11},{11,3},{4,12},{12,4},... | collective-permute-start | bytes 1572872 | tf_op jit(solution)/shard_map/back_first/ppermute | solution.py:483
  264.2 2.8 collective-permute-start.10
  283.5 20.5 %copy-start.2 = (bf16[3,1024,512]{2,1,0:T(8,128)(2,1)S(1)}, bf16[3,1024,512]{2,1,0:T(8,128)(2,1)}, u32[]{:S(2)}) copy-start(bf16[3,1024,512]{2,1,0:T(8,128)(2,1)} %first.1) | copy-start | bytes 9437188
  283.5 20.5 %copy-start.3 = (bf16[3,1024,512]{2,1,0:T(8,128)(2,1)S(1)}, bf16[3,1024,512]{2,1,0:T(8,128)(2,1)}, u32[]{:S(2)}) copy-start(bf16[3,1024,512]{2,1,0:T(8,128)(2,1)} %second.1) | copy-start | bytes 9437188
  283.5 20.5 %copy-start.6 = (f32[3,1024,2]{1,2,0:T(2,128)S(1)}, f32[3,1024,2]{1,2,0:T(2,128)}, u32[]{:S(2)}) copy-start(f32[3,1024,2]{1,2,0:T(2,128)} %param.17) | copy-start | bytes 73732
  283.5 20.5 %copy-start.7 = (f32[3,1024,2]{1,2,0:T(2,128)S(1)}, f32[3,1024,2]{1,2,0:T(2,128)}, u32[]{:S(2)}) copy-start(f32[3,1024,2]{1,2,0:T(2,128)} %param.19) | copy-start | bytes 73732

commit v6 on v5

--- a/solution.py
+++ b/solution.py
@@ -111,27 +111,26 @@
     return pl.BlockSpec(shape, lambda i, core: (0,) * len(shape))
 
 
-def half_out_kernel(group, taps, out):
+def half_out_kernel(group, taps, kept, out):
     sets, _, width = taps.shape
-    chunks = width // 1024
-    other = (1 - group[0] % 2) * 512
+    core = group[0] % 2
     for s in range(sets):
-        for chunk in range(chunks):
-            start = pl.multiple_of(chunk * 1024 + other, 512)
-            out[s, :, chunk * 512 : (chunk + 1) * 512] = taps[s, :, pl.ds(start, 512)]
-
-
-def half_join_kernel(core, taps, received, out):
-    sets, _, width = taps.shape
-    chunks = width // 1024
+        for chunk in range(width // 1024):
+            place = slice(chunk * 512, (chunk + 1) * 512)
+            for half, target in ((core, kept), (1 - core, out)):
+                start = pl.multiple_of(chunk * 1024 + half * 512, 512)
+                target[s, :, place] = taps[s, :, pl.ds(start, 512)]
+
+
+def half_join_kernel(core, kept, received, out):
+    sets, _, width = kept.shape
+    chunks = width // 512
     copies = out.shape[0] // chunks
-    own = core[0] * 512
     first = core[0] == 0
     for chunk in range(chunks):
         rows = []
         for s in range(sets):
-            start = pl.multiple_of(chunk * 1024 + own, 512)
-            mine = taps[s, :, pl.ds(start, 512)].astype(f32)
+            mine = kept[s, :, chunk * 512 : (chunk + 1) * 512].astype(f32)
             theirs = received[s, :, chunk * 512 : (chunk + 1) * 512].astype(f32)
             rows.append(jnp.where(first, mine, theirs))
             rows.append(jnp.where(first, theirs, mine))
@@ -313,15 +312,12 @@
 
 
 def grad_kernel(
-    core, own, other, mine, theirs, first, second, loss, grad, payload, squares
+    core, own, other, mine, theirs, first, second, loss, grad, payload, squares, summed
 ):
     tap = pl.program_id(0)
 
-    def both(lefts):
-        for half, (left, left_later) in enumerate(lefts):
-            value = contract_first(left, first[...]) + contract_first(
-                left_later, second[...]
-            )
+    def both(values):
+        for half, value in enumerate(values):
             grad[0, half_rows(core[0] if half == 0 else 1 - core[0])] = value
             total = jnp.sum((value * value).reshape(-1, 8, 512), 0)
             total = total[:, :128] + total[:, 128:256] + total[:, 256:384] + total[:, 384:]
@@ -330,14 +326,20 @@
     @pl.when(tap == 0)
     def _():
         squares[...] = jnp.zeros((8, LANES), f32)
+        summed[...] = (first[...].astype(f32) + second[...].astype(f32)).astype(bf16)
 
     @pl.when(tap < 2)
     def _():
-        both([(own[0], own[0]), (other[0], other[0])])
+        both([contract_first(left[0], summed[...]) for left in (own, other)])
 
     @pl.when(tap == 2)
     def _():
-        both([(own[0], mine[...]), (other[0], theirs[...])])
+        both(
+            [
+                contract_first(left[0], first[...]) + contract_first(later[...], second[...])
+                for left, later in ((own, mine), (other, theirs))
+            ]
+        )
         row = jnp.sum(squares[...], 0, keepdims=True)
         total = jnp.sum(row, -1, keepdims=True)
         lane = lax.broadcasted_iota(jnp.int32, (1, LANES), 1)
@@ -366,7 +368,7 @@
                 pl.BlockSpec((1, 1024, 512), tap),
                 pl.BlockSpec((128, 1, LANES), lambda s, core: (0, 0, 0)),
             ],
-            scratch_shapes=[pltpu.VMEM((8, LANES), f32)],
+            scratch_shapes=[pltpu.VMEM((8, LANES), f32), pltpu.VMEM((512, 512), bf16)],
         ),
         out_shape=[
             jax.ShapeDtypeStruct((3, 1024, 512), f32),
@@ -502,12 +504,13 @@
     half_flops = 2 * 512**3
 
     with jax.named_scope("taps_in"):
-        outgoing = call(
-            half_out_kernel, "half_out", [((3, 4, D // 2), bf16)], ("s", group), ("v", taps)
+        kept, outgoing = call(
+            half_out_kernel, "half_out", [((3, 4, D // 2), bf16)] * 2,
+            ("s", group), ("v", taps),
         )
         packed = call(
             half_join_kernel, "half_join", [((64, 24, 512), bf16)],
-            ("s", own), ("v", taps), ("v", swap(outgoing)),
+            ("s", own), ("v", kept), ("v", swap(outgoing)),
         )
         landed = exchange(packed)
         taps_own = landed.reshape(64, 3, 8, 512).transpose(1, 0, 2, 3).reshape(3, 512, 512)

time: 315 us -> 314 us (level)
  no operation moved by 1% of the time
where the time goes in v6:
time: 314 us; the launch traced here: 313 us
  blocking collectives  246 us (78%)
  Pallas kernels  28.6 us (9%)
  starting transfers between devices  23.3 us (7%)
  waiting for transfers between devices  12.1 us (4%)
    all_to_all x12, blocking collectives, exchange(): return lax.all_to_all(value, axes, 0, 0, tiled=False)  246 us
    ppermute x11, starting transfers between devices, swap(): return lax.ppermute(value, 'b', [(0, 1), (1, 0)])  23.3 us
    pallas_call x20, Pallas kernels, call(): pl.pallas_call(kernel, out_shape=[jax.ShapeDtypeStruct(shape, dtype) for...  13.5 us
    ppermute x11, waiting for transfers between devices, swap(): return lax.ppermute(value, 'b', [(0, 1), (1, 0)])  12.1 us
    pallas_call x1, Pallas kernels, adam(): pl.pallas_call(adam_kernel, grid=(3, 1024 // rows), in_specs=[pl.BlockSpe...  9.98 us
  transfers between devices with their start and end apart: 11, of which 11 were waited for; matrix products, arithmetic and copies ran while one was open for 0% of the time, Pallas kernels for 1%

profile of v6, /device:TPU:1, one launch (start us, length us, event | category | flops | bytes accessed | tf_op | source)
XLA Modules:
  0.0 313.0 jit_solution(2968831887166439892)
XLA Ops:
  4.2 33.0 %all_to_all.60 = bf16[64,24,512]{2,1,0:T(8,128)(2,1)S(1)} all-to-all(bf16[64,24,512]{2,1,0:T(8,128)(2,1)S(1)} %half_join.1), channel_id=1, replica_groups=mesh['p'=8,'b'=2,'m'=8] {'p','m'}, dimensions={0} | all-to-all | bytes 3145728 | tf_op jit(solution)/shard_map/taps_in/all_to_all | solution.py:488
  38.5 2.5 collective-permute-start.1
  41.1 2.4 join_own.1.begun
  44.3 2.4 join_other.1
  46.8 18.3 %all_to_all.61.got = bf16[64,8,640]{2,1,0:T(8,128)(2,1)S(1)} all-to-all(bf16[64,8,640]{2,1,0:T(8,128)(2,1)S(1)} %get-tuple-element.40), channel_id=1, replica_groups=mesh['p'=8,'b'=2,'m'=8] {'p','m'}, dimensions={0} | all-to-all | bytes 1310720 | tf_op jit(solution)/shard_map/join_first/all_to_all | solution.py:488
  65.2 2.0 collective-permute-start.2
  68.1 16.4 %all_to_all.62 = bf16[64,8,512]{2,1,0:T(8,128)(2,1)S(1)} all-to-all(bf16[64,8,512]{2,1,0:T(8,128)(2,1)S(1)} %get-tuple-element.44), channel_id=1, replica_groups=mesh['p'=8,'b'=2,'m'=8] {'p','m'}, dimensions={0} | all-to-all | bytes 1048576 | tf_op jit(solution)/shard_map/hidden_first/all_to_all | solution.py:488
  89.8 26.4 %all_to_all.63.got = bf16[64,8,1536]{2,1,0:T(8,128)(2,1)S(1)} all-to-all(bf16[64,8,1536]{2,1,0:T(8,128)(2,1)S(1)} %join_second.1), channel_id=1, replica_groups=mesh['p'=8,'b'=2,'m'=8] {'p','m'}, dimensions={0} | all-to-all | bytes 3145728 | tf_op jit(solution)/shard_map/join_second/all_to_all | solution.py:488
  116.5 2.5 collective-permute-start.4
  120.0 16.8 %all_to_all.64 = bf16[64,8,512]{2,1,0:T(8,128)(2,1)S(1)} all-to-all(bf16[64,8,512]{2,1,0:T(8,128)(2,1)S(1)} %get-tuple-element.48), channel_id=1, replica_groups=mesh['p'=8,'b'=2,'m'=8] {'p','m'}, dimensions={0} | all-to-all | bytes 1048576 | tf_op jit(solution)/shard_map/hidden_second/all_to_all | solution.py:488
  141.6 21.6 %all_to_all.65.got = bf16[64,8,1024]{2,1,0:T(8,128)(2,1)S(1)} all-to-all(bf16[64,8,1024]{2,1,0:T(8,128)(2,1)S(1)} %logits.1), channel_id=1, replica_groups=mesh['p'=8,'b'=2,'m'=8] {'p','m'}, dimensions={0} | all-to-all | bytes 2097152 | tf_op jit(solution)/shard_map/logits/all_to_all | solution.py:488
  163.5 2.3 collective-permute-start.6
  167.0 21.8 %all_to_all.66 = bf16[64,8,1024]{2,1,0:T(8,128)(2,1)S(1)} all-to-all(bf16[64,8,1024]{2,1,0:T(8,128)(2,1)S(1)} %get-tuple-element.53), channel_id=1, replica_groups=mesh['p'=8,'b'=2,'m'=8] {'p','m'}, dimensions={0} | all-to-all | bytes 2097152 | tf_op jit(solution)/shard_map/softmax/all_to_all | solution.py:488
  189.5 2.1 collective-permute-start.7
  193.9 16.6 %all_to_all.67.got = bf16[64,8,512]{2,1,0:T(8,128)(2,1)S(1)} all-to-all(bf16[64,8,512]{2,1,0:T(8,128)(2,1)S(1)} %head_keep.1), channel_id=1, replica_groups=mesh['p'=8,'b'=2,'m'=8] {'p','m'}, dimensions={0} | all-to-all | bytes 1048576 | tf_op jit(solution)/shard_map/back_second/all_to_all | solution.py:488
  210.7 2.0 collective-permute-start.8
  213.6 26.4 %all_to_all.68 = bf16[64,8,1536]{2,1,0:T(8,128)(2,1)S(1)} all-to-all(bf16[64,8,1536]{2,1,0:T(8,128)(2,1)S(1)} %norm_back.2), channel_id=1, replica_groups=mesh['p'=8,'b'=2,'m'=8] {'p','m'}, dimensions={0} | all-to-all | bytes 3145728 | tf_op jit(solution)/shard_map/back_second/all_to_all | solution.py:488
  241.0 2.6 collective-permute-start.9
  246.2 17.0 %all_to_all.69.got = bf16[64,8,512]{2,1,0:T(8,128)(2,1)S(1)} all-to-all(bf16[64,8,512]{2,1,0:T(8,128)(2,1)S(1)} %feed_keep.1), channel_id=1, replica_groups=mesh['p'=8,'b'=2,'m'=8] {'p','m'}, dimensions={0} | all-to-all | bytes 1048576 | tf_op jit(solution)/shard_map/back_first/all_to_all | solution.py:488
  263.3 2.0 collective-permute-start.10
  266.2 16.4 %all_to_all.70 = bf16[64,8,512]{2,1,0:T(8,128)(2,1)S(1)} all-to-all(bf16[64,8,512]{2,1,0:T(8,128)(2,1)S(1)} %norm_back.3), channel_id=1, replica_groups=mesh['p'=8,'b'=2,'m'=8] {'p','m'}, dimensions={0} | all-to-all | bytes 1048576 | tf_op jit(solution)/shard_map/back_first/all_to_all | solution.py:488
  282.6 5.1 %gradients.1 = (f32[3,1024,512]{2,1,0:T(8,128)S(1)}, f32[128,1,128]{2,1,0:T(1,128)S(1)}) custom-call(s32[1]{0:T(128)} %bitcast.core, bf16[3,512,512]{2,1,0:T(8,128)(2,1)} %copy_bitcast_fusion.taps.own, bf16[3,512,512]{2,1,0:T(8,128)(2,1)} %collective-permute-done.1.taps.other, bf16[512,512]{1,0:T(8,128)(2,1)S(1)} %bitcast.31, ...), custom_call_target="tpu_custom_call" | custom-call | flops 3221225472 | bytes 10485760 | tf_op jit(solution)/shard_map/gradients/gradients/pallas_call | solution.py:353
  287.8 15.0 %all_to_all.71.shared = f32[128,1,128]{2,1,0:T(1,128)S(1)} all-to-all(f32[128,1,128]{2,1,0:T(1,128)S(1)} %get-tuple-element.62), channel_id=1, replica_groups=mesh['p'=8,'b'=2,'m'=8] {'p','b','m'}, dimensions={0} | all-to-all | bytes 131072 | tf_op jit(solution)/shard_map/gradients/all_to_all | solution.py:488
  302.8 10.0 %update.1 = (bf16[3,1024,512]{2,1,0:T(8,128)(2,1)}, bf16[3,1024,512]{2,1,0:T(8,128)(2,1)}, bf16[3,1024,512]{2,1,0:T(8,128)(2,1)}, f32[3,2,1024]{2,1,0:T(2,128)}, f32[3,2,1024]{2,1,0:T(2,128)}, /*index=5*/f32[1,1]{1,0:T(1,128)}) custom-call(f32[128,1,128]{2,1,0:T(1,128)S(1)} %all_to_all.71.shared, bf16[3,1024,512]{2,1,0:T(8,128)(2,1)S(1)} %copy-done, ...), custom_call_target="tpu_custom_call" | custom-call | tf_op jit(solution)/shard_map/update/update/pallas_call | solution.py:449
  (56 shorter events, 28.5 us)
Async XLA Ops:
  0.6 0.9 copy-start.4
  1.6 2.4 collective-permute-start
  37.2 3.8 %copy-start.8 = (s32[2,16,4]{1,2,0:T(4,128)S(1)}, s32[2,16,4]{1,2,0:T(4,128)}, u32[]{:S(2)}) copy-start(s32[2,16,4]{1,2,0:T(4,128)} %param.15) | copy-start | bytes 1540
  37.2 3.9 %copy-start.9 = (f32[512]{0:T(512)S(1)}, f32[512]{0:T(512)}, u32[]{:S(2)}) copy-start(f32[512]{0:T(512)} %param.11) | copy-start | bytes 6148
  37.2 3.9 %copy-start = (bf16[3,1024,512]{2,1,0:T(8,128)(2,1)S(1)}, bf16[3,1024,512]{2,1,0:T(8,128)(2,1)}, u32[]{:S(2)}) copy-start(bf16[3,1024,512]{2,1,0:T(8,128)(2,1)} %weight.11) | copy-start | bytes 9437188
  38.5 5.9 %collective-permute-start.1 = (bf16[3,512,512]{2,1,0:T(8,128)(2,1)}, bf16[3,512,512]{2,1,0:T(8,128)(2,1)}, u32[]{:S(2)}, u32[]{:S(2)}) collective-permute-start(bf16[3,512,512]{2,1,0:T(8,128)(2,1)} %copy_bitcast_fusion.taps.own), channel_id=1, source_target_pairs={{0,8},{8,0},{1,9},{9,1},{2,10},{10,2},{3,11},{11,3},{4,12},{12,4},... | collective-permute-start | bytes 4718600 | tf_op jit(solution)/shard_map/taps_in/ppermute | solution.py:485
  46.8 41.2 %copy-start.1 = (bf16[1024,1024]{1,0:T(8,128)(2,1)S(1)}, bf16[1024,1024]{1,0:T(8,128)(2,1)}, u32[]{:S(2)}) copy-start(bf16[1024,1024]{1,0:T(8,128)(2,1)} %head.11) | copy-start | bytes 6291460
  65.2 2.8 collective-permute-start.2
  84.5 3.5 %collective-permute-start.3 = (bf16[512,512]{1,0:T(8,128)(2,1)S(1)}, bf16[512,512]{1,0:T(8,128)(2,1)S(1)}, u32[]{:S(2)}, u32[]{:S(2)}) collective-permute-start(bf16[512,512]{1,0:T(8,128)(2,1)S(1)} %bitcast.29), channel_id=1, source_target_pairs={{0,8},{8,0},{1,9},{9,1},{2,10},{10,2},{3,11},{11,3},{4,12},{12,4},... | collective-permute-start | bytes 1572872 | tf_op jit(solution)/shard_map/hidden_first/ppermute | solution.py:485
  116.5 3.3 %collective-permute-start.4 = (f32[8,128]{1,0:T(8,128)S(1)}, f32[8,128]{1,0:T(8,128)S(1)}, u32[]{:S(2)}, u32[]{:S(2)}) collective-permute-start(f32[8,128]{1,0:T(8,128)S(1)} %get-tuple-element.47.squares), channel_id=1, source_target_pairs={{0,8},{8,0},{1,9},{9,1},{2,10},{10,2},{3,11},{11,3},{4,12},{12,4},... | collective-permute-start | bytes 12296 | tf_op jit(solution)/shard_map/hidden_second/ppermute | solution.py:485
  136.8 3.5 %collective-permute-start.5 = (bf16[512,512]{1,0:T(8,128)(2,1)S(1)}, bf16[512,512]{1,0:T(8,128)(2,1)S(1)}, u32[]{:S(2)}, u32[]{:S(2)}) collective-permute-start(bf16[512,512]{1,0:T(8,128)(2,1)S(1)} %bitcast.32), channel_id=1, source_target_pairs={{0,8},{8,0},{1,9},{9,1},{2,10},{10,2},{3,11},{11,3},{4,12},{12,4},... | collective-permute-start | bytes 1572872 | tf_op jit(solution)/shard_map/hidden_second/ppermute | solution.py:485
  141.5 21.6 %copy-start.7 = (s32[2,16,4]{1,2,0:T(4,128)S(1)}, s32[2,16,4]{1,2,0:T(4,128)}, u32[]{:S(2)}) copy-start(s32[2,16,4]{1,2,0:T(4,128)} %param.14) | copy-start | bytes 1540
  163.5 3.1 collective-permute-start.6
  189.5 3.6 %collective-permute-start.7 = (bf16[64,8,512]{2,1,0:T(8,128)(2,1)S(1)}, bf16[64,8,512]{2,1,0:T(8,128)(2,1)S(1)}, u32[]{:S(2)}, u32[]{:S(2)}) collective-permute-start(bf16[64,8,512]{2,1,0:T(8,128)(2,1)S(1)} %head_away.1), channel_id=1, source_target_pairs={{0,8},{8,0},{1,9},{9,1},{2,10},{10,2},{3,11},{11,3},{4,12},{12,4},... | collective-permute-start | bytes 1572872 | tf_op jit(solution)/shard_map/back_second/ppermute | solution.py:485
  210.7 2.8 collective-permute-start.8
  241.0 4.1 %collective-permute-start.9 = (bf16[64,8,512]{2,1,0:T(8,128)(2,1)S(1)}, bf16[64,8,512]{2,1,0:T(8,128)(2,1)S(1)}, u32[]{:S(2)}, u32[]{:S(2)}) collective-permute-start(bf16[64,8,512]{2,1,0:T(8,128)(2,1)S(1)} %feed_away.1), channel_id=1, source_target_pairs={{0,8},{8,0},{1,9},{9,1},{2,10},{10,2},{3,11},{11,3},{4,12},{12,4},... | collective-permute-start | bytes 1572872 | tf_op jit(solution)/shard_map/back_first/ppermute | solution.py:485
  263.3 2.8 collective-permute-start.10
  282.6 20.2 %copy-start.2 = (bf16[3,1024,512]{2,1,0:T(8,128)(2,1)S(1)}, bf16[3,1024,512]{2,1,0:T(8,128)(2,1)}, u32[]{:S(2)}) copy-start(bf16[3,1024,512]{2,1,0:T(8,128)(2,1)} %first.1) | copy-start | bytes 9437188
  282.6 20.2 %copy-start.3 = (bf16[3,1024,512]{2,1,0:T(8,128)(2,1)S(1)}, bf16[3,1024,512]{2,1,0:T(8,128)(2,1)}, u32[]{:S(2)}) copy-start(bf16[3,1024,512]{2,1,0:T(8,128)(2,1)} %second.1) | copy-start | bytes 9437188
  282.6 20.2 %copy-start.5 = (f32[3,1024,2]{1,2,0:T(2,128)S(1)}, f32[3,1024,2]{1,2,0:T(2,128)}, u32[]{:S(2)}) copy-start(f32[3,1024,2]{1,2,0:T(2,128)} %param.17) | copy-start | bytes 73732
  282.6 20.2 %copy-start.6 = (f32[3,1024,2]{1,2,0:T(2,128)S(1)}, f32[3,1024,2]{1,2,0:T(2,128)}, u32[]{:S(2)}) copy-start(f32[3,1024,2]{1,2,0:T(2,128)} %param.19) | copy-start | bytes 73732

commit v7 on v6

--- a/solution.py
+++ b/solution.py
@@ -398,7 +398,7 @@
     shared, weight, grad, first, second, first_scale, second_scale,
     new_weight, new_first, new_second, new_first_scale, new_second_scale, loss,
 ):
-    rows = weight.shape[1]
+    rows = grad.shape[1]
     total = jnp.sum(shared[:, 0, :], 0, keepdims=True)
     loss[...] = total[:, 1:2]
     clip = jnp.minimum(1.0, clip_norm / (jnp.sqrt(total[:, 0:1]) + 1e-06))
@@ -411,14 +411,14 @@
         span = slice(block * BLOCK, (block + 1) * BLOCK)
         clipped = grad[0, :, span] * clip
         first_new = (
-            first[0, :, span].astype(f32) * old_first[:, span]
+            first[tap, here, span].astype(f32) * old_first[:, span]
             + (1.0 - beta_first) * clipped
         )
         second_new = (
-            second[0, :, span].astype(f32) * old_second[:, span]
+            second[tap, here, span].astype(f32) * old_second[:, span]
             + (1.0 - beta_second) * clipped * clipped
         )
-        current = weight[0, :, span].astype(f32)
+        current = weight[tap, here, span].astype(f32)
         spread_sq = second_new * (1.0 / (1.0 - beta_second**step_count))
         spread = spread_sq * lax.rsqrt(spread_sq) + adam_eps
         turned = pl.reciprocal(spread, approx=True)
@@ -451,7 +451,7 @@
         grid=(3, 1024 // rows),
         in_specs=[
             pl.BlockSpec((128, 1, LANES), lambda s, i: (0, 0, 0)),
-            wide, wide, wide, wide, thin, thin,
+            VMEM, wide, VMEM, VMEM, thin, thin,
         ],
         out_specs=[
             wide, wide, wide, thin, thin, pl.BlockSpec((1, 1), lambda s, i: (0, 0))

time: 314 us -> 314 us (level)
  no operation moved by 1% of the time
where the time goes in v7:
time: 314 us; the launch traced here: 313 us
  blocking collectives  246 us (78%)
  Pallas kernels  28.8 us (9%)
  starting transfers between devices  23.3 us (7%)
  waiting for transfers between devices  12.1 us (4%)
    all_to_all x12, blocking collectives, exchange(): return lax.all_to_all(value, axes, 0, 0, tiled=False)  246 us
    ppermute x11, starting transfers between devices, swap(): return lax.ppermute(value, 'b', [(0, 1), (1, 0)])  23.3 us
    pallas_call x20, Pallas kernels, call(): pl.pallas_call(kernel, out_shape=[jax.ShapeDtypeStruct(shape, dtype) for...  13.5 us
    ppermute x11, waiting for transfers between devices, swap(): return lax.ppermute(value, 'b', [(0, 1), (1, 0)])  12.1 us
    pallas_call x1, Pallas kernels, adam(): pl.pallas_call(adam_kernel, grid=(3, 1024 // rows), in_specs=[pl.BlockSpe...  10.1 us
  transfers between devices with their start and end apart: 11, of which 11 were waited for; matrix products, arithmetic and copies ran while one was open for 0% of the time, Pallas kernels for 1%

profile of v7, /device:TPU:1, one launch (start us, length us, event | category | flops | bytes accessed | tf_op | source)
XLA Modules:
  0.0 313.1 jit_solution(17261374501536124456)
XLA Ops:
  4.2 33.0 %all_to_all.60 = bf16[64,24,512]{2,1,0:T(8,128)(2,1)S(1)} all-to-all(bf16[64,24,512]{2,1,0:T(8,128)(2,1)S(1)} %half_join.1), channel_id=1, replica_groups=mesh['p'=8,'b'=2,'m'=8] {'p','m'}, dimensions={0} | all-to-all | bytes 3145728 | tf_op jit(solution)/shard_map/taps_in/all_to_all | solution.py:488
  38.5 2.5 collective-permute-start.1
  41.1 2.4 join_own.1.begun
  44.3 2.4 join_other.1
  46.8 18.3 %all_to_all.61.got = bf16[64,8,640]{2,1,0:T(8,128)(2,1)S(1)} all-to-all(bf16[64,8,640]{2,1,0:T(8,128)(2,1)S(1)} %get-tuple-element.40), channel_id=1, replica_groups=mesh['p'=8,'b'=2,'m'=8] {'p','m'}, dimensions={0} | all-to-all | bytes 1310720 | tf_op jit(solution)/shard_map/join_first/all_to_all | solution.py:488
  65.2 2.0 collective-permute-start.2
  68.1 16.4 %all_to_all.62 = bf16[64,8,512]{2,1,0:T(8,128)(2,1)S(1)} all-to-all(bf16[64,8,512]{2,1,0:T(8,128)(2,1)S(1)} %get-tuple-element.44), channel_id=1, replica_groups=mesh['p'=8,'b'=2,'m'=8] {'p','m'}, dimensions={0} | all-to-all | bytes 1048576 | tf_op jit(solution)/shard_map/hidden_first/all_to_all | solution.py:488
  89.8 26.4 %all_to_all.63.got = bf16[64,8,1536]{2,1,0:T(8,128)(2,1)S(1)} all-to-all(bf16[64,8,1536]{2,1,0:T(8,128)(2,1)S(1)} %join_second.1), channel_id=1, replica_groups=mesh['p'=8,'b'=2,'m'=8] {'p','m'}, dimensions={0} | all-to-all | bytes 3145728 | tf_op jit(solution)/shard_map/join_second/all_to_all | solution.py:488
  116.5 2.5 collective-permute-start.4
  120.0 16.8 %all_to_all.64 = bf16[64,8,512]{2,1,0:T(8,128)(2,1)S(1)} all-to-all(bf16[64,8,512]{2,1,0:T(8,128)(2,1)S(1)} %get-tuple-element.48), channel_id=1, replica_groups=mesh['p'=8,'b'=2,'m'=8] {'p','m'}, dimensions={0} | all-to-all | bytes 1048576 | tf_op jit(solution)/shard_map/hidden_second/all_to_all | solution.py:488
  141.6 21.6 %all_to_all.65.got = bf16[64,8,1024]{2,1,0:T(8,128)(2,1)S(1)} all-to-all(bf16[64,8,1024]{2,1,0:T(8,128)(2,1)S(1)} %logits.1), channel_id=1, replica_groups=mesh['p'=8,'b'=2,'m'=8] {'p','m'}, dimensions={0} | all-to-all | bytes 2097152 | tf_op jit(solution)/shard_map/logits/all_to_all | solution.py:488
  163.5 2.3 collective-permute-start.6
  167.0 21.8 %all_to_all.66 = bf16[64,8,1024]{2,1,0:T(8,128)(2,1)S(1)} all-to-all(bf16[64,8,1024]{2,1,0:T(8,128)(2,1)S(1)} %get-tuple-element.53), channel_id=1, replica_groups=mesh['p'=8,'b'=2,'m'=8] {'p','m'}, dimensions={0} | all-to-all | bytes 2097152 | tf_op jit(solution)/shard_map/softmax/all_to_all | solution.py:488
  189.5 2.1 collective-permute-start.7
  193.9 16.6 %all_to_all.67.got = bf16[64,8,512]{2,1,0:T(8,128)(2,1)S(1)} all-to-all(bf16[64,8,512]{2,1,0:T(8,128)(2,1)S(1)} %head_keep.1), channel_id=1, replica_groups=mesh['p'=8,'b'=2,'m'=8] {'p','m'}, dimensions={0} | all-to-all | bytes 1048576 | tf_op jit(solution)/shard_map/back_second/all_to_all | solution.py:488
  210.7 2.0 collective-permute-start.8
  213.6 26.4 %all_to_all.68 = bf16[64,8,1536]{2,1,0:T(8,128)(2,1)S(1)} all-to-all(bf16[64,8,1536]{2,1,0:T(8,128)(2,1)S(1)} %norm_back.2), channel_id=1, replica_groups=mesh['p'=8,'b'=2,'m'=8] {'p','m'}, dimensions={0} | all-to-all | bytes 3145728 | tf_op jit(solution)/shard_map/back_second/all_to_all | solution.py:488
  241.0 2.6 collective-permute-start.9
  246.2 17.0 %all_to_all.69.got = bf16[64,8,512]{2,1,0:T(8,128)(2,1)S(1)} all-to-all(bf16[64,8,512]{2,1,0:T(8,128)(2,1)S(1)} %feed_keep.1), channel_id=1, replica_groups=mesh['p'=8,'b'=2,'m'=8] {'p','m'}, dimensions={0} | all-to-all | bytes 1048576 | tf_op jit(solution)/shard_map/back_first/all_to_all | solution.py:488
  263.3 2.0 collective-permute-start.10
  266.2 16.4 %all_to_all.70 = bf16[64,8,512]{2,1,0:T(8,128)(2,1)S(1)} all-to-all(bf16[64,8,512]{2,1,0:T(8,128)(2,1)S(1)} %norm_back.3), channel_id=1, replica_groups=mesh['p'=8,'b'=2,'m'=8] {'p','m'}, dimensions={0} | all-to-all | bytes 1048576 | tf_op jit(solution)/shard_map/back_first/all_to_all | solution.py:488
  282.6 5.1 %gradients.1 = (f32[3,1024,512]{2,1,0:T(8,128)S(1)}, f32[128,1,128]{2,1,0:T(1,128)S(1)}) custom-call(s32[1]{0:T(128)} %bitcast.core, bf16[3,512,512]{2,1,0:T(8,128)(2,1)} %copy_bitcast_fusion.taps.own, bf16[3,512,512]{2,1,0:T(8,128)(2,1)} %collective-permute-done.1.taps.other, bf16[512,512]{1,0:T(8,128)(2,1)S(1)} %bitcast.31, ...), custom_call_target="tpu_custom_call" | custom-call | flops 3221225472 | bytes 10485760 | tf_op jit(solution)/shard_map/gradients/gradients/pallas_call | solution.py:353
  287.8 15.0 %all_to_all.71.shared = f32[128,1,128]{2,1,0:T(1,128)S(1)} all-to-all(f32[128,1,128]{2,1,0:T(1,128)S(1)} %get-tuple-element.62), channel_id=1, replica_groups=mesh['p'=8,'b'=2,'m'=8] {'p','b','m'}, dimensions={0} | all-to-all | bytes 131072 | tf_op jit(solution)/shard_map/gradients/all_to_all | solution.py:488
  302.8 10.1 %update.1 = (bf16[3,1024,512]{2,1,0:T(8,128)(2,1)}, bf16[3,1024,512]{2,1,0:T(8,128)(2,1)}, bf16[3,1024,512]{2,1,0:T(8,128)(2,1)}, f32[3,2,1024]{2,1,0:T(2,128)}, f32[3,2,1024]{2,1,0:T(2,128)}, /*index=5*/f32[1,1]{1,0:T(1,128)}) custom-call(f32[128,1,128]{2,1,0:T(1,128)S(1)} %all_to_all.71.shared, bf16[3,1024,512]{2,1,0:T(8,128)(2,1)S(1)} %copy-done, ...), custom_call_target="tpu_custom_call" | custom-call | tf_op jit(solution)/shard_map/update/update/pallas_call | solution.py:449
  (56 shorter events, 28.5 us)
Async XLA Ops:
  0.6 0.9 copy-start.4
  1.6 2.4 collective-permute-start
  37.2 3.8 %copy-start.8 = (s32[2,16,4]{1,2,0:T(4,128)S(1)}, s32[2,16,4]{1,2,0:T(4,128)}, u32[]{:S(2)}) copy-start(s32[2,16,4]{1,2,0:T(4,128)} %param.15) | copy-start | bytes 1540
  37.2 3.9 %copy-start.9 = (f32[512]{0:T(512)S(1)}, f32[512]{0:T(512)}, u32[]{:S(2)}) copy-start(f32[512]{0:T(512)} %param.11) | copy-start | bytes 6148
  37.2 3.9 %copy-start = (bf16[3,1024,512]{2,1,0:T(8,128)(2,1)S(1)}, bf16[3,1024,512]{2,1,0:T(8,128)(2,1)}, u32[]{:S(2)}) copy-start(bf16[3,1024,512]{2,1,0:T(8,128)(2,1)} %weight.11) | copy-start | bytes 9437188
  38.5 5.9 %collective-permute-start.1 = (bf16[3,512,512]{2,1,0:T(8,128)(2,1)}, bf16[3,512,512]{2,1,0:T(8,128)(2,1)}, u32[]{:S(2)}, u32[]{:S(2)}) collective-permute-start(bf16[3,512,512]{2,1,0:T(8,128)(2,1)} %copy_bitcast_fusion.taps.own), channel_id=1, source_target_pairs={{0,8},{8,0},{1,9},{9,1},{2,10},{10,2},{3,11},{11,3},{4,12},{12,4},... | collective-permute-start | bytes 4718600 | tf_op jit(solution)/shard_map/taps_in/ppermute | solution.py:485
  46.8 41.2 %copy-start.1 = (bf16[1024,1024]{1,0:T(8,128)(2,1)S(1)}, bf16[1024,1024]{1,0:T(8,128)(2,1)}, u32[]{:S(2)}) copy-start(bf16[1024,1024]{1,0:T(8,128)(2,1)} %head.11) | copy-start | bytes 6291460
  65.2 2.8 collective-permute-start.2
  84.5 3.5 %collective-permute-start.3 = (bf16[512,512]{1,0:T(8,128)(2,1)S(1)}, bf16[512,512]{1,0:T(8,128)(2,1)S(1)}, u32[]{:S(2)}, u32[]{:S(2)}) collective-permute-start(bf16[512,512]{1,0:T(8,128)(2,1)S(1)} %bitcast.29), channel_id=1, source_target_pairs={{0,8},{8,0},{1,9},{9,1},{2,10},{10,2},{3,11},{11,3},{4,12},{12,4},... | collective-permute-start | bytes 1572872 | tf_op jit(solution)/shard_map/hidden_first/ppermute | solution.py:485
  116.5 3.3 %collective-permute-start.4 = (f32[8,128]{1,0:T(8,128)S(1)}, f32[8,128]{1,0:T(8,128)S(1)}, u32[]{:S(2)}, u32[]{:S(2)}) collective-permute-start(f32[8,128]{1,0:T(8,128)S(1)} %get-tuple-element.47.squares), channel_id=1, source_target_pairs={{0,8},{8,0},{1,9},{9,1},{2,10},{10,2},{3,11},{11,3},{4,12},{12,4},... | collective-permute-start | bytes 12296 | tf_op jit(solution)/shard_map/hidden_second/ppermute | solution.py:485
  136.8 3.5 %collective-permute-start.5 = (bf16[512,512]{1,0:T(8,128)(2,1)S(1)}, bf16[512,512]{1,0:T(8,128)(2,1)S(1)}, u32[]{:S(2)}, u32[]{:S(2)}) collective-permute-start(bf16[512,512]{1,0:T(8,128)(2,1)S(1)} %bitcast.32), channel_id=1, source_target_pairs={{0,8},{8,0},{1,9},{9,1},{2,10},{10,2},{3,11},{11,3},{4,12},{12,4},... | collective-permute-start | bytes 1572872 | tf_op jit(solution)/shard_map/hidden_second/ppermute | solution.py:485
  141.5 21.6 %copy-start.7 = (s32[2,16,4]{1,2,0:T(4,128)S(1)}, s32[2,16,4]{1,2,0:T(4,128)}, u32[]{:S(2)}) copy-start(s32[2,16,4]{1,2,0:T(4,128)} %param.14) | copy-start | bytes 1540
  163.5 3.1 collective-permute-start.6
  189.5 3.6 %collective-permute-start.7 = (bf16[64,8,512]{2,1,0:T(8,128)(2,1)S(1)}, bf16[64,8,512]{2,1,0:T(8,128)(2,1)S(1)}, u32[]{:S(2)}, u32[]{:S(2)}) collective-permute-start(bf16[64,8,512]{2,1,0:T(8,128)(2,1)S(1)} %head_away.1), channel_id=1, source_target_pairs={{0,8},{8,0},{1,9},{9,1},{2,10},{10,2},{3,11},{11,3},{4,12},{12,4},... | collective-permute-start | bytes 1572872 | tf_op jit(solution)/shard_map/back_second/ppermute | solution.py:485
  210.7 2.8 collective-permute-start.8
  241.0 4.1 %collective-permute-start.9 = (bf16[64,8,512]{2,1,0:T(8,128)(2,1)S(1)}, bf16[64,8,512]{2,1,0:T(8,128)(2,1)S(1)}, u32[]{:S(2)}, u32[]{:S(2)}) collective-permute-start(bf16[64,8,512]{2,1,0:T(8,128)(2,1)S(1)} %feed_away.1), channel_id=1, source_target_pairs={{0,8},{8,0},{1,9},{9,1},{2,10},{10,2},{3,11},{11,3},{4,12},{12,4},... | collective-permute-start | bytes 1572872 | tf_op jit(solution)/shard_map/back_first/ppermute | solution.py:485
  263.3 2.8 collective-permute-start.10
  282.6 20.2 %copy-start.2 = (bf16[3,1024,512]{2,1,0:T(8,128)(2,1)S(1)}, bf16[3,1024,512]{2,1,0:T(8,128)(2,1)}, u32[]{:S(2)}) copy-start(bf16[3,1024,512]{2,1,0:T(8,128)(2,1)} %first.1) | copy-start | bytes 9437188
  282.6 20.2 %copy-start.3 = (bf16[3,1024,512]{2,1,0:T(8,128)(2,1)S(1)}, bf16[3,1024,512]{2,1,0:T(8,128)(2,1)}, u32[]{:S(2)}) copy-start(bf16[3,1024,512]{2,1,0:T(8,128)(2,1)} %second.1) | copy-start | bytes 9437188
  282.6 20.2 %copy-start.5 = (f32[3,1024,2]{1,2,0:T(2,128)S(1)}, f32[3,1024,2]{1,2,0:T(2,128)}, u32[]{:S(2)}) copy-start(f32[3,1024,2]{1,2,0:T(2,128)} %param.17) | copy-start | bytes 73732
  282.6 20.2 %copy-start.6 = (f32[3,1024,2]{1,2,0:T(2,128)S(1)}, f32[3,1024,2]{1,2,0:T(2,128)}, u32[]{:S(2)}) copy-start(f32[3,1024,2]{1,2,0:T(2,128)} %param.19) | copy-start | bytes 73732
